TPU v7x, 256 devices: a whole 4x4x8 slice. The times are simulated.
256 devices in a mesh: seq: 32 (over y_hi, z, core), head: 8 (over x, y_lo).
Axes of the slice: x: 4, y: 4 (y_hi: 2, y_lo: 2; y = y_hi * 2 + y_lo), z: 8, core: 2. Of those that a mesh axis runs over, the one named last changes fastest.
Arguments:
- q1: bfloat16 [8192, 6144], P('seq', 'head'), may hold values from -6 to 6
- k1: bfloat16 [8192, 6144], P('seq', 'head'), may hold values from -6 to 6
- v1: bfloat16 [8192, 6144], P('seq', 'head'), may hold values from -6 to 6
- decay1: float32 [8192, 48], P('seq', 'head'), may hold values from -1 to 0, as said below
- gain_out1: float32 [6144], P('head'), may hold values from 0.25 to 1.75
- wo1: bfloat16 [6144, 3072], P('head'), may hold values from -0.109375 to 0.109375
- stream_in: bfloat16 [8192, 3072], P('seq', 'head'), may hold values from -20 to 20
- gain_in2: float32 [3072], replicated, may hold values from 0.25 to 1.75
- wq2: bfloat16 [3072, 6144], P('seq', 'head'), may hold values from -0.109375 to 0.109375
- wk2: bfloat16 [3072, 6144], P('seq', 'head'), may hold values from -0.109375 to 0.109375
- wv2: bfloat16 [3072, 6144], P('seq', 'head'), may hold values from -0.109375 to 0.109375
- decay2: float32 [8192, 48], P('seq', 'head'), may hold values from -1 to 0, as said below
- gain_out2: float32 [6144], P('head'), may hold values from 0.25 to 1.75
- wo2: bfloat16 [6144, 3072], P('head'), may hold values from -0.109375 to 0.109375
Outputs:
- mixed: bfloat16 [8192, 3072], P('seq', 'head')
Inputs may be any that keep to these rules, and one draw needn't show every extreme that they name: `decay1`: every value is negative. `decay2`: every value is negative.
All inputs are finite; a program needn't handle non-finite values.
Results may differ from a plain program's by a relative error of at most 0.02.
Values may be sent and summed in bfloat16 or wider, within the bound.
No kernel may reach another device: no remote copies, remote signals or barrier semaphores. Data moves between devices by JAX's collectives and lax.ppermute only.
A program may use at most 128 MiB of HBM per device.

v0:
```python
import jax
import jax.numpy as jnp
from jax import lax
from jax.sharding import PartitionSpec as P

DH = 128


def shifted(shard, axis, by):
    count = lax.axis_size(axis)
    pairs = [(i, i + by) for i in range(count) if 0 <= i + by < count]
    return lax.ppermute(shard, axis, pairs)


def silu_round(value_rows):
    wide = value_rows.astype(jnp.float32)
    return jax.nn.silu(wide).astype(jnp.bfloat16)


def relay_states(decay_total, local_state):

    def advance(position, carry):
        return shifted(decay_total[:, None, None] * carry + local_state, "seq", 1)

    return lax.fori_loop(0, lax.axis_size("seq") - 1, advance, jnp.zeros_like(local_state))


def attend(query_pre, key_pre, value_pre, log_decay, gain, linker):
    rows_here, heads_here = log_decay.shape
    query_act = silu_round(query_pre).reshape(rows_here, heads_here, DH)
    key_act = silu_round(key_pre).reshape(rows_here, heads_here, DH)
    value_act = silu_round(value_pre).reshape(rows_here, heads_here, DH)
    cumdecay = jnp.cumsum(log_decay, axis=0)
    across = cumdecay.T
    lower = (jnp.arange(rows_here)[:, None] >= jnp.arange(rows_here)[None, :])[None]
    spread = across[:, :, None] - across[:, None, :]
    factor = jnp.where(lower, jnp.exp(jnp.where(lower, spread, 0.0)), 0.0)
    scores = jnp.einsum("thd,shd->hts", query_act, key_act, preferred_element_type=jnp.float32)
    weights = (scores * factor).astype(jnp.bfloat16)
    intra = jnp.einsum("hts,shd->thd", weights, value_act, preferred_element_type=jnp.float32)
    last_total = across[:, -1]
    tail = jnp.exp(last_total[None, :] - cumdecay)
    local_state = jnp.einsum(
        "thd,the->hde",
        key_act.astype(jnp.float32) * tail[:, :, None],
        value_act.astype(jnp.float32),
        precision=lax.Precision.HIGHEST,
    )
    incoming = linker(jnp.exp(last_total), local_state)
    carried = (
        jnp.einsum(
            "thd,hde->the", query_act.astype(jnp.float32), incoming, precision=lax.Precision.HIGHEST
        )
        * jnp.exp(cumdecay)[:, :, None]
    )
    att = intra + carried
    mean_square = jnp.mean(att * att, axis=-1, keepdims=True)
    normed = att * lax.rsqrt(mean_square + 1e-06) * gain.reshape(heads_here, DH)
    return normed.reshape(rows_here, heads_here * DH).astype(jnp.bfloat16)


def local(
    q1, k1, v1, decay1, gain_out1, wo1, stream_in, gain_in2, wq2, wk2, wv2, decay2, gain_out2, wo2
):
    first_out = attend(q1, k1, v1, decay1, gain_out1, relay_states)
    first_term = jnp.dot(first_out, wo1, preferred_element_type=jnp.float32)
    first_share = lax.psum_scatter(
        first_term.astype(jnp.bfloat16), "head", scatter_dimension=1, tiled=True
    ).astype(jnp.float32)
    stream = (stream_in.astype(jnp.float32) + first_share).astype(jnp.bfloat16)
    whole = lax.all_gather(stream, "head", axis=1, tiled=True)
    wide = whole.astype(jnp.float32)
    normed_in = (
        wide * lax.rsqrt(jnp.mean(wide * wide, axis=-1, keepdims=True) + 1e-06) * gain_in2
    ).astype(jnp.bfloat16)
    pieces = (
        lax.all_gather(wq2, "seq", axis=0, tiled=True),
        lax.all_gather(wk2, "seq", axis=0, tiled=True),
        lax.all_gather(wv2, "seq", axis=0, tiled=True),
    )
    gathered = tuple(
        (jnp.dot(normed_in, piece_now, preferred_element_type=jnp.float32) for piece_now in pieces)
    )
    second_out = attend(gathered[0], gathered[1], gathered[2], decay2, gain_out2, relay_states)
    second_term = jnp.dot(second_out, wo2, preferred_element_type=jnp.float32)
    second_share = lax.psum_scatter(
        second_term.astype(jnp.bfloat16), "head", scatter_dimension=1, tiled=True
    ).astype(jnp.float32)
    return (stream.astype(jnp.float32) + second_share).astype(jnp.bfloat16)


def solution(mesh):
    placed = (
        P("seq", "head"),
        P("seq", "head"),
        P("seq", "head"),
        P("seq", "head"),
        P("head"),
        P("head", None),
        P("seq", "head"),
        P(),
        P("seq", "head"),
        P("seq", "head"),
        P("seq", "head"),
        P("seq", "head"),
        P("head"),
        P("head", None),
    )
    return jax.shard_map(
        local, mesh=mesh, in_specs=placed, out_specs=P("seq", "head"), check_vma=False
    )
```

profile of v0, /device:TPU:1, one launch (start us, length us, event | category | flops | bytes accessed | tf_op | source)
XLA Modules:
  0.0 1233.3 jit_solution(18190444541295812899)
XLA Ops:
  13.8 297.3 %while.20 = (s32[]{:T(128)}, f32[6,128,128]{2,1,0:T(8,128)S(1)}, f32[6]{0:T(128)S(1)}, f32[6,128,128]{2,1,0:T(8,128)S(1)}, s32[]{:T(128)}) while((s32[]{:T(128)}, f32[6,128,128]{2,1,0:T(8,128)S(1)}, f32[6]{0:T(128)S(1)}, f32[6,128,128]{2,1,0:T(8,128)S(1)}, s32[]{:T(128)}) %tuple.35), condition=%wide.region_3.4_spmd, body=%wide.region_2.3_spmd.sunk | while | flops 196610 | bytes 2752637 | solution.py:25
  13.9 4.9 collective-permute-start
  18.8 4.7 collective-permute-done
  28.0 4.7 collective-permute-done
  37.3 4.7 collective-permute-done
  46.5 4.7 collective-permute-done
  55.7 4.7 collective-permute-done
  64.9 4.7 collective-permute-done
  74.1 4.7 collective-permute-done
  83.3 4.7 collective-permute-done
  92.5 4.7 collective-permute-done
  101.7 4.7 collective-permute-done
  110.9 4.7 collective-permute-done
  120.1 4.7 collective-permute-done
  129.3 4.7 collective-permute-done
  138.5 4.7 collective-permute-done
  147.7 4.7 collective-permute-done
  156.9 4.7 collective-permute-done
  166.1 4.7 collective-permute-done
  175.3 4.7 collective-permute-done
  184.5 4.7 collective-permute-done
  193.7 4.7 collective-permute-done
  207.7 4.9 collective-permute-start
  212.6 4.7 collective-permute-done
  217.4 5.6 collective-permute-start
  223.0 4.7 collective-permute-done
  227.8 5.6 collective-permute-start
  238.2 5.6 collective-permute-start
  248.6 5.6 collective-permute-start
  259.1 5.6 collective-permute-start
  264.7 4.7 collective-permute-done
  269.5 5.6 collective-permute-start
  275.1 4.7 collective-permute-done
  279.9 5.6 collective-permute-start
  285.5 4.7 collective-permute-done
  290.3 5.6 collective-permute-start
  300.7 5.6 collective-permute-start
  317.3 141.4 %reduce-scatter.7.cloned.1.call-done = bf16[384,256]{1,0:T(8,128)(2,1)} async-done(((bf16[3072,256]{1,0:T(8,128)(2,1)}), bf16[384,256]{1,0:T(8,128)(2,1)}) %reduce-scatter.7.cloned.1.call-update) | async-done | bytes 196624
  465.2 42.2 %all-gather.5.cloned.1.call-done = bf16[256,3072]{1,0:T(8,128)(2,1)} async-done(((bf16[256,384]{1,0:T(8,128)(2,1)}), bf16[256,3072]{1,0:T(8,128)(2,1)}) %all-gather.5.cloned.1.call-update) | async-done | bytes 1572880 | tf_op jit(solution)/shard_map/all_gather | solution.py:71
  509.1 92.5 %all-gather.7.cloned.1.call-done = bf16[3072,768]{1,0:T(8,128)(2,1)} async-done(((bf16[96,768]{1,0:T(8,128)(2,1)}), bf16[3072,768]{1,0:T(8,128)(2,1)}) %all-gather.7.cloned.1.call-update) | async-done | bytes 4718608 | tf_op jit(solution)/shard_map/all_gather | solution.py:79
  606.1 83.7 %all-gather.9.cloned.1.call-done = bf16[3072,768]{1,0:T(8,128)(2,1)} async-done(((bf16[96,768]{1,0:T(8,128)(2,1)}), bf16[3072,768]{1,0:T(8,128)(2,1)}) %all-gather.9.cloned.1.call-update) | async-done | bytes 4718608 | tf_op jit(solution)/shard_map/all_gather | solution.py:77
  693.9 84.2 %all-gather.11.cloned.1.call-done = bf16[3072,768]{1,0:T(8,128)(2,1)} async-done(((bf16[96,768]{1,0:T(8,128)(2,1)}), bf16[3072,768]{1,0:T(8,128)(2,1)}) %all-gather.11.cloned.1.call-update) | async-done | bytes 4718608 | tf_op jit(solution)/shard_map/all_gather | solution.py:78
  783.5 292.3 %while.21 = (s32[]{:T(128)}, f32[6,128,128]{2,1,0:T(8,128)S(1)}, f32[6]{0:T(128)S(1)}, f32[6,128,128]{2,1,0:T(8,128)S(1)}, s32[]{:T(128)}) while((s32[]{:T(128)}, f32[6,128,128]{2,1,0:T(8,128)S(1)}, f32[6]{0:T(128)S(1)}, f32[6,128,128]{2,1,0:T(8,128)S(1)}, s32[]{:T(128)}) %tuple.38), condition=%wide.region_10.11_spmd, body=%wide.region_9.10_spmd.sunk | while | flops 196610 | bytes 2752637 | solution.py:25
  795.7 4.7 collective-permute-done.1
  814.1 4.7 collective-permute-done.1
  832.5 4.7 collective-permute-done.1
  860.1 4.7 collective-permute-done.1
  878.5 4.7 collective-permute-done.1
  896.9 4.7 collective-permute-done.1
  915.3 4.7 collective-permute-done.1
  933.7 4.7 collective-permute-done.1
  952.1 4.7 collective-permute-done.1
  970.6 4.7 collective-permute-done.1
  989.0 4.7 collective-permute-done.1
  1003.0 5.0 collective-permute-start.1
  1012.8 5.6 collective-permute-start.1
  1023.2 5.6 collective-permute-start.1
  1033.6 5.6 collective-permute-start.1
  1044.0 5.6 collective-permute-start.1
  1049.6 4.7 collective-permute-done.1
  1054.4 5.6 collective-permute-start.1
  1060.0 4.7 collective-permute-done.1
  1064.8 6.2 collective-permute-start.1
  1081.9 142.8 %reduce-scatter.9.cloned.1.call-done = bf16[384,256]{1,0:T(8,128)(2,1)} async-done(((bf16[3072,256]{1,0:T(8,128)(2,1)}), bf16[384,256]{1,0:T(8,128)(2,1)}) %reduce-scatter.9.cloned.1.call-update) | async-done | bytes 196624
  (221 shorter events, 354.2 us)
Async XLA Ops:
  6.5 452.2 %reduce-scatter.7.cloned.1.call-start = ((), (), s32[]{:S(2)}) async-start(), calls=%async_computation.6 | async-start | bytes 1769472
  13.9 9.7 collective-permute-start
  23.6 9.1 collective-permute-start
  32.9 9.1 collective-permute-start
  42.1 9.1 collective-permute-start
  51.3 9.1 collective-permute-start
  60.5 9.1 collective-permute-start
  69.7 9.1 collective-permute-start
  78.9 9.1 collective-permute-start
  88.1 9.1 collective-permute-start
  97.3 9.1 collective-permute-start
  106.5 9.1 collective-permute-start
  115.7 9.1 collective-permute-start
  124.9 9.1 collective-permute-start
  134.1 9.1 collective-permute-start
  143.3 9.1 collective-permute-start
  152.5 9.1 collective-permute-start
  161.7 9.1 collective-permute-start
  170.9 9.1 collective-permute-start
  180.1 9.1 collective-permute-start
  189.3 9.1 collective-permute-start
  198.5 9.1 collective-permute-start
  207.7 9.6 collective-permute-start
  217.4 10.3 collective-permute-start
  227.8 10.3 collective-permute-start
  238.2 10.3 collective-permute-start
  248.6 10.3 collective-permute-start
  259.1 10.3 collective-permute-start
  269.5 10.3 collective-permute-start
  279.9 10.3 collective-permute-start
  290.3 10.3 collective-permute-start
  300.7 10.3 collective-permute-start
  317.2 190.1 %all-gather.5.cloned.1.call-start = ((), (), s32[]{:S(2)}) async-start(), calls=%async_computation.2 | async-start | bytes 1769472 | tf_op jit(solution)/shard_map/all_gather | solution.py:71
  460.5 141.1 %all-gather.7.cloned.1.call-start = ((), (), s32[]{:S(2)}) async-start(), calls=%async_computation.3 | async-start | bytes 4866048 | tf_op jit(solution)/shard_map/all_gather | solution.py:79
  461.3 228.5 %all-gather.9.cloned.1.call-start = ((), (), s32[]{:S(2)}) async-start(), calls=%async_computation.4 | async-start | bytes 4866048 | tf_op jit(solution)/shard_map/all_gather | solution.py:77
  461.9 316.2 %all-gather.11.cloned.1.call-start = ((), (), s32[]{:S(2)}) async-start(), calls=%async_computation.5 | async-start | bytes 4866048 | tf_op jit(solution)/shard_map/all_gather | solution.py:78
  462.4 762.2 %reduce-scatter.9.cloned.1.call-start = ((), (), s32[]{:S(2)}) async-start(), calls=%async_computation.7 | async-start | bytes 1769472
  791.3 9.1 collective-permute-start.1
  800.5 9.1 collective-permute-start.1
  809.7 9.1 collective-permute-start.1
  818.9 9.1 collective-permute-start.1
  828.1 9.1 collective-permute-start.1
  837.3 9.1 collective-permute-start.1
  846.5 9.1 collective-permute-start.1
  855.7 9.1 collective-permute-start.1
  864.9 9.1 collective-permute-start.1
  874.1 9.1 collective-permute-start.1
  883.3 9.1 collective-permute-start.1
  892.5 9.1 collective-permute-start.1
  901.7 9.1 collective-permute-start.1
  910.9 9.1 collective-permute-start.1
  920.1 9.1 collective-permute-start.1
  929.3 9.1 collective-permute-start.1
  938.5 9.1 collective-permute-start.1
  947.7 9.1 collective-permute-start.1
  966.2 9.1 collective-permute-start.1
  984.6 9.1 collective-permute-start.1
  1003.0 9.7 collective-permute-start.1
  1012.8 10.3 collective-permute-start.1
  1023.2 10.3 collective-permute-start.1
  1033.6 10.3 collective-permute-start.1
  1044.0 10.3 collective-permute-start.1
  1054.4 10.3 collective-permute-start.1
  1064.8 10.9 collective-permute-start.1
  (13 other events, 1533.8 us)
Sparse Core Ops, SparseCore 0:
  317.3 141.3 reduce-scatter.6
  460.7 46.6 all-gather.4
  510.1 91.4 all-gather.6
  604.2 85.5 all-gather.8
  692.4 85.5 all-gather.10
  1082.0 142.5 reduce-scatter.8
where the time goes:
time: 1240 us; the launch traced here: 1230 us
  waiting for transfers between devices  880 us (71%)
  starting transfers between devices  291 us (23%)
  matrix products  23.4 us (2%)
  other arithmetic  16.9 us (1%)
  between operations  13.8 us (1%)
    ppermute x62, waiting for transfers between devices, shifted(): return lax.ppermute(shard, axis, pairs)  291 us
    ppermute x62, starting transfers between devices, shifted(): return lax.ppermute(shard, axis, pairs)  291 us
    unnamed x8, waiting for transfers between devices  286 us
    all_gather x1, waiting for transfers between devices, local(): lax.all_gather(wv2, 'seq', axis=0, tiled=True)  92.5 us
    all_gather x1, waiting for transfers between devices, local(): lax.all_gather(wk2, 'seq', axis=0, tiled=True)  84.2 us
    all_gather x1, waiting for transfers between devices, local(): lax.all_gather(wq2, 'seq', axis=0, tiled=True)  83.7 us
    all_gather x1, waiting for transfers between devices, local(): whole = lax.all_gather(stream, 'head', axis=1, tiled=True)  42.2 us
  transfers between devices with their start and end apart: 68, of which 68 were waited for; matrix products, arithmetic and copies ran while one was open for 1% of the time, Pallas kernels for 0%

commit v1 on v0

v1 whole, which is shorter than its diff:
```python
import functools

import jax
import jax.numpy as jnp
from jax import lax
from jax.experimental import pallas as pl
from jax.experimental.pallas import tpu as pltpu
from jax.sharding import Mesh
from jax.sharding import PartitionSpec as P

DH = 128
BLK = 256
TOK = 512
HC = 3
HW = HC * DH
NCHIP = 16
SUB = DH // NCHIP
PIECE = 32
WIDTH = 384
NHEAD = 8
SWAP = [(0, 1), (1, 0)]
VMEM = 40 * 1024 * 1024


def silu(u):
    return u / (1.0 + jnp.exp(-u))


def attn_core(qs, ks, vs, dec, pieces_ref, intra_ref, cum_ref):
    row = lax.broadcasted_iota(jnp.int32, (TOK, TOK), 0)
    col = lax.broadcasted_iota(jnp.int32, (TOK, TOK), 1)
    tri = (row >= col).astype(jnp.float32)
    cum = jnp.dot(tri, dec, preferred_element_type=jnp.float32, precision=lax.Precision.HIGHEST)
    cum_ref[...] = cum
    across = cum.T
    lower = lax.broadcasted_iota(jnp.int32, (BLK, BLK), 0) >= lax.broadcasted_iota(
        jnp.int32, (BLK, BLK), 1
    )
    states = []
    decays = jnp.zeros((SUB, DH), jnp.float32)
    slot = lax.broadcasted_iota(jnp.int32, (SUB, DH), 0)
    for h in range(HC):
        cols = slice(h * DH, (h + 1) * DH)
        q, k, v = qs[:, cols], ks[:, cols], vs[:, cols]
        ch = cum[:, h : h + 1]
        rh = across[h : h + 1, :]
        for i in range(2):
            rows = slice(i * BLK, (i + 1) * BLK)
            parts = []
            for j in range(i + 1):
                keys = slice(j * BLK, (j + 1) * BLK)
                scores = lax.dot_general(
                    q[rows], k[keys], (((1,), (1,)), ((), ())), preferred_element_type=jnp.float32
                )
                spread = ch[rows] - rh[:, keys]
                if i == j:
                    factor = jnp.where(lower, jnp.exp(jnp.where(lower, spread, 0.0)), 0.0)
                else:
                    factor = jnp.exp(spread)
                weights = (scores * factor).astype(jnp.bfloat16)
                parts.append(jnp.dot(weights, v[keys], preferred_element_type=jnp.float32))
            intra_ref[rows, cols] = parts[0] if i == 0 else parts[0] + parts[1]
        last = cum[TOK - 1 : TOK, h : h + 1]
        kt = (k.astype(jnp.float32) * jnp.exp(last - ch)).astype(jnp.bfloat16)
        state = lax.dot_general(
            kt, v, (((0,), (0,)), ((), ())), preferred_element_type=jnp.float32
        )
        states.append(state.reshape(NCHIP, SUB, DH))
        total = jnp.exp(last)
        high = total.astype(jnp.bfloat16).astype(jnp.float32)
        decays = jnp.where(slot == h, high, decays)
        decays = jnp.where(slot == HC + h, total - high, decays)
    states.append(jnp.broadcast_to(decays[None], (NCHIP, SUB, DH)))
    pieces_ref[...] = jnp.concatenate(states, axis=1).astype(jnp.bfloat16)


def first_kernel(place, q_ref, k_ref, v_ref, other_ref, dec_ref, pieces_ref, intra_ref, cum_ref, qs, ks, vs):
    core = place[0]
    mine = pl.ds(pl.multiple_of(core * BLK, BLK), BLK)
    yours = pl.ds(pl.multiple_of((1 - core) * BLK, BLK), BLK)
    cols = pl.ds(pl.multiple_of(core * HW, DH), HW)
    for n, (src, dst) in enumerate(((q_ref, qs), (k_ref, ks), (v_ref, vs))):
        dst[mine, :] = silu(src[:, cols].astype(jnp.float32)).astype(jnp.bfloat16)
        dst[yours, :] = silu(other_ref[:, n * HW : (n + 1) * HW].astype(jnp.float32)).astype(
            jnp.bfloat16
        )
    attn_core(qs, ks, vs, dec_ref[...], pieces_ref, intra_ref, cum_ref)


def core_outs():
    return (
        jax.ShapeDtypeStruct((NCHIP, PIECE, DH), jnp.bfloat16),
        jax.ShapeDtypeStruct((TOK, HW), jnp.float32),
        jax.ShapeDtypeStruct((TOK, DH), jnp.float32),
        jax.ShapeDtypeStruct((TOK, HW), jnp.bfloat16),
    )


def whole(shape):
    return pl.BlockSpec(shape, lambda *_: (0,) * len(shape))


def first_prep(place, q, k, v, other, dec):
    outs = core_outs()
    return pl.pallas_call(
        first_kernel,
        out_shape=outs,
        grid_spec=pltpu.PrefetchScalarGridSpec(
            num_scalar_prefetch=1,
            grid=(1,),
            in_specs=[whole(a.shape) for a in (q, k, v, other, dec)],
            out_specs=[whole(o.shape) for o in outs],
            scratch_shapes=[pltpu.VMEM((TOK, HW), jnp.bfloat16)] * 2,
        ),
        compiler_params=pltpu.CompilerParams(vmem_limit_bytes=VMEM),
        name="first_prep",
    )(place, q, k, v, other, dec)


def second_kernel(
    place, mine_ref, yours_ref, wa_ref, wb_ref, gain_ref, dec_ref,
    pieces_ref, intra_ref, cum_ref, qs, ks, vs, scale, acc,
):
    core, side = place[0], place[1]
    step = pl.program_id(0)
    half = NHEAD // 2

    @pl.when(step == 0)
    def _():
        for n, src in enumerate((mine_ref, yours_ref)):
            total = jnp.zeros((BLK, 1), jnp.float32)
            for i in range(NHEAD):
                wide = src[i].astype(jnp.float32)
                total = total + jnp.sum(wide * wide, axis=-1, keepdims=True)
            root = lax.rsqrt(total / (NHEAD * WIDTH) + 1e-06)
            scale[n * BLK : (n + 1) * BLK, :] = jnp.broadcast_to(root, (BLK, DH))
        acc[...] = jnp.zeros_like(acc)

    chunk = jnp.where(step < half, side * half + step, (1 - side) * half + step - half)
    gain = gain_ref[chunk]

    def normed(src, n):
        root = scale[n * BLK : (n + 1) * BLK, 0:1]
        return (src[chunk].astype(jnp.float32) * root * gain).astype(jnp.bfloat16)

    rows = jnp.concatenate([normed(mine_ref, 0), normed(yours_ref, 1)], axis=0)

    @pl.when(step < half)
    def _():
        acc[...] += jnp.dot(rows, wa_ref[...], preferred_element_type=jnp.float32)

    @pl.when(step >= half)
    def _():
        acc[...] += jnp.dot(rows, wb_ref[...], preferred_element_type=jnp.float32)

    @pl.when(step == NHEAD - 1)
    def _():
        first = pl.ds(pl.multiple_of(core * BLK, BLK), BLK)
        second = pl.ds(pl.multiple_of((1 - core) * BLK, BLK), BLK)
        for n, dst in enumerate((ks, vs, qs)):
            cols = slice(n * HW, (n + 1) * HW)
            dst[first, :] = silu(acc[:BLK, cols]).astype(jnp.bfloat16)
            dst[second, :] = silu(acc[BLK:, cols]).astype(jnp.bfloat16)
        attn_core(qs, ks, vs, dec_ref[...], pieces_ref, intra_ref, cum_ref)


def second_prep(place, mine, yours, wa, wb, gain, dec):
    outs = core_outs()
    half = NHEAD // 2
    return pl.pallas_call(
        second_kernel,
        out_shape=outs,
        grid_spec=pltpu.PrefetchScalarGridSpec(
            num_scalar_prefetch=1,
            grid=(NHEAD,),
            in_specs=[
                whole(mine.shape),
                whole(yours.shape),
                pl.BlockSpec((WIDTH, 3 * HW), lambda i, *_: (jnp.minimum(i, half - 1), 0)),
                pl.BlockSpec((WIDTH, 3 * HW), lambda i, *_: (jnp.maximum(i - half, 0), 0)),
                whole(gain.shape),
                whole(dec.shape),
            ],
            out_specs=[whole(o.shape) for o in outs],
            scratch_shapes=[
                pltpu.VMEM((TOK, HW), jnp.bfloat16),
                pltpu.VMEM((TOK, HW), jnp.bfloat16),
                pltpu.VMEM((TOK, DH), jnp.float32),
                pltpu.VMEM((TOK, 3 * HW), jnp.float32),
            ],
        ),
        compiler_params=pltpu.CompilerParams(vmem_limit_bytes=VMEM),
        name="second_prep",
    )(place, mine, yours, wa, wb, gain, dec)


def scan_kernel(in_ref, out_ref):
    states = [jnp.zeros((SUB, DH), jnp.float32) for _ in range(HC)]
    empty = jnp.zeros((PIECE - HC * SUB, DH), jnp.float32)
    for p in range(NCHIP):
        piece = in_ref[p].astype(jnp.float32)
        out_ref[p] = jnp.concatenate(states + [empty], axis=0).astype(jnp.bfloat16)
        decays = piece[HC * SUB :]
        for h in range(HC):
            decay = decays[h : h + 1] + decays[HC + h : HC + h + 1]
            states[h] = states[h] * decay + piece[h * SUB : (h + 1) * SUB]


def scan(pieces):
    return pl.pallas_call(
        scan_kernel,
        out_shape=jax.ShapeDtypeStruct(pieces.shape, pieces.dtype),
        name="scan",
    )(pieces)


def finish_kernel(place, pieces_ref, intra_ref, cum_ref, qs_ref, gain_ref, mine_ref, yours_ref, out):
    core = place[0]
    pieces = pieces_ref[...].astype(jnp.float32)
    for h in range(HC):
        cols = slice(h * DH, (h + 1) * DH)
        state = pieces[:, h * SUB : (h + 1) * SUB].reshape(DH, DH).astype(jnp.bfloat16)
        carried = jnp.dot(qs_ref[:, cols], state, preferred_element_type=jnp.float32)
        att = intra_ref[:, cols] + carried * jnp.exp(cum_ref[:, h : h + 1])
        square = jnp.mean(att * att, axis=-1, keepdims=True)
        out[:, cols] = (att * lax.rsqrt(square + 1e-06) * gain_ref[:, cols]).astype(jnp.bfloat16)
    mine_ref[...] = out[pl.ds(pl.multiple_of(core * BLK, BLK), BLK), :]
    yours_ref[...] = out[pl.ds(pl.multiple_of((1 - core) * BLK, BLK), BLK), :]


def finish(place, pieces, intra, cum, qs, gain):
    args = (pieces, intra, cum, qs, gain)
    return pl.pallas_call(
        finish_kernel,
        out_shape=(jax.ShapeDtypeStruct((BLK, HW), jnp.bfloat16),) * 2,
        grid_spec=pltpu.PrefetchScalarGridSpec(
            num_scalar_prefetch=1,
            grid=(1,),
            in_specs=[whole(a.shape) for a in args],
            out_specs=[whole((BLK, HW))] * 2,
            scratch_shapes=[pltpu.VMEM((TOK, HW), jnp.bfloat16)],
        ),
        compiler_params=pltpu.CompilerParams(vmem_limit_bytes=VMEM),
        name="finish",
    )(place, *args)


def project_kernel(place, mine_ref, yours_ref, w_ref, out_ref):
    core = place[0]
    top = pl.ds(pl.multiple_of(core * HW, DH), HW)
    low = pl.ds(pl.multiple_of((1 - core) * HW, DH), HW)
    term = jnp.dot(mine_ref[...], w_ref[top, :], preferred_element_type=jnp.float32)
    term = term + jnp.dot(yours_ref[...], w_ref[low, :], preferred_element_type=jnp.float32)
    out_ref[0] = term.astype(jnp.bfloat16)


def project(place, mine, yours, w):
    return pl.pallas_call(
        project_kernel,
        out_shape=jax.ShapeDtypeStruct((NHEAD, BLK, WIDTH), jnp.bfloat16),
        grid_spec=pltpu.PrefetchScalarGridSpec(
            num_scalar_prefetch=1,
            grid=(NHEAD,),
            in_specs=[
                whole(mine.shape),
                whole(yours.shape),
                pl.BlockSpec((2 * HW, WIDTH), lambda i, *_: (0, i)),
            ],
            out_specs=pl.BlockSpec((1, BLK, WIDTH), lambda i, *_: (i, 0, 0)),
        ),
        compiler_params=pltpu.CompilerParams(vmem_limit_bytes=VMEM),
        name="project",
    )(place, mine, yours, w)


def exchange(parts, axes):
    return lax.all_to_all(parts, axes, 0, 0)


def rest(place, prepared, gain, w):
    pieces, intra, cum, qs = prepared
    before = exchange(scan(exchange(pieces, ("yh", "z"))), ("yh", "z"))
    mine, yours = finish(place, before, intra, cum, qs, gain)
    yours = lax.ppermute(yours, "c", SWAP)
    terms = exchange(project(place, mine, yours, w), ("x", "yl"))
    return jnp.sum(terms.astype(jnp.float32), axis=0)


def local(
    q1, k1, v1, decay1, gain_out1, wo1, stream_in, gain_in2, wq2, wk2, wv2, decay2, gain_out2, wo2
):
    core = lax.axis_index("c")
    place = jnp.stack([core, lax.axis_index("yh")]).astype(jnp.int32)

    def cut(arrays, which):
        return jnp.concatenate(
            [lax.dynamic_slice_in_dim(a, which * HW, HW, axis=1) for a in arrays], axis=1
        )

    def in_order(own, other):
        first = jnp.where(core == 0, own, other)
        second = jnp.where(core == 0, other, own)
        return jnp.concatenate([first, second], axis=0)

    weights = (wk2, wv2, wq2)
    other_w = lax.ppermute(cut(weights, 1 - core), "c", SWAP)
    chip_w = in_order(cut(weights, core), other_w)
    far_w = lax.ppermute(chip_w, "yh", SWAP)
    wa = lax.all_gather(chip_w, "z", axis=0, tiled=True)
    wb = lax.all_gather(far_w, "z", axis=0, tiled=True)

    other = lax.ppermute(cut((q1, k1, v1), 1 - core), "c", SWAP)
    both = jnp.concatenate([decay1, decay2], axis=1)
    decays = in_order(both, lax.ppermute(both, "c", SWAP))

    def lanes(start):
        part = lax.dynamic_slice_in_dim(decays, start, HC, axis=1)
        return jnp.pad(part, ((0, 0), (0, DH - HC)))

    def own_gain(gain):
        return lax.dynamic_slice_in_dim(gain, core * HW, HW, axis=0)[None]

    prepared = first_prep(place, q1, k1, v1, other, lanes(core * HC))
    first_share = rest(place, prepared, own_gain(gain_out1), wo1)
    stream = (stream_in.astype(jnp.float32) + first_share).astype(jnp.bfloat16)
    mine = exchange(jnp.broadcast_to(stream[None], (NHEAD, BLK, WIDTH)), ("x", "yl"))
    yours = lax.ppermute(mine, "c", SWAP)
    prepared = second_prep(
        place, mine, yours, wa, wb, gain_in2.reshape(NHEAD, 1, WIDTH), lanes(2 * HC + core * HC)
    )
    second_share = rest(place, prepared, own_gain(gain_out2), wo2)
    return (stream.astype(jnp.float32) + second_share).astype(jnp.bfloat16)


def solution(mesh):
    fine = Mesh(mesh.devices.reshape(2, 8, 2, 4, 2), ("yh", "z", "c", "x", "yl"))
    seq, head = ("yh", "z", "c"), ("x", "yl")
    placed = (
        P(seq, head),
        P(seq, head),
        P(seq, head),
        P(seq, head),
        P(head),
        P(head, None),
        P(seq, head),
        P(),
        P(seq, head),
        P(seq, head),
        P(seq, head),
        P(seq, head),
        P(head),
        P(head, None),
    )
    return jax.shard_map(
        local, mesh=fine, in_specs=placed, out_specs=P(seq, head), check_vma=False
    )
```

time: 1240 us -> 229 us (0.18)
  waiting for transfers between devices: 880 us -> 35.7 us
  starting transfers between devices: 291 us -> 22.5 us
  blocking collectives: 0 us -> 102 us
  Pallas kernels: 0 us -> 31.9 us
  matrix products: 23.4 us -> 0 us
  other arithmetic: 16.9 us -> 2.25 us
  local copies, waits for them, and re-layouts: 7.42 us -> 20.8 us
    all_gather x4 -> x2, waiting for transfers between devices: 302 us -> 0.01 us  [the longest x1 0.01 us: local(): wa = lax.all_gather(chip_w, 'z', axis=0, tiled=True)]
    unnamed x8 -> x2, waiting for transfers between devices: 286 us -> 0.03 us
    ppermute x62 -> x7, starting transfers between devices: 291 us -> 14.3 us  [the longest x2 5.51 us: rest(): yours = lax.ppermute(yours, 'c', SWAP)]
    ppermute x62 -> x7, waiting for transfers between devices: 291 us -> 17.7 us  [the longest x1 11.8 us: local(): far_w = lax.ppermute(chip_w, 'yh', SWAP)]
    all_to_all x0 -> x5, blocking collectives: none -> 102 us  [exchange(): return lax.all_to_all(parts, axes, 0, 0)]
    pallas_call x0 -> x8, Pallas kernels: none -> 31.9 us  [the longest x1 13.1 us: second_prep(): pl.pallas_call(second_kernel, out_shape=outs, grid_spec=pltpu.PrefetchSca...]
    dot_general x11 -> x0, matrix products: 23.4 us -> none  [the longest x3 12 us: local(): jnp.dot(normed_in, piece_now, preferred_element_type=jnp.float32)]
    all_to_all x0 -> x2, waiting for transfers between devices: none -> 18 us  [exchange(): return lax.all_to_all(parts, axes, 0, 0)]
  transfers between devices with their start and end apart: 68 -> 11, of which waited for: 68 -> 8; matrix products, arithmetic and copies ran while one was open for 1% -> 1% of each run, Pallas kernels for 0% -> 5%
where the time goes in v1:
time: 229 us; the launch traced here: 228 us
  blocking collectives  102 us (45%)
  waiting for transfers between devices  35.7 us (16%)
  Pallas kernels  31.9 us (14%)
  starting transfers between devices  22.5 us (10%)
  local copies, waits for them, and re-layouts  20.8 us (9%)
  between operations  13.7 us (6%)
    all_to_all x5, blocking collectives, exchange(): return lax.all_to_all(parts, axes, 0, 0)  102 us
    all_to_all x2, waiting for transfers between devices, exchange(): return lax.all_to_all(parts, axes, 0, 0)  18 us
    unnamed x46, local copies, waits for them, and re-layouts  17.4 us
    pallas_call x1, Pallas kernels, second_prep(): pl.pallas_call(second_kernel, out_shape=outs, grid_spec=pltpu.PrefetchSca...  13.1 us
    ppermute x1, waiting for transfers between devices, local(): far_w = lax.ppermute(chip_w, 'yh', SWAP)  11.8 us
    pallas_call x2, Pallas kernels, project(): pl.pallas_call(project_kernel, out_shape=jax.ShapeDtypeStruct((NHEAD, BLK...  8.68 us
    all_to_all x2, starting transfers between devices, exchange(): return lax.all_to_all(parts, axes, 0, 0)  8.18 us
    ppermute x2, starting transfers between devices, rest(): yours = lax.ppermute(yours, 'c', SWAP)  5.51 us
  transfers between devices with their start and end apart: 11, of which 8 were waited for; matrix products, arithmetic and copies ran while one was open for 1% of the time, Pallas kernels for 5%

profile of v1, /device:TPU:1, one launch (start us, length us, event | category | flops | bytes accessed | tf_op | source)
XLA Modules:
  0.0 228.5 jit_solution(9816952776544847599)
XLA Ops:
  6.5 0.9 constant_dynamic-slice_fusion.5
  7.5 0.0 copy-start.4
  7.5 1.1 constant_dynamic-slice_fusion.3
  8.6 0.0 copy-start.5
  8.6 0.0 copy-start.6
  8.6 3.3 %collective-permute-start.4 = (bf16[96,1152]{1,0:T(8,128)(2,1)S(1)}, bf16[96,1152]{1,0:T(8,128)(2,1)S(1)}, u32[]{:S(2)}, u32[]{:S(2)}) collective-permute-start(bf16[96,1152]{1,0:T(8,128)(2,1)S(1)} %pad_maximum_fusion.3), channel_id=1, source_target_pairs={{0,8},{8,0},{1,9},{9,1},{2,10},{10,2},{3,11},{11,3},{4,12},{12,4},... | collective-permute-start | bytes 663560 | tf_op jit(solution)/shard_map/ppermute | solution.py:306
  12.0 1.1 collective-permute-done.4
  13.1 0.1 broadcast_select_fusion.1
  13.1 0.8 pad_maximum_fusion.1
  13.9 0.0 all-gather.3.cloned.1.call-update
  14.0 0.0 all-gather.5.cloned.1.call-start
  14.0 1.3 collective-permute-start.5
  15.4 11.8 %collective-permute-done.5 = bf16[192,1152]{1,0:T(8,128)(2,1)S(1)} collective-permute-done((bf16[192,1152]{1,0:T(8,128)(2,1)}, bf16[192,1152]{1,0:T(8,128)(2,1)S(1)}, u32[]{:S(2)}, u32[]{:S(2)}) %collective-permute-start.5) | collective-permute-done | bytes 442400 | tf_op jit(solution)/shard_map/ppermute | solution.py:308
  27.2 0.8 copy-done.16
  28.0 0.0 all-gather.5.cloned.1.call-update
  28.0 0.1 pad_maximum_fusion
  28.1 1.3 collective-permute-start
  29.4 0.1 collective-permute-start.1
  29.5 0.1 pad_add_fusion.place
  29.6 1.4 collective-permute-done.1
  31.1 0.1 copy.19
  31.3 4.5 %first_prep.1 = (bf16[16,32,128]{2,1,0:T(8,128)(2,1)S(1)}, f32[512,384]{1,0:T(8,128)S(1)}, f32[512,128]{1,0:T(8,128)S(1)}, bf16[512,384]{1,0:T(8,128)(2,1)S(1)}) custom-call(s32[2]{0:T(128)S(1)} %pad_add_fusion.place, bf16[256,768]{1,0:T(8,128)(2,1)S(1)} %copy-done.4, bf16[256,768]{1,0:T(8,128)(2,1)S(1)} %copy-done.5, bf16[256,768]{1,0:T(8,128)(2,1)S(1)} %copy-done.6, ...), custom_call_target="tpu_custom_call" | custom-call | tf_op jit(solution)/shard_map/first_prep/pallas_call | solution.py:105
  35.8 19.5 %all_to_all.35.in_ref = bf16[16,32,128]{2,1,0:T(8,128)(2,1)} all-to-all(bf16[16,32,128]{2,1,0:T(8,128)(2,1)S(1)} %get-tuple-element.17), channel_id=1, replica_groups=mesh['yh'=2,'z'=8,'c'=2,'x'=4,'yl'=2] {'yh','z'}, dimensions={0} | all-to-all | bytes 262144 | tf_op jit(solution)/shard_map/all_to_all | solution.py:277
  55.3 1.6 scan.2
  56.9 4.2 %all-to-all-start.1 = ((bf16[16,32,128]{2,1,0:T(8,128)(2,1)}), bf16[16,32,128]{2,1,0:T(8,128)(2,1)S(1)}, u32[]{:S(2)}, u32[]{:S(2)}) async-start(bf16[16,32,128]{2,1,0:T(8,128)(2,1)} %scan.2), calls=%async_computation.1 | async-start | bytes 262144 | tf_op jit(solution)/shard_map/all_to_all | solution.py:277
  61.1 0.1 dynamic_slice.43
  61.2 9.1 %all-to-all-done.1.pieces_ref = bf16[16,32,128]{2,1,0:T(8,128)(2,1)S(1)} async-done(((bf16[16,32,128]{2,1,0:T(8,128)(2,1)}), bf16[16,32,128]{2,1,0:T(8,128)(2,1)S(1)}, u32[]{:S(2)}, u32[]{:S(2)}) %all-to-all-start.1) | async-done | bytes 131104 | tf_op jit(solution)/shard_map/all_to_all | solution.py:277
  70.3 1.3 finish.2
  71.6 2.8 %collective-permute-start.2 = (bf16[256,384]{1,0:T(8,128)(2,1)S(1)}, bf16[256,384]{1,0:T(8,128)(2,1)S(1)}, u32[]{:S(2)}, u32[]{:S(2)}) collective-permute-start(bf16[256,384]{1,0:T(8,128)(2,1)S(1)} %get-tuple-element.22), channel_id=1, source_target_pairs={{0,8},{8,0},{1,9},{9,1},{2,10},{10,2},{3,11},{11,3},{4,12},{12,4},... | collective-permute-start | bytes 589832 | tf_op jit(solution)/shard_map/ppermute | solution.py:284
  74.4 1.1 collective-permute-done.2.yours_ref
  75.5 2.3 %copy-done = bf16[768,3072]{1,0:T(8,128)(2,1)S(1)} copy-done((bf16[768,3072]{1,0:T(8,128)(2,1)S(1)}, bf16[768,3072]{1,0:T(8,128)(2,1)}, u32[]{:S(2)}) %copy-start) | copy-done | bytes 4718616
  77.8 4.3 %project.2 = bf16[8,256,384]{2,1,0:T(8,128)(2,1)S(1)} custom-call(s32[2]{0:T(128)S(1)} %pad_add_fusion.place, bf16[256,384]{1,0:T(8,128)(2,1)S(1)} %get-tuple-element.21.mine_ref, bf16[256,384]{1,0:T(8,128)(2,1)S(1)} %collective-permute-done.2.yours_ref, bf16[768,3072]{1,0:T(8,128)(2,1)S(1)} %copy-done), custom_call_target="tpu_custom_call" | custom-call | tf_op jit(solution)/shard_map/project/pallas_call | solution.py:258
  82.1 23.8 %all_to_all.36 = bf16[8,256,384]{2,1,0:T(8,128)(2,1)S(1)} all-to-all(bf16[8,256,384]{2,1,0:T(8,128)(2,1)S(1)} %project.2), channel_id=1, replica_groups=mesh['yh'=2,'z'=8,'c'=2,'x'=4,'yl'=2] {'x','yl'}, dimensions={0} | all-to-all | bytes 3145728 | tf_op jit(solution)/shard_map/all_to_all | solution.py:277
  105.9 0.2 convert_reduce_fusion.1
  106.1 0.7 copy-done.17
  106.9 0.1 broadcast_in_dim.13
  107.1 22.7 %all_to_all.37.mine_ref = bf16[8,256,384]{2,1,0:T(8,128)(2,1)S(1)} all-to-all(bf16[8,256,384]{2,1,0:T(8,128)(2,1)S(1)} %broadcast_in_dim.13), channel_id=1, replica_groups=mesh['yh'=2,'z'=8,'c'=2,'x'=4,'yl'=2] {'x','yl'}, dimensions={0} | all-to-all | bytes 3145728 | tf_op jit(solution)/shard_map/all_to_all | solution.py:277
  129.8 2.8 %collective-permute-start.3 = (bf16[8,256,384]{2,1,0:T(8,128)(2,1)S(1)}, bf16[8,256,384]{2,1,0:T(8,128)(2,1)S(1)}, u32[]{:S(2)}, u32[]{:S(2)}) collective-permute-start(bf16[8,256,384]{2,1,0:T(8,128)(2,1)S(1)} %all_to_all.37.mine_ref), channel_id=1, source_target_pairs={{0,8},{8,0},{1,9},{9,1},{2,10},{10,2},{3,11},{11,3},{4,12},{12,4},... | collective-permute-start | bytes 4718600 | tf_op jit(solution)/shard_map/ppermute | solution.py:327
  132.5 0.9 copy.20
  133.4 1.0 pad.8.dec_ref
  134.4 1.2 collective-permute-done.3.yours_ref
  135.6 2.0 copy-done.2
  137.6 2.0 copy-done.3
  139.6 13.1 %second_prep.1 = (bf16[16,32,128]{2,1,0:T(8,128)(2,1)S(1)}, f32[512,384]{1,0:T(8,128)S(1)}, f32[512,128]{1,0:T(8,128)S(1)}, bf16[512,384]{1,0:T(8,128)(2,1)S(1)}) custom-call(s32[2]{0:T(128)S(1)} %pad_add_fusion.place, bf16[8,256,384]{2,1,0:T(8,128)(2,1)S(1)} %all_to_all.37.mine_ref, bf16[8,256,384]{2,1,0:T(8,128)(2,1)S(1)} %collective-permute-done.3.yours_ref, ...), custom_call_target="tpu_custom_call" | custom-call | tf_op jit(solution)/shard_map/second_prep/pallas_call | solution.py:170
  152.7 0.9 copy-done.7
  153.6 0.7 copy-done.9
  154.3 0.7 copy-done.11
  155.0 12.9 %all_to_all.38.in_ref = bf16[16,32,128]{2,1,0:T(8,128)(2,1)} all-to-all(bf16[16,32,128]{2,1,0:T(8,128)(2,1)S(1)} %get-tuple-element.23), channel_id=1, replica_groups=mesh['yh'=2,'z'=8,'c'=2,'x'=4,'yl'=2] {'yh','z'}, dimensions={0} | all-to-all | bytes 262144 | tf_op jit(solution)/shard_map/all_to_all | solution.py:277
  167.9 1.6 scan.3
  169.5 3.9 %all-to-all-start.5 = ((bf16[16,32,128]{2,1,0:T(8,128)(2,1)}), bf16[16,32,128]{2,1,0:T(8,128)(2,1)S(1)}, u32[]{:S(2)}, u32[]{:S(2)}) async-start(bf16[16,32,128]{2,1,0:T(8,128)(2,1)} %scan.3), calls=%async_computation.5 | async-start | bytes 262144 | tf_op jit(solution)/shard_map/all_to_all | solution.py:277
  173.5 0.1 dynamic_slice.51
  173.6 8.8 %all-to-all-done.5.pieces_ref = bf16[16,32,128]{2,1,0:T(8,128)(2,1)S(1)} async-done(((bf16[16,32,128]{2,1,0:T(8,128)(2,1)}), bf16[16,32,128]{2,1,0:T(8,128)(2,1)S(1)}, u32[]{:S(2)}, u32[]{:S(2)}) %all-to-all-start.5) | async-done | bytes 131104 | tf_op jit(solution)/shard_map/all_to_all | solution.py:277
  182.4 1.1 copy-done.8
  183.5 1.0 copy-done.10
  184.5 0.9 copy-done.12
  185.5 1.2 finish.3
  186.7 2.7 %collective-permute-start.6 = (bf16[256,384]{1,0:T(8,128)(2,1)S(1)}, bf16[256,384]{1,0:T(8,128)(2,1)S(1)}, u32[]{:S(2)}, u32[]{:S(2)}) collective-permute-start(bf16[256,384]{1,0:T(8,128)(2,1)S(1)} %get-tuple-element.28), channel_id=1, source_target_pairs={{0,8},{8,0},{1,9},{9,1},{2,10},{10,2},{3,11},{11,3},{4,12},{12,4},... | collective-permute-start | bytes 589832 | tf_op jit(solution)/shard_map/ppermute | solution.py:284
  189.5 1.1 collective-permute-done.6.yours_ref
  190.5 2.3 %copy-done.1 = bf16[768,3072]{1,0:T(8,128)(2,1)S(1)} copy-done((bf16[768,3072]{1,0:T(8,128)(2,1)S(1)}, bf16[768,3072]{1,0:T(8,128)(2,1)}, u32[]{:S(2)}) %copy-start.1) | copy-done | bytes 4718616
  192.9 4.3 %project.3 = bf16[8,256,384]{2,1,0:T(8,128)(2,1)S(1)} custom-call(s32[2]{0:T(128)S(1)} %pad_add_fusion.place, bf16[256,384]{1,0:T(8,128)(2,1)S(1)} %get-tuple-element.27.mine_ref, bf16[256,384]{1,0:T(8,128)(2,1)S(1)} %collective-permute-done.6.yours_ref, bf16[768,3072]{1,0:T(8,128)(2,1)S(1)} %copy-done.1), custom_call_target="tpu_custom_call" | custom-call | tf_op jit(solution)/shard_map/project/pallas_call | solution.py:258
  197.2 22.8 %all_to_all.39 = bf16[8,256,384]{2,1,0:T(8,128)(2,1)S(1)} all-to-all(bf16[8,256,384]{2,1,0:T(8,128)(2,1)S(1)} %project.3), channel_id=1, replica_groups=mesh['yh'=2,'z'=8,'c'=2,'x'=4,'yl'=2] {'x','yl'}, dimensions={0} | all-to-all | bytes 3145728 | tf_op jit(solution)/shard_map/all_to_all | solution.py:277
  220.0 0.2 convert_reduce_fusion
  220.2 0.7 copy-done.15
  220.9 0.7 add_convert_fusion
  (42 shorter events, 0.3 us)
Async XLA Ops:
  6.5 129.0 %all-gather.3.cloned.1.call-start = ((), (), s32[]{:S(2)}) async-start(), calls=%async_computation.7 | async-start | bytes 3981312 | tf_op jit(solution)/shard_map/all_gather | solution.py:309
  7.5 7.8 %copy-start.4 = (bf16[256,768]{1,0:T(8,128)(2,1)S(1)}, bf16[256,768]{1,0:T(8,128)(2,1)}, u32[]{:S(2)}) copy-start(bf16[256,768]{1,0:T(8,128)(2,1)} %q_ref.1) | copy-start | bytes 1179652
  8.6 6.7 %copy-start.5 = (bf16[256,768]{1,0:T(8,128)(2,1)S(1)}, bf16[256,768]{1,0:T(8,128)(2,1)}, u32[]{:S(2)}) copy-start(bf16[256,768]{1,0:T(8,128)(2,1)} %k_ref.1) | copy-start | bytes 1179652
  8.6 6.7 %copy-start.6 = (bf16[256,768]{1,0:T(8,128)(2,1)S(1)}, bf16[256,768]{1,0:T(8,128)(2,1)}, u32[]{:S(2)}) copy-start(bf16[256,768]{1,0:T(8,128)(2,1)} %v_ref.1) | copy-start | bytes 1179652
  8.6 4.4 %collective-permute-start.4 = (bf16[96,1152]{1,0:T(8,128)(2,1)S(1)}, bf16[96,1152]{1,0:T(8,128)(2,1)S(1)}, u32[]{:S(2)}, u32[]{:S(2)}) collective-permute-start(bf16[96,1152]{1,0:T(8,128)(2,1)S(1)} %pad_maximum_fusion.3), channel_id=1, source_target_pairs={{0,8},{8,0},{1,9},{9,1},{2,10},{10,2},{3,11},{11,3},{4,12},{12,4},... | collective-permute-start | bytes 663560 | tf_op jit(solution)/shard_map/ppermute | solution.py:306
  13.9 15.5 %copy-start.18 = (f32[256,6]{0,1:T(8,128)S(1)}, f32[256,6]{0,1:T(8,128)}, u32[]{:S(2)}) copy-start(f32[256,6]{0,1:T(8,128)} %param.25) | copy-start | bytes 18436
  13.9 15.5 %copy-start.19 = (f32[256,6]{0,1:T(8,128)S(1)}, f32[256,6]{0,1:T(8,128)}, u32[]{:S(2)}) copy-start(f32[256,6]{0,1:T(8,128)} %param.17) | copy-start | bytes 18436
  14.0 121.6 %all-gather.5.cloned.1.call-start = ((), (), s32[]{:S(2)}) async-start(), calls=%async_computation.8 | async-start | bytes 3981312 | tf_op jit(solution)/shard_map/all_gather | solution.py:310
  14.0 13.2 %collective-permute-start.5 = (bf16[192,1152]{1,0:T(8,128)(2,1)}, bf16[192,1152]{1,0:T(8,128)(2,1)S(1)}, u32[]{:S(2)}, u32[]{:S(2)}) collective-permute-start(bf16[192,1152]{1,0:T(8,128)(2,1)} %pad_maximum_fusion.1), channel_id=1, source_target_pairs={{0,128},{128,0},{1,129},{129,1},{2,130},{130,2},{3,131},{131,3},{4... | collective-permute-start | bytes 1327112 | tf_op jit(solution)/shard_map/ppermute | solution.py:308
  27.2 0.8 copy-start.16
  28.1 3.2 %collective-permute-start = (bf16[256,1152]{1,0:T(8,128)(2,1)S(1)}, bf16[256,1152]{1,0:T(8,128)(2,1)S(1)}, u32[]{:S(2)}, u32[]{:S(2)}) collective-permute-start(bf16[256,1152]{1,0:T(8,128)(2,1)S(1)} %pad_maximum_fusion), channel_id=1, source_target_pairs={{0,8},{8,0},{1,9},{9,1},{2,10},{10,2},{3,11},{11,3},{4,12},{12,4},... | collective-permute-start | bytes 1769480 | tf_op jit(solution)/shard_map/ppermute | solution.py:312
  29.4 1.6 collective-permute-start.1
  31.2 29.9 %copy-start.20 = (f32[768]{0:T(1024)S(1)}, f32[768]{0:T(1024)}, u32[]{:S(2)}) copy-start(f32[768]{0:T(1024)} %param.18) | copy-start | bytes 9220
  56.9 13.5 %all-to-all-start.1 = ((bf16[16,32,128]{2,1,0:T(8,128)(2,1)}), bf16[16,32,128]{2,1,0:T(8,128)(2,1)S(1)}, u32[]{:S(2)}, u32[]{:S(2)}) async-start(bf16[16,32,128]{2,1,0:T(8,128)(2,1)} %scan.2), calls=%async_computation.1 | async-start | bytes 262144 | tf_op jit(solution)/shard_map/all_to_all | solution.py:277
  71.6 3.9 %collective-permute-start.2 = (bf16[256,384]{1,0:T(8,128)(2,1)S(1)}, bf16[256,384]{1,0:T(8,128)(2,1)S(1)}, u32[]{:S(2)}, u32[]{:S(2)}) collective-permute-start(bf16[256,384]{1,0:T(8,128)(2,1)S(1)} %get-tuple-element.22), channel_id=1, source_target_pairs={{0,8},{8,0},{1,9},{9,1},{2,10},{10,2},{3,11},{11,3},{4,12},{12,4},... | collective-permute-start | bytes 589832 | tf_op jit(solution)/shard_map/ppermute | solution.py:284
  75.5 2.3 %copy-start = (bf16[768,3072]{1,0:T(8,128)(2,1)S(1)}, bf16[768,3072]{1,0:T(8,128)(2,1)}, u32[]{:S(2)}) copy-start(bf16[768,3072]{1,0:T(8,128)(2,1)} %w_ref.2) | copy-start | bytes 14155780
  105.9 0.9 copy-start.17
  106.9 22.9 %copy-start.14 = (bf16[256,384]{1,0:T(8,128)(2,1)}, bf16[256,384]{1,0:T(8,128)(2,1)S(1)}, u32[]{:S(2)}) copy-start(bf16[256,384]{1,0:T(8,128)(2,1)S(1)} %add_convert_fusion.1) | copy-start | bytes 589828
  107.0 28.5 %copy-start.13 = (f32[3072]{0:T(1024)S(1)}, f32[3072]{0:T(1024)}, u32[]{:S(2)}) copy-start(f32[3072]{0:T(1024)} %param.21) | copy-start | bytes 36868
  129.8 5.8 %collective-permute-start.3 = (bf16[8,256,384]{2,1,0:T(8,128)(2,1)S(1)}, bf16[8,256,384]{2,1,0:T(8,128)(2,1)S(1)}, u32[]{:S(2)}, u32[]{:S(2)}) collective-permute-start(bf16[8,256,384]{2,1,0:T(8,128)(2,1)S(1)} %all_to_all.37.mine_ref), channel_id=1, source_target_pairs={{0,8},{8,0},{1,9},{9,1},{2,10},{10,2},{3,11},{11,3},{4,12},{12,4},... | collective-permute-start | bytes 4718600 | tf_op jit(solution)/shard_map/ppermute | solution.py:327
  135.6 2.0 copy-start.2
  137.6 2.0 copy-start.3
  139.6 33.9 %copy-start.21 = (f32[768]{0:T(1024)S(1)}, f32[768]{0:T(1024)}, u32[]{:S(2)}) copy-start(f32[768]{0:T(1024)} %param.26) | copy-start | bytes 9220
  152.6 0.9 copy-start.7
  153.5 0.7 copy-start.9
  154.3 0.7 copy-start.11
  169.5 12.9 %all-to-all-start.5 = ((bf16[16,32,128]{2,1,0:T(8,128)(2,1)}), bf16[16,32,128]{2,1,0:T(8,128)(2,1)S(1)}, u32[]{:S(2)}, u32[]{:S(2)}) async-start(bf16[16,32,128]{2,1,0:T(8,128)(2,1)} %scan.3), calls=%async_computation.5 | async-start | bytes 262144 | tf_op jit(solution)/shard_map/all_to_all | solution.py:277
  182.4 1.1 copy-start.8
  183.5 1.0 copy-start.10
  184.5 0.9 copy-start.12
  186.7 3.8 %collective-permute-start.6 = (bf16[256,384]{1,0:T(8,128)(2,1)S(1)}, bf16[256,384]{1,0:T(8,128)(2,1)S(1)}, u32[]{:S(2)}, u32[]{:S(2)}) collective-permute-start(bf16[256,384]{1,0:T(8,128)(2,1)S(1)} %get-tuple-element.28), channel_id=1, source_target_pairs={{0,8},{8,0},{1,9},{9,1},{2,10},{10,2},{3,11},{11,3},{4,12},{12,4},... | collective-permute-start | bytes 589832 | tf_op jit(solution)/shard_map/ppermute | solution.py:284
  190.5 2.3 %copy-start.1 = (bf16[768,3072]{1,0:T(8,128)(2,1)S(1)}, bf16[768,3072]{1,0:T(8,128)(2,1)}, u32[]{:S(2)}) copy-start(bf16[768,3072]{1,0:T(8,128)(2,1)} %w_ref.3) | copy-start | bytes 14155780
  220.0 0.9 copy-start.15
Sparse Core Ops, SparseCore 0:
  14.1 53.0 all-gather.2
  68.9 48.0 all-gather.4

commit v2 on v0

v2 whole, which is shorter than its diff:
```python
import jax
import jax.numpy as jnp
from jax import lax
from jax.experimental import pallas as pl
from jax.experimental.pallas import tpu as pltpu
from jax.sharding import Mesh
from jax.sharding import PartitionSpec as P

DH = 128
BLK = 256
TOK = 512
HC = 3
HW = HC * DH
NCHIP = 16
SUB = DH // NCHIP
PIECE = 32
WIDTH = 384
NHEAD = 8
STEPS = 4
KSTEP = 2 * WIDTH
SWAP = [(0, 1), (1, 0)]
VMEM = 16 * 1024 * 1024
F32 = jnp.float32
BF16 = jnp.bfloat16


def silu(u):
    return u / (1.0 + jnp.exp(-u))


def whole(shape):
    return pl.BlockSpec(shape, lambda *_: (0,) * len(shape))


def span(index, size):
    return pl.ds(pl.multiple_of(index * size, DH), size)


def call(kernel, name, place, args, outs, grid=(1,), in_specs=None, out_specs=None, scratch=(), flops=0):
    return pl.pallas_call(
        kernel,
        out_shape=outs,
        grid_spec=pltpu.PrefetchScalarGridSpec(
            num_scalar_prefetch=1,
            grid=grid,
            in_specs=in_specs or [whole(a.shape) for a in args],
            out_specs=out_specs or [whole(o.shape) for o in outs],
            scratch_shapes=scratch,
        ),
        compiler_params=pltpu.CompilerParams(vmem_limit_bytes=VMEM),
        cost_estimate=pl.CostEstimate(flops=flops, bytes_accessed=0, transcendentals=0),
        name=name,
    )(place, *args)


def struct(shape, dtype):
    return jax.ShapeDtypeStruct(shape, dtype)


def in_hbm(a):
    return pltpu.with_memory_space_constraint(a, pltpu.HBM)


def sum_decays(core, mine_ref, yours_ref, cum_ref, across_ref, rows):
    rows[...] = jnp.zeros_like(rows)
    rows[: 4 * HC, span(core, BLK)] = mine_ref[...]
    rows[: 4 * HC, span(1 - core, BLK)] = yours_ref[...]
    before = lax.broadcasted_iota(jnp.int32, (TOK, TOK), 0)
    after = lax.broadcasted_iota(jnp.int32, (TOK, TOK), 1)
    upper = (before <= after).astype(F32)
    sums = jnp.dot(rows[...], upper, preferred_element_type=F32, precision=lax.Precision.HIGHEST)
    first = jnp.where(core == 0, sums[0:HC], sums[HC : 2 * HC])
    second = jnp.where(core == 0, sums[2 * HC : 3 * HC], sums[3 * HC : 4 * HC])
    across = jnp.concatenate([first, second, jnp.zeros((2, TOK), F32)], axis=0)
    across_ref[...] = across
    cum_ref[...] = jnp.concatenate([across, jnp.zeros((DH - 8, TOK), F32)], axis=0).T


def make_pieces(ks, vs, cum_ref, layer, pieces_ref):
    states = []
    decays = jnp.zeros((SUB, DH), F32)
    slot = lax.broadcasted_iota(jnp.int32, (SUB, DH), 0)
    for h in range(HC):
        cols = slice(h * DH, (h + 1) * DH)
        lane = layer * HC + h
        ch = cum_ref[:, lane : lane + 1]
        last = ch[TOK - 1 : TOK]
        kt = (ks[:, cols].astype(F32) * jnp.exp(last - ch)).astype(BF16)
        state = lax.dot_general(kt, vs[:, cols], (((0,), (0,)), ((), ())), preferred_element_type=F32)
        states.append(state.reshape(NCHIP, SUB, DH))
        total = jnp.exp(last)
        high = total.astype(BF16).astype(F32)
        decays = jnp.where(slot == h, high, decays)
        decays = jnp.where(slot == HC + h, total - high, decays)
    states.append(jnp.broadcast_to(decays[None], (NCHIP, SUB, DH)))
    pieces_ref[...] = jnp.concatenate(states, axis=1).astype(BF16)


def make_intra(qs, ks, vs, cum_ref, across_ref, layer, intra_ref):
    lower = lax.broadcasted_iota(jnp.int32, (BLK, BLK), 0) >= lax.broadcasted_iota(
        jnp.int32, (BLK, BLK), 1
    )
    for h in range(HC):
        cols = slice(h * DH, (h + 1) * DH)
        lane = layer * HC + h
        for i in range(2):
            rows = slice(i * BLK, (i + 1) * BLK)
            total = None
            for j in range(i + 1):
                keys = slice(j * BLK, (j + 1) * BLK)
                scores = lax.dot_general(
                    qs[rows, cols], ks[keys, cols], (((1,), (1,)), ((), ())),
                    preferred_element_type=F32,
                )
                spread = cum_ref[rows, lane : lane + 1] - across_ref[lane : lane + 1, keys]
                if i == j:
                    factor = jnp.where(lower, jnp.exp(jnp.where(lower, spread, 0.0)), 0.0)
                else:
                    factor = jnp.exp(spread)
                weights = (scores * factor).astype(BF16)
                part = jnp.dot(weights, vs[keys, cols], preferred_element_type=F32)
                total = part if total is None else total + part
            intra_ref[rows, cols] = total


def both_cores(core, mine_ref, yours_ref, out):
    out[span(core, BLK), :] = silu(mine_ref[:, span(core, HW)].astype(F32)).astype(BF16)
    out[span(1 - core, BLK), :] = silu(yours_ref[:, span(core, HW)].astype(F32)).astype(BF16)


def first_state_kernel(
    place, k_ref, other_k_ref, v_ref, other_v_ref, decay_ref, other_decay_ref,
    pieces_ref, ks, vs, cum_ref, across_ref, rows,
):
    core = place[0]
    both_cores(core, k_ref, other_k_ref, ks)
    both_cores(core, v_ref, other_v_ref, vs)
    sum_decays(core, decay_ref, other_decay_ref, cum_ref, across_ref, rows)
    make_pieces(ks, vs, cum_ref, 0, pieces_ref)


HEADS_OUT = pltpu.HBM((TOK, HW), BF16)
INTRA_OUT = pltpu.HBM((TOK, HW), F32)
PIECES_OUT = struct((NCHIP, PIECE, DH), BF16)


def first_state(place, *args):
    outs = (PIECES_OUT, HEADS_OUT, HEADS_OUT, struct((TOK, DH), F32), struct((8, TOK), F32))
    scratch = (pltpu.VMEM((16, TOK), F32),)
    return call(first_state_kernel, "first_state", place, args, outs, scratch=scratch)


def first_intra_kernel(
    place, q_ref, other_ref, ks, vs, cum_ref, across_ref, intra_ref, qs
):
    core = place[0]
    both_cores(core, q_ref, other_ref, qs)
    make_intra(qs, ks, vs, cum_ref, across_ref, 0, intra_ref)


def first_intra(place, q, other, ks, vs, cum, across):
    args = (q, other, in_hbm(ks), in_hbm(vs), cum, across)
    return call(first_intra_kernel, "first_intra", place, args, (INTRA_OUT, HEADS_OUT))


def project_step(h_ref, w_ref, gain_ref, acc, square, rows):
    step = pl.program_id(0)
    parts = []
    total = None
    for i in range(2):
        wide = h_ref[i].astype(F32)
        parts.append((wide * gain_ref[i]).astype(BF16))
        for n in range(WIDTH // DH):
            tile = wide[:, n * DH : (n + 1) * DH]
            total = tile * tile if total is None else total + tile * tile
    part = jnp.concatenate(parts, axis=1)

    term = jnp.dot(part, w_ref[0], preferred_element_type=F32)

    @pl.when(step == 0)
    def _():
        square[rows, :] = total
        acc[rows, :] = term

    @pl.when(step > 0)
    def _():
        square[rows, :] += total
        acc[rows, :] += term


def row_scale(square):
    mean = jnp.sum(square, axis=-1, keepdims=True) / (NHEAD * WIDTH)
    return lax.rsqrt(mean + 1e-06)


def chunk_at(i, place):
    half = STEPS // 2
    return jnp.where(i < half, place[1] * half + i, (1 - place[1]) * half + i - half), 0, 0


def projection_specs(width):
    half = STEPS // 2
    return (
        pl.BlockSpec((2, BLK, WIDTH), chunk_at),
        pl.BlockSpec((1, KSTEP, width), lambda i, _: (i // half, i % half, 0)),
        pl.BlockSpec((2, 1, WIDTH), chunk_at),
    )


def own_kv_kernel(place, h_ref, w_ref, gain_ref, out_ref, acc, square):
    project_step(h_ref, w_ref, gain_ref, acc, square, slice(0, BLK))

    @pl.when(pl.program_id(0) == STEPS - 1)
    def _():
        out_ref[...] = silu(acc[...] * row_scale(square[...])).astype(BF16)


def own_kv(place, h, w, gain):
    hs, ws, gs = projection_specs(2 * HW)
    return call(
        own_kv_kernel, "own_kv", place, (h, in_hbm(w), gain),
        (struct((BLK, 2 * HW), BF16),),
        grid=(STEPS,), in_specs=[hs, ws, gs],
        scratch=(pltpu.VMEM((BLK, 2 * HW), F32), pltpu.VMEM((BLK, DH), F32)),
        flops=2 * BLK * 2 * HW * NHEAD * WIDTH,
    )[0]


def second_state_kernel(
    place, h_ref, w_ref, gain_ref, own_ref, cum_ref, pieces_ref, ks, vs, acc, square
):
    core = place[0]
    project_step(h_ref, w_ref, gain_ref, acc, square, slice(0, BLK))

    @pl.when(pl.program_id(0) == STEPS - 1)
    def _():
        scale = row_scale(square[...])
        for n, dst in enumerate((ks, vs)):
            cols = slice(n * HW, (n + 1) * HW)
            dst[span(core, BLK), :] = own_ref[:, cols]
            dst[span(1 - core, BLK), :] = silu(acc[:, cols] * scale).astype(BF16)
        make_pieces(ks, vs, cum_ref, 1, pieces_ref)


def second_state(place, h, w, gain, own, cum):
    hs, ws, gs = projection_specs(2 * HW)
    return call(
        second_state_kernel, "second_state", place,
        (h, in_hbm(w), gain, own, cum),
        (PIECES_OUT, HEADS_OUT, HEADS_OUT),
        grid=(STEPS,), in_specs=[hs, ws, gs, whole(own.shape), whole(cum.shape)],
        scratch=(pltpu.VMEM((BLK, 2 * HW), F32), pltpu.VMEM((BLK, DH), F32)),
        flops=2 * BLK * 2 * HW * NHEAD * WIDTH,
    )


def second_intra_kernel(
    place, mine_ref, yours_ref, w_ref, gain_ref, ks, vs, cum_ref, across_ref,
    intra_ref, qs, acc, square,
):
    core = place[0]
    for n, src in enumerate((mine_ref, yours_ref)):
        rows = slice(n * BLK, (n + 1) * BLK)
        project_step(src, w_ref, gain_ref, acc, square, rows)

    @pl.when(pl.program_id(0) == STEPS - 1)
    def _():
        act = silu(acc[...] * row_scale(square[...])).astype(BF16)
        qs[span(core, BLK), :] = act[:BLK]
        qs[span(1 - core, BLK), :] = act[BLK:]
        make_intra(qs, ks, vs, cum_ref, across_ref, 1, intra_ref)


def second_intra(place, mine, yours, w, gain, ks, vs, cum, across):
    hs, ws, gs = projection_specs(HW)
    return call(
        second_intra_kernel, "second_intra", place,
        (mine, yours, in_hbm(w), gain, in_hbm(ks), in_hbm(vs), cum, across),
        (INTRA_OUT, HEADS_OUT),
        grid=(STEPS,),
        in_specs=[hs, hs, ws, gs] + [whole(a.shape) for a in (ks, vs, cum, across)],
        scratch=(pltpu.VMEM((TOK, HW), F32), pltpu.VMEM((TOK, DH), F32)),
    )


def scan_kernel(place, in_ref, out_ref):
    states = [jnp.zeros((SUB, DH), F32) for _ in range(HC)]
    empty = jnp.zeros((PIECE - HC * SUB, DH), F32)
    for p in range(NCHIP):
        piece = in_ref[p].astype(F32)
        out_ref[p] = jnp.concatenate(states + [empty], axis=0).astype(BF16)
        decays = piece[HC * SUB :]
        for h in range(HC):
            decay = decays[h : h + 1] + decays[HC + h : HC + h + 1]
            states[h] = states[h] * decay + piece[h * SUB : (h + 1) * SUB]


def scan(place, pieces):
    return call(scan_kernel, "scan", place, (pieces,), (PIECES_OUT,))[0]


def finish_kernel(
    layer, place, pieces_ref, intra_ref, cum_ref, qs_ref, gain_ref, mine_ref, yours_ref, out
):
    core = place[0]
    pieces = pieces_ref[...].astype(F32)
    for h in range(HC):
        cols = slice(h * DH, (h + 1) * DH)
        lane = layer * HC + h
        state = pieces[:, h * SUB : (h + 1) * SUB].reshape(DH, DH).astype(BF16)
        carried = jnp.dot(qs_ref[:, cols], state, preferred_element_type=F32)
        att = intra_ref[:, cols] + carried * jnp.exp(cum_ref[:, lane : lane + 1])
        square = jnp.mean(att * att, axis=-1, keepdims=True)
        gain = gain_ref[pl.ds(core * HC + h, 1), :]
        out[:, cols] = (att * lax.rsqrt(square + 1e-06) * gain).astype(BF16)
    mine_ref[...] = out[span(core, BLK), :]
    yours_ref[...] = out[span(1 - core, BLK), :]


def finish(place, layer, pieces, intra, cum, qs, gain):
    return call(
        lambda *refs: finish_kernel(layer, *refs), "finish", place,
        (pieces, in_hbm(intra), cum, in_hbm(qs), gain),
        (struct((BLK, HW), BF16),) * 2, scratch=(pltpu.VMEM((TOK, HW), BF16),), flops=0,
    )


def project_kernel(place, mine_ref, yours_ref, w_ref, out_ref, rows):
    core = place[0]

    @pl.when(pl.program_id(0) == 0)
    def _():
        rows[:, span(core, HW)] = mine_ref[...]
        rows[:, span(1 - core, HW)] = yours_ref[...]

    term = jnp.dot(rows[...], w_ref[...], preferred_element_type=F32).astype(BF16)
    out_ref[0] = term[:, :WIDTH]
    out_ref[1] = term[:, WIDTH:]


def project(place, mine, yours, w):
    return call(
        project_kernel, "project", place, (mine, yours, in_hbm(w)),
        (struct((NHEAD, BLK, WIDTH), BF16),),
        grid=(STEPS,),
        in_specs=[
            whole(mine.shape), whole(yours.shape),
            pl.BlockSpec((2 * HW, KSTEP), lambda i, _: (0, i)),
        ],
        out_specs=[pl.BlockSpec((2, BLK, WIDTH), lambda i, _: (i, 0, 0))],
        scratch=(pltpu.VMEM((BLK, 2 * HW), BF16),),
        flops=2 * BLK * 2 * HW * NHEAD * WIDTH,
    )[0]


def exchange(parts, axes):
    return lax.all_to_all(parts, axes, 0, 0)


def after(value, *others):
    return lax.optimization_barrier((value, *others))[0]


def rest(place, layer, before, intra, cum, qs, gain, w):
    mine, yours = finish(place, layer, before, intra, cum, qs, gain.reshape(2 * HC, DH))
    yours = lax.ppermute(yours, "c", SWAP)
    terms = exchange(project(place, mine, yours, w), ("x", "yl"))
    return jnp.sum(terms.astype(F32), axis=0)


def local(
    q1, k1, v1, decay1, gain_out1, wo1, stream_in, gain_in2, wq2, wk2, wv2, decay2, gain_out2, wo2
):
    core = lax.axis_index("c")
    place = jnp.stack([core, lax.axis_index("yh")]).astype(jnp.int32)

    def swapped(*arrays):
        return [lax.ppermute(a, "c", SWAP) for a in arrays]

    decays = jnp.concatenate([decay1.T, decay2.T], axis=0)
    other_k, other_v, other_decays = swapped(k1, v1, decays)
    pieces, ks, vs, cum, across = first_state(
        place, in_hbm(k1), other_k, in_hbm(v1), other_v, decays, other_decays
    )

    *weights, q1, _ = lax.optimization_barrier((wk2, wv2, wq2, q1, pieces))
    other_q, = swapped(q1)
    own_w = jnp.concatenate([lax.dynamic_slice_in_dim(w, core * HW, HW, axis=1) for w in weights], axis=1)
    send_w = [lax.dynamic_slice_in_dim(w, (1 - core) * HW, HW, axis=1) for w in weights]
    other_w, = swapped(jnp.concatenate(send_w, axis=1))
    first = jnp.where(core == 0, own_w, other_w)
    second = jnp.where(core == 0, other_w, own_w)
    near = jnp.concatenate([first, second], axis=0)
    far = lax.ppermute(near, "yh", SWAP)

    sums = after(exchange(pieces, ("yh", "z")), near, other_q)
    far_late = after(far, sums)
    before = exchange(scan(place, sums), ("yh", "z"))

    def gather(cols):
        both = jnp.concatenate([near[None, :, cols], far_late[None, :, cols]], axis=0)
        return both, lambda rows: lax.all_gather(rows, "z", axis=1, tiled=True)

    rows_kv, gather_kv = gather(slice(0, 2 * HW))
    rows_q, gather_q = gather(slice(2 * HW, 3 * HW))
    ks, rows_kv, rows_q = lax.optimization_barrier((ks, rows_kv, rows_q))
    wkv = gather_kv(rows_kv)
    intra, qs = first_intra(place, q1, other_q, ks, vs, cum, across)
    first_share = rest(place, 0, before, intra, cum, qs, gain_out1, wo1)
    stream = (stream_in.astype(F32) + first_share).astype(BF16)
    wq = gather_q(after(rows_q, stream))

    mine = exchange(jnp.broadcast_to(stream[None], (NHEAD, BLK, WIDTH)), ("x", "yl"))
    yours = lax.ppermute(mine, "c", SWAP)
    gain = gain_in2.reshape(NHEAD, 1, WIDTH)
    own = own_kv(place, mine, wkv, gain)
    pieces, ks, vs = second_state(place, yours, wkv, gain, own, cum)
    sums = exchange(pieces, ("yh", "z"))
    before = exchange(scan(place, sums), ("yh", "z"))
    intra, qs = second_intra(place, mine, yours, wq, gain, ks, vs, cum, across)
    second_share = rest(place, 1, before, intra, cum, qs, gain_out2, wo2)
    return (stream.astype(F32) + second_share).astype(BF16)


def solution(mesh):
    fine = Mesh(mesh.devices.reshape(2, 8, 2, 4, 2), ("yh", "z", "c", "x", "yl"))
    seq, head = ("yh", "z", "c"), ("x", "yl")
    both = P(seq, head)
    placed = (
        both, both, both, both, P(head), P(head, None), both, P(),
        both, both, both, both, P(head), P(head, None),
    )
    return jax.shard_map(local, mesh=fine, in_specs=placed, out_specs=both, check_vma=False)
```

time: 1240 us -> 200 us (0.16)
  waiting for transfers between devices: 880 us -> 17.9 us
  starting transfers between devices: 291 us -> 31.8 us
  blocking collectives: 0 us -> 83.3 us
  Pallas kernels: 0 us -> 44.4 us
  matrix products: 23.4 us -> 0 us
  other arithmetic: 16.9 us -> 3.8 us
    all_gather x4 -> x2, waiting for transfers between devices: 302 us -> 0.02 us  [gather(): return (both, lambda rows: lax.all_gather(rows, 'z', axis=1, tiled=True))]
    ppermute x62 -> x9, waiting for transfers between devices: 291 us -> 4.08 us  [the longest x2 2.14 us: rest(): yours = lax.ppermute(yours, 'c', SWAP)]
    unnamed x8 -> x2, waiting for transfers between devices: 286 us -> 0.03 us
    ppermute x62 -> x9, starting transfers between devices: 291 us -> 13.9 us  [the longest x2 5.03 us: rest(): yours = lax.ppermute(yours, 'c', SWAP)]
    all_to_all x0 -> x4, blocking collectives: none -> 83.3 us  [exchange(): return lax.all_to_all(parts, axes, 0, 0)]
    pallas_call x0 -> x11, Pallas kernels: none -> 44.4 us  [call(): pl.pallas_call(kernel, out_shape=outs, grid_spec=pltpu.PrefetchScalarGrid...]
    dot_general x11 -> x0, matrix products: 23.4 us -> none  [the longest x3 12 us: local(): jnp.dot(normed_in, piece_now, preferred_element_type=jnp.float32)]
    all_to_all x0 -> x3, starting transfers between devices: none -> 17.8 us  [exchange(): return lax.all_to_all(parts, axes, 0, 0)]
  transfers between devices with their start and end apart: 68 -> 14, of which waited for: 68 -> 6; matrix products, arithmetic and copies ran while one was open for 1% -> 1% of each run, Pallas kernels for 0% -> 17%
where the time goes in v2:
time: 200 us; the launch traced here: 199 us
  blocking collectives  83.3 us (42%)
  Pallas kernels  44.4 us (22%)
  starting transfers between devices  31.8 us (16%)
  waiting for transfers between devices  17.9 us (9%)
  between operations  13.7 us (7%)
  local copies, waits for them, and re-layouts  4.39 us (2%)
  other arithmetic  3.8 us (2%)
    all_to_all x4, blocking collectives, exchange(): return lax.all_to_all(parts, axes, 0, 0)  83.3 us
    pallas_call x11, Pallas kernels, call(): pl.pallas_call(kernel, out_shape=outs, grid_spec=pltpu.PrefetchScalarGrid...  44.4 us
    all_to_all x3, starting transfers between devices, exchange(): return lax.all_to_all(parts, axes, 0, 0)  17.8 us
    all_to_all x3, waiting for transfers between devices, exchange(): return lax.all_to_all(parts, axes, 0, 0)  13.7 us
    ppermute x2, starting transfers between devices, rest(): yours = lax.ppermute(yours, 'c', SWAP)  5.03 us
    ppermute x5, starting transfers between devices, swapped(): return [lax.ppermute(a, 'c', SWAP) for a in arrays]  4.84 us
    unnamed x26, local copies, waits for them, and re-layouts  4.14 us
  transfers between devices with their start and end apart: 14, of which 6 were waited for; matrix products, arithmetic and copies ran while one was open for 1% of the time, Pallas kernels for 17%

profile of v2, /device:TPU:1, one launch (start us, length us, event | category | flops | bytes accessed | tf_op | source)
XLA Modules:
  0.0 199.2 jit_solution(9028188351487675113)
XLA Ops:
  6.5 3.2 %collective-permute-start = (bf16[256,768]{1,0:T(8,128)(2,1)}, bf16[256,768]{1,0:T(8,128)(2,1)S(1)}, u32[]{:S(2)}, u32[]{:S(2)}) collective-permute-start(bf16[256,768]{1,0:T(8,128)(2,1)} %k_ref.1), channel_id=1, source_target_pairs={{0,8},{8,0},{1,9},{9,1},{2,10},{10,2},{3,11},{11,3},{4,12},{12,4},... | collective-permute-start | bytes 1179656 | tf_op jit(solution)/shard_map/ppermute | solution.py:378
  9.8 0.1 collective-permute-start.1
  9.9 0.7 pad_maximum_fusion.5.decay_ref
  10.6 0.4 collective-permute-start.2
  11.0 0.1 pad_add_fusion.place.refs_0_
  11.1 0.8 collective-permute-done.2.other_decay_ref
  11.9 0.0 collective-permute-done.other_k_ref
  11.9 0.0 collective-permute-done.1.other_v_ref
  11.9 3.9 %first_state.1 = (bf16[16,32,128]{2,1,0:T(8,128)(2,1)}, bf16[512,384]{1,0:T(8,128)(2,1)}, bf16[512,384]{1,0:T(8,128)(2,1)}, f32[512,128]{1,0:T(8,128)S(1)}, f32[8,512]{1,0:T(8,128)S(1)}) custom-call(s32[2]{0:T(128)S(1)} %pad_add_fusion.place.refs_0_, bf16[256,768]{1,0:T(8,128)(2,1)} %k_ref.1, bf16[256,768]{1,0:T(8,128)(2,1)S(1)} %collective-permute-done.other_k_ref, ...), custom_call_target="tpu_custom_call" | custom-call | tf_op jit(solution)/shard_map/first_state/pallas_call | solution.py:40
  15.8 0.0 copy-done.10
  15.9 0.4 collective-permute-start.3
  16.4 1.1 collective-permute-done.3
  17.5 0.1 broadcast_select_fusion.1
  17.6 1.3 collective-permute-start.5
  18.9 0.0 copy-done.1
  18.9 0.6 collective-permute-start.4
  19.5 8.3 %all-to-all-start = ((bf16[16,32,128]{2,1,0:T(8,128)(2,1)}), bf16[16,32,128]{2,1,0:T(8,128)(2,1)S(1)}, u32[]{:S(2)}, u32[]{:S(2)}) async-start(bf16[16,32,128]{2,1,0:T(8,128)(2,1)} %get-tuple-element.31), calls=%async_computation | async-start | bytes 262144 | tf_op jit(solution)/shard_map/all_to_all | solution.py:357
  27.8 0.0 all-gather.3.cloned.1.call-start
  27.9 8.9 %all-to-all-done.in_ref = bf16[16,32,128]{2,1,0:T(8,128)(2,1)S(1)} async-done(((bf16[16,32,128]{2,1,0:T(8,128)(2,1)}), bf16[16,32,128]{2,1,0:T(8,128)(2,1)S(1)}, u32[]{:S(2)}, u32[]{:S(2)}) %all-to-all-start) | async-done | bytes 131104 | tf_op jit(solution)/shard_map/all_to_all | solution.py:357
  36.8 0.0 collective-permute-done.4.other_ref
  36.8 0.0 collective-permute-done.5
  36.9 0.9 pad_maximum_fusion
  37.8 0.8 pad_maximum_fusion.2
  38.5 0.0 all-gather.3.cloned.1.call-update
  38.6 1.2 scan.2
  39.8 4.3 %all-to-all-start.1 = ((bf16[16,32,128]{2,1,0:T(8,128)(2,1)}), bf16[16,32,128]{2,1,0:T(8,128)(2,1)S(1)}, u32[]{:S(2)}, u32[]{:S(2)}) async-start(bf16[16,32,128]{2,1,0:T(8,128)(2,1)} %scan.2), calls=%async_computation.1 | async-start | bytes 262144 | tf_op jit(solution)/shard_map/all_to_all | solution.py:357
  44.1 0.0 all-gather.5.cloned.1.call-start
  44.2 4.1 %first_intra.1 = (f32[512,384]{1,0:T(8,128)}, bf16[512,384]{1,0:T(8,128)(2,1)}) custom-call(s32[2]{0:T(128)S(1)} %pad_add_fusion.place.refs_0_, bf16[256,768]{1,0:T(8,128)(2,1)S(1)} %copy-done.1, bf16[256,768]{1,0:T(8,128)(2,1)S(1)} %collective-permute-done.4.other_ref, bf16[512,384]{1,0:T(8,128)(2,1)} %get-tuple-element.39.ks, ...), custom_call_target="tpu_custom_call" | custom-call | tf_op jit(solution)/shard_map/first_intra/pallas_call | solution.py:40
  48.3 4.8 %all-to-all-done.1.refs_1_ = bf16[16,32,128]{2,1,0:T(8,128)(2,1)S(1)} async-done(((bf16[16,32,128]{2,1,0:T(8,128)(2,1)}), bf16[16,32,128]{2,1,0:T(8,128)(2,1)S(1)}, u32[]{:S(2)}, u32[]{:S(2)}) %all-to-all-start.1) | async-done | bytes 131104 | tf_op jit(solution)/shard_map/all_to_all | solution.py:357
  53.1 2.5 %finish.2 = (bf16[256,384]{1,0:T(8,128)(2,1)S(1)}, bf16[256,384]{1,0:T(8,128)(2,1)S(1)}) custom-call(s32[2]{0:T(128)S(1)} %pad_add_fusion.place.refs_0_, bf16[16,32,128]{2,1,0:T(8,128)(2,1)S(1)} %all-to-all-done.1.refs_1_, f32[512,384]{1,0:T(8,128)} %get-tuple-element.43.refs_2_, f32[512,128]{1,0:T(8,128)S(1)} %get-tuple-element.41.cum_ref.refs_3_, ...), custom_call_target="tpu_custom_call" | custom-call | tf_op jit(solution)/shard_map/finish/pallas_call | solution.py:40
  55.6 2.8 %collective-permute-start.6 = (bf16[256,384]{1,0:T(8,128)(2,1)S(1)}, bf16[256,384]{1,0:T(8,128)(2,1)S(1)}, u32[]{:S(2)}, u32[]{:S(2)}) collective-permute-start(bf16[256,384]{1,0:T(8,128)(2,1)S(1)} %get-tuple-element.46), channel_id=1, source_target_pairs={{0,8},{8,0},{1,9},{9,1},{2,10},{10,2},{3,11},{11,3},{4,12},{12,4},... | collective-permute-start | bytes 589832 | tf_op jit(solution)/shard_map/ppermute | solution.py:366
  58.4 1.1 collective-permute-done.6.yours_ref
  59.5 4.7 %project.2 = bf16[8,256,384]{2,1,0:T(8,128)(2,1)S(1)} custom-call(s32[2]{0:T(128)S(1)} %pad_add_fusion.place.refs_0_, bf16[256,384]{1,0:T(8,128)(2,1)S(1)} %get-tuple-element.45.mine_ref, bf16[256,384]{1,0:T(8,128)(2,1)S(1)} %collective-permute-done.6.yours_ref, bf16[768,3072]{1,0:T(8,128)(2,1)} %w_ref.2), custom_call_target="tpu_custom_call" | custom-call | flops 1207959552 | tf_op jit(solution)/shard_map/project/pallas_call | solution.py:40
  64.2 24.2 %all_to_all.35 = bf16[8,256,384]{2,1,0:T(8,128)(2,1)S(1)} all-to-all(bf16[8,256,384]{2,1,0:T(8,128)(2,1)S(1)} %project.2), channel_id=1, replica_groups=mesh['yh'=2,'z'=8,'c'=2,'x'=4,'yl'=2] {'x','yl'}, dimensions={0} | all-to-all | bytes 3145728 | tf_op jit(solution)/shard_map/all_to_all | solution.py:357
  88.4 0.2 convert_reduce_fusion.1
  88.6 0.7 copy-done.9
  89.3 0.0 copy-start.7
  89.4 0.0 all-gather.5.cloned.1.call-update
  89.4 0.6 copy-done.7
  90.0 0.1 broadcast_in_dim.22
  90.2 0.0 copy-start.2
  90.2 22.7 %all_to_all.36.h_ref.mine_ref = bf16[8,256,384]{2,1,0:T(8,128)(2,1)S(1)} all-to-all(bf16[8,256,384]{2,1,0:T(8,128)(2,1)S(1)} %broadcast_in_dim.22), channel_id=1, replica_groups=mesh['yh'=2,'z'=8,'c'=2,'x'=4,'yl'=2] {'x','yl'}, dimensions={0} | all-to-all | bytes 3145728 | tf_op jit(solution)/shard_map/all_to_all | solution.py:357
  112.9 2.8 %collective-permute-start.7 = (bf16[8,256,384]{2,1,0:T(8,128)(2,1)S(1)}, bf16[8,256,384]{2,1,0:T(8,128)(2,1)S(1)}, u32[]{:S(2)}, u32[]{:S(2)}) collective-permute-start(bf16[8,256,384]{2,1,0:T(8,128)(2,1)S(1)} %all_to_all.36.h_ref.mine_ref), channel_id=1, source_target_pairs={{0,8},{8,0},{1,9},{9,1},{2,10},{10,2},{3,11},{11,3},{4,12},{12,4},... | collective-permute-start | bytes 4718600 | tf_op jit(solution)/shard_map/ppermute | solution.py:414
  115.7 0.0 copy-done.2
  115.7 5.3 %own_kv.1.own_ref = bf16[256,768]{1,0:T(8,128)(2,1)S(1)} custom-call(s32[2]{0:T(128)S(1)} %pad_add_fusion.place.refs_0_, bf16[8,256,384]{2,1,0:T(8,128)(2,1)S(1)} %all_to_all.36.h_ref.mine_ref, bf16[2,1536,768]{2,1,0:T(8,128)(2,1)} %all-gather.3.cloned.1.call-done.w_ref, f32[8,1,384]{2,1,0:T(1,128)S(1)} %bitcast.15), custom_call_target="tpu_custom_call" | custom-call | flops 1207959552 | tf_op jit(solution)/shard_map/own_kv/pallas_call | solution.py:40
  121.0 0.0 collective-permute-done.7.h_ref.yours_ref
  121.0 6.8 %second_state.1 = (bf16[16,32,128]{2,1,0:T(8,128)(2,1)S(1)}, bf16[512,384]{1,0:T(8,128)(2,1)}, bf16[512,384]{1,0:T(8,128)(2,1)}) custom-call(s32[2]{0:T(128)S(1)} %pad_add_fusion.place.refs_0_, bf16[8,256,384]{2,1,0:T(8,128)(2,1)S(1)} %collective-permute-done.7.h_ref.yours_ref, bf16[2,1536,768]{2,1,0:T(8,128)(2,1)} %all-gather.3.cloned.1.call-done.w_ref, ...), custom_call_target="tpu_custom_call" | custom-call | flops 1207959552 | tf_op jit(solution)/shard_map/second_state/pallas_call | solution.py:40
  127.8 13.4 %all_to_all.37.in_ref = bf16[16,32,128]{2,1,0:T(8,128)(2,1)S(1)} all-to-all(bf16[16,32,128]{2,1,0:T(8,128)(2,1)S(1)} %get-tuple-element.48), channel_id=1, replica_groups=mesh['yh'=2,'z'=8,'c'=2,'x'=4,'yl'=2] {'yh','z'}, dimensions={0} | all-to-all | bytes 262144 | tf_op jit(solution)/shard_map/all_to_all | solution.py:357
  141.2 0.6 scan.3
  141.8 0.6 copy-done
  142.4 5.2 %all-to-all-start.5 = ((bf16[16,32,128]{2,1,0:T(8,128)(2,1)}), bf16[16,32,128]{2,1,0:T(8,128)(2,1)S(1)}, u32[]{:S(2)}, u32[]{:S(2)}) async-start(bf16[16,32,128]{2,1,0:T(8,128)(2,1)} %copy-done), calls=%async_computation.5 | async-start | bytes 262144 | tf_op jit(solution)/shard_map/all_to_all | solution.py:357
  147.6 0.0 all-gather.5.cloned.1.call-done.w_ref
  147.6 0.7 copy-done.4
  148.3 8.2 %second_intra.1 = (f32[512,384]{1,0:T(8,128)}, bf16[512,384]{1,0:T(8,128)(2,1)}) custom-call(s32[2]{0:T(128)S(1)} %pad_add_fusion.place.refs_0_, bf16[8,256,384]{2,1,0:T(8,128)(2,1)S(1)} %all_to_all.36.h_ref.mine_ref, bf16[8,256,384]{2,1,0:T(8,128)(2,1)S(1)} %collective-permute-done.7.h_ref.yours_ref, ...), custom_call_target="tpu_custom_call" | custom-call | tf_op jit(solution)/shard_map/second_intra/pallas_call | solution.py:40
  156.5 0.0 all-to-all-done.5.refs_1_
  156.5 0.7 copy-done.6
  157.2 2.5 %finish.3 = (bf16[256,384]{1,0:T(8,128)(2,1)S(1)}, bf16[256,384]{1,0:T(8,128)(2,1)S(1)}) custom-call(s32[2]{0:T(128)S(1)} %pad_add_fusion.place.refs_0_, bf16[16,32,128]{2,1,0:T(8,128)(2,1)S(1)} %all-to-all-done.5.refs_1_, f32[512,384]{1,0:T(8,128)} %get-tuple-element.53.refs_2_, f32[512,128]{1,0:T(8,128)S(1)} %get-tuple-element.41.cum_ref.refs_3_, ...), custom_call_target="tpu_custom_call" | custom-call | tf_op jit(solution)/shard_map/finish/pallas_call | solution.py:40
  159.7 2.2 %collective-permute-start.8 = (bf16[256,384]{1,0:T(8,128)(2,1)S(1)}, bf16[256,384]{1,0:T(8,128)(2,1)S(1)}, u32[]{:S(2)}, u32[]{:S(2)}) collective-permute-start(bf16[256,384]{1,0:T(8,128)(2,1)S(1)} %get-tuple-element.56), channel_id=1, source_target_pairs={{0,8},{8,0},{1,9},{9,1},{2,10},{10,2},{3,11},{11,3},{4,12},{12,4},... | collective-permute-start | bytes 589832 | tf_op jit(solution)/shard_map/ppermute | solution.py:366
  161.9 1.1 collective-permute-done.8.yours_ref
  163.0 4.7 %project.3 = bf16[8,256,384]{2,1,0:T(8,128)(2,1)S(1)} custom-call(s32[2]{0:T(128)S(1)} %pad_add_fusion.place.refs_0_, bf16[256,384]{1,0:T(8,128)(2,1)S(1)} %get-tuple-element.55.mine_ref, bf16[256,384]{1,0:T(8,128)(2,1)S(1)} %collective-permute-done.8.yours_ref, bf16[768,3072]{1,0:T(8,128)(2,1)} %w_ref.3), custom_call_target="tpu_custom_call" | custom-call | flops 1207959552 | tf_op jit(solution)/shard_map/project/pallas_call | solution.py:40
  167.7 23.0 %all_to_all.38 = bf16[8,256,384]{2,1,0:T(8,128)(2,1)S(1)} all-to-all(bf16[8,256,384]{2,1,0:T(8,128)(2,1)S(1)} %project.3), channel_id=1, replica_groups=mesh['yh'=2,'z'=8,'c'=2,'x'=4,'yl'=2] {'x','yl'}, dimensions={0} | all-to-all | bytes 3145728 | tf_op jit(solution)/shard_map/all_to_all | solution.py:357
  190.7 0.2 convert_reduce_fusion
  190.9 0.7 copy-done.8
  191.6 0.7 add_convert_fusion
  (25 shorter events, 0.3 us)
Async XLA Ops:
  6.5 9.2 %copy-start.10 = (bf16[96,768]{1,0:T(8,128)(2,1)S(1)}, bf16[96,768]{1,0:T(8,128)(2,1)}, u32[]{:S(2)}) copy-start(bf16[96,768]{1,0:T(8,128)(2,1)} %param.23) | copy-start | bytes 442372
  6.5 9.3 %copy-start.12 = (bf16[96,768]{1,0:T(8,128)(2,1)S(1)}, bf16[96,768]{1,0:T(8,128)(2,1)}, u32[]{:S(2)}) copy-start(bf16[96,768]{1,0:T(8,128)(2,1)} %param.24) | copy-start | bytes 442372
  6.5 9.3 %copy-start.11 = (bf16[96,768]{1,0:T(8,128)(2,1)S(1)}, bf16[96,768]{1,0:T(8,128)(2,1)}, u32[]{:S(2)}) copy-start(bf16[96,768]{1,0:T(8,128)(2,1)} %param.22) | copy-start | bytes 442372
  6.5 5.3 %collective-permute-start = (bf16[256,768]{1,0:T(8,128)(2,1)}, bf16[256,768]{1,0:T(8,128)(2,1)S(1)}, u32[]{:S(2)}, u32[]{:S(2)}) collective-permute-start(bf16[256,768]{1,0:T(8,128)(2,1)} %k_ref.1), channel_id=1, source_target_pairs={{0,8},{8,0},{1,9},{9,1},{2,10},{10,2},{3,11},{11,3},{4,12},{12,4},... | collective-permute-start | bytes 1179656 | tf_op jit(solution)/shard_map/ppermute | solution.py:378
  9.8 2.1 %collective-permute-start.1 = (bf16[256,768]{1,0:T(8,128)(2,1)}, bf16[256,768]{1,0:T(8,128)(2,1)S(1)}, u32[]{:S(2)}, u32[]{:S(2)}) collective-permute-start(bf16[256,768]{1,0:T(8,128)(2,1)} %v_ref.1), channel_id=1, source_target_pairs={{0,8},{8,0},{1,9},{9,1},{2,10},{10,2},{3,11},{11,3},{4,12},{12,4},... | collective-permute-start | bytes 1179656 | tf_op jit(solution)/shard_map/ppermute | solution.py:378
  10.6 1.3 collective-permute-start.2
  15.8 28.4 %copy-start.3 = (f32[8,512]{1,0:T(8,128)}, f32[8,512]{1,0:T(8,128)S(1)}, u32[]{:S(2)}) copy-start(f32[8,512]{1,0:T(8,128)S(1)} %get-tuple-element.42.across_ref) | copy-start | bytes 49156
  15.8 3.1 %copy-start.1 = (bf16[256,768]{1,0:T(8,128)(2,1)S(1)}, bf16[256,768]{1,0:T(8,128)(2,1)}, u32[]{:S(2)}) copy-start(bf16[256,768]{1,0:T(8,128)(2,1)} %q_ref) | copy-start | bytes 1179652
  15.9 1.6 collective-permute-start.3
  17.6 19.2 %collective-permute-start.5 = (bf16[192,1152]{1,0:T(8,128)(2,1)S(1)}, bf16[192,1152]{1,0:T(8,128)(2,1)S(1)}, u32[]{:S(2)}, u32[]{:S(2)}) collective-permute-start(bf16[192,1152]{1,0:T(8,128)(2,1)S(1)} %pad_maximum_fusion.1), channel_id=1, source_target_pairs={{0,128},{128,0},{1,129},{129,1},{2,130},{130,2},{3,131},{131,3},{4... | collective-permute-start | bytes 1327112 | tf_op jit(solution)/shard_map/ppermute | solution.py:394
  18.9 18.0 %collective-permute-start.4 = (bf16[256,768]{1,0:T(8,128)(2,1)S(1)}, bf16[256,768]{1,0:T(8,128)(2,1)S(1)}, u32[]{:S(2)}, u32[]{:S(2)}) collective-permute-start(bf16[256,768]{1,0:T(8,128)(2,1)S(1)} %copy-done.1), channel_id=1, source_target_pairs={{0,8},{8,0},{1,9},{9,1},{2,10},{10,2},{3,11},{11,3},{4,12},{12,4},... | collective-permute-start | bytes 1179656 | tf_op jit(solution)/shard_map/ppermute | solution.py:378
  19.5 17.3 %all-to-all-start = ((bf16[16,32,128]{2,1,0:T(8,128)(2,1)}), bf16[16,32,128]{2,1,0:T(8,128)(2,1)S(1)}, u32[]{:S(2)}, u32[]{:S(2)}) async-start(bf16[16,32,128]{2,1,0:T(8,128)(2,1)} %get-tuple-element.31), calls=%async_computation | async-start | bytes 262144 | tf_op jit(solution)/shard_map/all_to_all | solution.py:357
  27.8 87.9 %all-gather.3.cloned.1.call-start = ((), (), s32[]{:S(2)}) async-start(), calls=%async_computation.7 | async-start | bytes 5308416 | tf_op jit(solution)/shard_map/all_gather | solution.py:402
  38.5 14.5 %copy-start.5 = (f32[768]{0:T(1024)S(1)}, f32[768]{0:T(1024)}, u32[]{:S(2)}) copy-start(f32[768]{0:T(1024)} %param.18) | copy-start | bytes 9220
  39.8 13.3 %all-to-all-start.1 = ((bf16[16,32,128]{2,1,0:T(8,128)(2,1)}), bf16[16,32,128]{2,1,0:T(8,128)(2,1)S(1)}, u32[]{:S(2)}, u32[]{:S(2)}) async-start(bf16[16,32,128]{2,1,0:T(8,128)(2,1)} %scan.2), calls=%async_computation.1 | async-start | bytes 262144 | tf_op jit(solution)/shard_map/all_to_all | solution.py:357
  44.1 103.5 %all-gather.5.cloned.1.call-start = ((), (), s32[]{:S(2)}) async-start(), calls=%async_computation.8 | async-start | bytes 2654208 | tf_op jit(solution)/shard_map/all_gather | solution.py:402
  55.6 3.9 %collective-permute-start.6 = (bf16[256,384]{1,0:T(8,128)(2,1)S(1)}, bf16[256,384]{1,0:T(8,128)(2,1)S(1)}, u32[]{:S(2)}, u32[]{:S(2)}) collective-permute-start(bf16[256,384]{1,0:T(8,128)(2,1)S(1)} %get-tuple-element.46), channel_id=1, source_target_pairs={{0,8},{8,0},{1,9},{9,1},{2,10},{10,2},{3,11},{11,3},{4,12},{12,4},... | collective-permute-start | bytes 589832 | tf_op jit(solution)/shard_map/ppermute | solution.py:366
  88.4 0.9 copy-start.9
  89.3 0.7 copy-start.7
  90.2 25.5 %copy-start.2 = (f32[3072]{0:T(1024)S(1)}, f32[3072]{0:T(1024)}, u32[]{:S(2)}) copy-start(f32[3072]{0:T(1024)} %param.21) | copy-start | bytes 36868
  112.9 8.1 %collective-permute-start.7 = (bf16[8,256,384]{2,1,0:T(8,128)(2,1)S(1)}, bf16[8,256,384]{2,1,0:T(8,128)(2,1)S(1)}, u32[]{:S(2)}, u32[]{:S(2)}) collective-permute-start(bf16[8,256,384]{2,1,0:T(8,128)(2,1)S(1)} %all_to_all.36.h_ref.mine_ref), channel_id=1, source_target_pairs={{0,8},{8,0},{1,9},{9,1},{2,10},{10,2},{3,11},{11,3},{4,12},{12,4},... | collective-permute-start | bytes 4718600 | tf_op jit(solution)/shard_map/ppermute | solution.py:414
  141.8 0.6 copy-start
  142.4 14.1 %all-to-all-start.5 = ((bf16[16,32,128]{2,1,0:T(8,128)(2,1)}), bf16[16,32,128]{2,1,0:T(8,128)(2,1)S(1)}, u32[]{:S(2)}, u32[]{:S(2)}) async-start(bf16[16,32,128]{2,1,0:T(8,128)(2,1)} %copy-done), calls=%async_computation.5 | async-start | bytes 262144 | tf_op jit(solution)/shard_map/all_to_all | solution.py:357
  147.6 0.7 copy-start.4
  156.5 0.7 copy-start.6
  159.7 3.3 %collective-permute-start.8 = (bf16[256,384]{1,0:T(8,128)(2,1)S(1)}, bf16[256,384]{1,0:T(8,128)(2,1)S(1)}, u32[]{:S(2)}, u32[]{:S(2)}) collective-permute-start(bf16[256,384]{1,0:T(8,128)(2,1)S(1)} %get-tuple-element.56), channel_id=1, source_target_pairs={{0,8},{8,0},{1,9},{9,1},{2,10},{10,2},{3,11},{11,3},{4,12},{12,4},... | collective-permute-start | bytes 589832 | tf_op jit(solution)/shard_map/ppermute | solution.py:366
  190.7 0.9 copy-start.8
Sparse Core Ops, SparseCore 0:
  38.7 58.0 all-gather.2
  98.6 36.8 all-gather.4

commit v3 on v2

--- a/solution.py
+++ b/solution.py
@@ -139,8 +139,13 @@
     make_pieces(ks, vs, cum_ref, 0, pieces_ref)
 
 
+IN_VMEM = pl.BlockSpec(memory_space=pltpu.VMEM)
+ANY = pl.BlockSpec(memory_space=pl.ANY)
 HEADS_OUT = pltpu.HBM((TOK, HW), BF16)
-INTRA_OUT = pltpu.HBM((TOK, HW), F32)
+QUERY_OUT = struct((TOK, HW), BF16)
+INTRA_OUT = struct((TOK, HW), F32)
+WO_OUT = pltpu.VMEM((2 * HW, NHEAD * WIDTH), BF16)
+WKV_OUT = pltpu.VMEM((2, NHEAD * WIDTH // 2, 2 * HW), BF16)
 PIECES_OUT = struct((NCHIP, PIECE, DH), BF16)
 
 
@@ -160,10 +165,10 @@
 
 def first_intra(place, q, other, ks, vs, cum, across):
     args = (q, other, in_hbm(ks), in_hbm(vs), cum, across)
-    return call(first_intra_kernel, "first_intra", place, args, (INTRA_OUT, HEADS_OUT))
-
-
-def project_step(h_ref, w_ref, gain_ref, acc, square, rows):
+    return call(first_intra_kernel, "first_intra", place, args, (INTRA_OUT, QUERY_OUT))
+
+
+def project_step(h_ref, w, gain_ref, acc, square, rows):
     step = pl.program_id(0)
     parts = []
     total = None
@@ -175,7 +180,7 @@
             total = tile * tile if total is None else total + tile * tile
     part = jnp.concatenate(parts, axis=1)
 
-    term = jnp.dot(part, w_ref[0], preferred_element_type=F32)
+    term = jnp.dot(part, w, preferred_element_type=F32)
 
     @pl.when(step == 0)
     def _():
@@ -207,30 +212,58 @@
     )
 
 
-def own_kv_kernel(place, h_ref, w_ref, gain_ref, out_ref, acc, square):
-    project_step(h_ref, w_ref, gain_ref, acc, square, slice(0, BLK))
-
-    @pl.when(pl.program_id(0) == STEPS - 1)
+def weight_rows(w_ref):
+    half = STEPS // 2
+    step = pl.program_id(0)
+    return w_ref.at[step // half, pl.ds(pl.multiple_of(step % half * KSTEP, KSTEP), KSTEP), :]
+
+
+def own_kv_kernel(place, h_ref, w_ref, gain_ref, out_ref, held, acc, square, sems):
+    step = pl.program_id(0)
+    half = STEPS // 2
+
+    def fetch(n):
+        rows = pl.ds(n % half * KSTEP, KSTEP)
+        return pltpu.make_async_copy(
+            w_ref.at[n // half, rows, :], held.at[n // half, rows, :], sems.at[n]
+        )
+
+    @pl.when(step == 0)
+    def _():
+        for n in range(STEPS):
+            fetch(n).start()
+
+    for n in range(STEPS):
+
+        @pl.when(step == n)
+        def _(n=n):
+            fetch(n).wait()
+
+    project_step(h_ref, weight_rows(held)[...], gain_ref, acc, square, slice(0, BLK))
+
+    @pl.when(step == STEPS - 1)
     def _():
         out_ref[...] = silu(acc[...] * row_scale(square[...])).astype(BF16)
 
 
 def own_kv(place, h, w, gain):
-    hs, ws, gs = projection_specs(2 * HW)
+    hs, _, gs = projection_specs(2 * HW)
     return call(
         own_kv_kernel, "own_kv", place, (h, in_hbm(w), gain),
-        (struct((BLK, 2 * HW), BF16),),
-        grid=(STEPS,), in_specs=[hs, ws, gs],
-        scratch=(pltpu.VMEM((BLK, 2 * HW), F32), pltpu.VMEM((BLK, DH), F32)),
-        flops=2 * BLK * 2 * HW * NHEAD * WIDTH,
-    )[0]
+        (struct((BLK, 2 * HW), BF16), WKV_OUT),
+        grid=(STEPS,), in_specs=[hs, ANY, gs], out_specs=[whole((BLK, 2 * HW)), IN_VMEM],
+        scratch=(
+            pltpu.VMEM((BLK, 2 * HW), F32), pltpu.VMEM((BLK, DH), F32),
+            pltpu.SemaphoreType.DMA((STEPS,)),
+        ),
+    )
 
 
 def second_state_kernel(
     place, h_ref, w_ref, gain_ref, own_ref, cum_ref, pieces_ref, ks, vs, acc, square
 ):
     core = place[0]
-    project_step(h_ref, w_ref, gain_ref, acc, square, slice(0, BLK))
+    project_step(h_ref, weight_rows(w_ref)[...], gain_ref, acc, square, slice(0, BLK))
 
     @pl.when(pl.program_id(0) == STEPS - 1)
     def _():
@@ -243,14 +276,12 @@
 
 
 def second_state(place, h, w, gain, own, cum):
-    hs, ws, gs = projection_specs(2 * HW)
+    hs, _, gs = projection_specs(2 * HW)
     return call(
-        second_state_kernel, "second_state", place,
-        (h, in_hbm(w), gain, own, cum),
+        second_state_kernel, "second_state", place, (h, w, gain, own, cum),
         (PIECES_OUT, HEADS_OUT, HEADS_OUT),
-        grid=(STEPS,), in_specs=[hs, ws, gs, whole(own.shape), whole(cum.shape)],
+        grid=(STEPS,), in_specs=[hs, IN_VMEM, gs, whole(own.shape), whole(cum.shape)],
         scratch=(pltpu.VMEM((BLK, 2 * HW), F32), pltpu.VMEM((BLK, DH), F32)),
-        flops=2 * BLK * 2 * HW * NHEAD * WIDTH,
     )
 
 
@@ -261,7 +292,7 @@
     core = place[0]
     for n, src in enumerate((mine_ref, yours_ref)):
         rows = slice(n * BLK, (n + 1) * BLK)
-        project_step(src, w_ref, gain_ref, acc, square, rows)
+        project_step(src, w_ref[0], gain_ref, acc, square, rows)
 
     @pl.when(pl.program_id(0) == STEPS - 1)
     def _():
@@ -276,11 +307,28 @@
     return call(
         second_intra_kernel, "second_intra", place,
         (mine, yours, in_hbm(w), gain, in_hbm(ks), in_hbm(vs), cum, across),
-        (INTRA_OUT, HEADS_OUT),
+        (pltpu.HBM((TOK, HW), F32), HEADS_OUT),
         grid=(STEPS,),
         in_specs=[hs, hs, ws, gs] + [whole(a.shape) for a in (ks, vs, cum, across)],
         scratch=(pltpu.VMEM((TOK, HW), F32), pltpu.VMEM((TOK, DH), F32)),
     )
+
+
+def pack_kernel(place, own_ref, other_ref, far_ref, far_other_ref, kv_ref, q_ref):
+    core = place[0]
+    rows = own_ref.shape[0]
+    for n, pair in enumerate(((own_ref, other_ref), (far_ref, far_other_ref))):
+        for src, owner in zip(pair, (core, 1 - core)):
+            at = pl.ds(pl.multiple_of(owner * rows, rows), rows)
+            for i in range(2):
+                kv_ref[n, at, i * HW : (i + 1) * HW] = src[:, span(2 * i + core, HW)]
+            q_ref[n, at, :] = src[:, span(4 + core, HW)]
+
+
+def pack(place, *args):
+    rows = 2 * args[0].shape[0]
+    outs = (struct((2, rows, 2 * HW), BF16), struct((2, rows, HW), BF16))
+    return call(pack_kernel, "pack", place, args, outs)
 
 
 def scan_kernel(place, in_ref, out_ref):
@@ -300,9 +348,12 @@
 
 
 def finish_kernel(
-    layer, place, pieces_ref, intra_ref, cum_ref, qs_ref, gain_ref, mine_ref, yours_ref, out
-):
-    core = place[0]
+    layer, place, pieces_ref, intra_ref, cum_ref, qs_ref, gain_ref, wo_ref,
+    mine_ref, yours_ref, held, out, sem,
+):
+    core = place[0]
+    fetch = pltpu.make_async_copy(wo_ref, held, sem)
+    fetch.start()
     pieces = pieces_ref[...].astype(F32)
     for h in range(HC):
         cols = slice(h * DH, (h + 1) * DH)
@@ -315,13 +366,19 @@
         out[:, cols] = (att * lax.rsqrt(square + 1e-06) * gain).astype(BF16)
     mine_ref[...] = out[span(core, BLK), :]
     yours_ref[...] = out[span(1 - core, BLK), :]
-
-
-def finish(place, layer, pieces, intra, cum, qs, gain):
+    fetch.wait()
+
+
+def finish(place, layer, pieces, intra, cum, qs, gain, wo):
+    if layer:
+        intra, qs = in_hbm(intra), in_hbm(qs)
+    args = (pieces, intra, cum, qs, gain)
     return call(
-        lambda *refs: finish_kernel(layer, *refs), "finish", place,
-        (pieces, in_hbm(intra), cum, in_hbm(qs), gain),
-        (struct((BLK, HW), BF16),) * 2, scratch=(pltpu.VMEM((TOK, HW), BF16),), flops=0,
+        lambda *refs: finish_kernel(layer, *refs), "finish", place, (*args, in_hbm(wo)),
+        (struct((BLK, HW), BF16), struct((BLK, HW), BF16), WO_OUT),
+        in_specs=[whole(a.shape) for a in args] + [ANY],
+        out_specs=[whole((BLK, HW)), whole((BLK, HW)), IN_VMEM],
+        scratch=(pltpu.VMEM((TOK, HW), BF16), pltpu.SemaphoreType.DMA),
     )
 
 
@@ -333,19 +390,20 @@
         rows[:, span(core, HW)] = mine_ref[...]
         rows[:, span(1 - core, HW)] = yours_ref[...]
 
-    term = jnp.dot(rows[...], w_ref[...], preferred_element_type=F32).astype(BF16)
+    cols = span(pl.program_id(0), KSTEP)
+    term = jnp.dot(rows[...], w_ref[:, cols], preferred_element_type=F32).astype(BF16)
     out_ref[0] = term[:, :WIDTH]
     out_ref[1] = term[:, WIDTH:]
 
 
 def project(place, mine, yours, w):
     return call(
-        project_kernel, "project", place, (mine, yours, in_hbm(w)),
+        project_kernel, "project", place, (mine, yours, w),
         (struct((NHEAD, BLK, WIDTH), BF16),),
         grid=(STEPS,),
         in_specs=[
             whole(mine.shape), whole(yours.shape),
-            pl.BlockSpec((2 * HW, KSTEP), lambda i, _: (0, i)),
+            IN_VMEM,
         ],
         out_specs=[pl.BlockSpec((2, BLK, WIDTH), lambda i, _: (i, 0, 0))],
         scratch=(pltpu.VMEM((BLK, 2 * HW), BF16),),
@@ -362,7 +420,7 @@
 
 
 def rest(place, layer, before, intra, cum, qs, gain, w):
-    mine, yours = finish(place, layer, before, intra, cum, qs, gain.reshape(2 * HC, DH))
+    mine, yours, w = finish(place, layer, before, intra, cum, qs, gain.reshape(2 * HC, DH), w)
     yours = lax.ppermute(yours, "c", SWAP)
     terms = exchange(project(place, mine, yours, w), ("x", "yl"))
     return jnp.sum(terms.astype(F32), axis=0)
@@ -383,37 +441,32 @@
         place, in_hbm(k1), other_k, in_hbm(v1), other_v, decays, other_decays
     )
 
-    *weights, q1, _ = lax.optimization_barrier((wk2, wv2, wq2, q1, pieces))
+    w_cat = jnp.concatenate([wk2, wv2, wq2], axis=1)
+    far = lax.ppermute(w_cat, "yh", SWAP)
+    other_w, = swapped(w_cat)
+    q1 = after(q1, pieces)
     other_q, = swapped(q1)
-    own_w = jnp.concatenate([lax.dynamic_slice_in_dim(w, core * HW, HW, axis=1) for w in weights], axis=1)
-    send_w = [lax.dynamic_slice_in_dim(w, (1 - core) * HW, HW, axis=1) for w in weights]
-    other_w, = swapped(jnp.concatenate(send_w, axis=1))
-    first = jnp.where(core == 0, own_w, other_w)
-    second = jnp.where(core == 0, other_w, own_w)
-    near = jnp.concatenate([first, second], axis=0)
-    far = lax.ppermute(near, "yh", SWAP)
-
-    sums = after(exchange(pieces, ("yh", "z")), near, other_q)
-    far_late = after(far, sums)
-    before = exchange(scan(place, sums), ("yh", "z"))
-
-    def gather(cols):
-        both = jnp.concatenate([near[None, :, cols], far_late[None, :, cols]], axis=0)
-        return both, lambda rows: lax.all_gather(rows, "z", axis=1, tiled=True)
-
-    rows_kv, gather_kv = gather(slice(0, 2 * HW))
-    rows_q, gather_q = gather(slice(2 * HW, 3 * HW))
+    sums = after(exchange(pieces, ("yh", "z")), other_q)
+    scanned = scan(place, sums)
+    far = after(far, scanned)
+    far_other, = swapped(far)
+    rows_kv, rows_q = pack(place, w_cat, other_w, far, far_other)
+    before = exchange(scanned, ("yh", "z"))
+
+    def gather(rows):
+        return lax.all_gather(rows, "z", axis=1, tiled=True)
+
     ks, rows_kv, rows_q = lax.optimization_barrier((ks, rows_kv, rows_q))
-    wkv = gather_kv(rows_kv)
+    wkv = gather(rows_kv)
     intra, qs = first_intra(place, q1, other_q, ks, vs, cum, across)
     first_share = rest(place, 0, before, intra, cum, qs, gain_out1, wo1)
     stream = (stream_in.astype(F32) + first_share).astype(BF16)
-    wq = gather_q(after(rows_q, stream))
+    wq = gather(after(rows_q, stream))
 
     mine = exchange(jnp.broadcast_to(stream[None], (NHEAD, BLK, WIDTH)), ("x", "yl"))
     yours = lax.ppermute(mine, "c", SWAP)
     gain = gain_in2.reshape(NHEAD, 1, WIDTH)
-    own = own_kv(place, mine, wkv, gain)
+    own, wkv = own_kv(place, mine, wkv, gain)
     pieces, ks, vs = second_state(place, yours, wkv, gain, own, cum)
     sums = exchange(pieces, ("yh", "z"))
     before = exchange(scan(place, sums), ("yh", "z"))

time: 200 us -> 196 us (0.980)
  Pallas kernels: 44.4 us -> 40.1 us
    pallas_call x11 -> x12, Pallas kernels: 44.4 us -> 40.1 us  [call(): pl.pallas_call(kernel, out_shape=outs, grid_spec=pltpu.PrefetchScalarGrid...]
    ppermute x5 -> x6, starting transfers between devices: 4.84 us -> 6.36 us  [swapped(): return [lax.ppermute(a, 'c', SWAP) for a in arrays]]
    unnamed x26 -> x22, local copies, waits for them, and re-layouts: 4.14 us -> 4.56 us
  transfers between devices with their start and end apart: 14 -> 15, of which waited for: 6 -> 6; matrix products, arithmetic and copies ran while one was open for 1% -> 2% of each run, Pallas kernels for 17% -> 16%
where the time goes in v3:
time: 196 us; the launch traced here: 195 us
  blocking collectives  85 us (43%)
  Pallas kernels  40.1 us (20%)
  starting transfers between devices  31.2 us (16%)
  waiting for transfers between devices  17.7 us (9%)
  between operations  13.6 us (7%)
  local copies, waits for them, and re-layouts  5.62 us (3%)
  other arithmetic  2.05 us (1%)
    all_to_all x4, blocking collectives, exchange(): return lax.all_to_all(parts, axes, 0, 0)  85 us
    pallas_call x12, Pallas kernels, call(): pl.pallas_call(kernel, out_shape=outs, grid_spec=pltpu.PrefetchScalarGrid...  40.1 us
    all_to_all x3, starting transfers between devices, exchange(): return lax.all_to_all(parts, axes, 0, 0)  16.6 us
    all_to_all x3, waiting for transfers between devices, exchange(): return lax.all_to_all(parts, axes, 0, 0)  14.1 us
    ppermute x6, starting transfers between devices, swapped(): return [lax.ppermute(a, 'c', SWAP) for a in arrays]  6.36 us
    unnamed x22, local copies, waits for them, and re-layouts  4.56 us
    ppermute x2, starting transfers between devices, rest(): yours = lax.ppermute(yours, 'c', SWAP)  4.09 us
  transfers between devices with their start and end apart: 15, of which 6 were waited for; matrix products, arithmetic and copies ran while one was open for 2% of the time, Pallas kernels for 16%

profile of v3, /device:TPU:1, one launch (start us, length us, event | category | flops | bytes accessed | tf_op | source)
XLA Modules:
  0.0 195.3 jit_solution(11858107848353912714)
XLA Ops:
  6.5 0.8 pad_maximum_fusion.decay_ref
  7.3 3.2 %collective-permute-start.2 = (f32[12,256]{1,0:T(8,128)S(1)}, f32[12,256]{1,0:T(8,128)S(1)}, u32[]{:S(2)}, u32[]{:S(2)}) collective-permute-start(f32[12,256]{1,0:T(8,128)S(1)} %pad_maximum_fusion.decay_ref), channel_id=1, source_target_pairs={{0,8},{8,0},{1,9},{9,1},{2,10},{10,2},{3,11},{11,3},{4,12},{12,4},... | collective-permute-start | bytes 36872 | tf_op jit(solution)/shard_map/ppermute | solution.py:436
  10.6 0.1 collective-permute-start
  10.6 0.4 collective-permute-start.1
  11.1 0.9 constant_dynamic-update-slice_fusion.2
  12.0 0.9 constant_dynamic-update-slice_fusion.1
  12.9 0.9 constant_dynamic-update-slice_fusion.own_ref
  13.8 1.3 collective-permute-start.5
  15.1 0.1 pad_add_fusion.place.refs_0_
  15.2 0.0 collective-permute-done.2.other_decay_ref
  15.2 0.0 collective-permute-done.other_k_ref
  15.2 0.0 collective-permute-done.1.other_v_ref
  15.2 3.9 %first_state.1 = (bf16[16,32,128]{2,1,0:T(8,128)(2,1)}, bf16[512,384]{1,0:T(8,128)(2,1)}, bf16[512,384]{1,0:T(8,128)(2,1)}, f32[512,128]{1,0:T(8,128)S(1)}, f32[8,512]{1,0:T(8,128)S(1)}) custom-call(s32[2]{0:T(128)S(1)} %pad_add_fusion.place.refs_0_, bf16[256,768]{1,0:T(8,128)(2,1)} %k_ref.1, bf16[256,768]{1,0:T(8,128)(2,1)S(1)} %collective-permute-done.other_k_ref, ...), custom_call_target="tpu_custom_call" | custom-call | tf_op jit(solution)/shard_map/first_state/pallas_call | solution.py:40
  19.1 0.3 collective-permute-start.3
  19.4 8.3 %all-to-all-start = ((bf16[16,32,128]{2,1,0:T(8,128)(2,1)}), bf16[16,32,128]{2,1,0:T(8,128)(2,1)S(1)}, u32[]{:S(2)}, u32[]{:S(2)}) async-start(bf16[16,32,128]{2,1,0:T(8,128)(2,1)} %get-tuple-element.34), calls=%async_computation | async-start | bytes 262144 | tf_op jit(solution)/shard_map/all_to_all | solution.py:415
  27.7 0.0 copy-start.5
  27.7 0.0 all-gather.3.cloned.1.call-start
  27.8 0.5 collective-permute-start.4
  28.3 8.3 %all-to-all-done.in_ref = bf16[16,32,128]{2,1,0:T(8,128)(2,1)S(1)} async-done(((bf16[16,32,128]{2,1,0:T(8,128)(2,1)}), bf16[16,32,128]{2,1,0:T(8,128)(2,1)S(1)}, u32[]{:S(2)}, u32[]{:S(2)}) %all-to-all-start) | async-done | bytes 131104 | tf_op jit(solution)/shard_map/all_to_all | solution.py:415
  36.6 0.0 collective-permute-done.3.other_ref
  36.6 1.2 scan.2
  37.9 0.0 collective-permute-done.5.far_ref
  37.9 1.7 collective-permute-start.6
  39.6 0.0 collective-permute-done.4.other_ref
  39.6 1.4 collective-permute-done.6.far_other_ref
  41.0 1.6 pack.1
  42.7 0.0 all-gather.3.cloned.1.call-update
  42.7 3.5 %all-to-all-start.1 = ((bf16[16,32,128]{2,1,0:T(8,128)(2,1)}), bf16[16,32,128]{2,1,0:T(8,128)(2,1)S(1)}, u32[]{:S(2)}, u32[]{:S(2)}) async-start(bf16[16,32,128]{2,1,0:T(8,128)(2,1)} %scan.2), calls=%async_computation.1 | async-start | bytes 262144 | tf_op jit(solution)/shard_map/all_to_all | solution.py:415
  46.2 0.0 all-gather.5.cloned.1.call-start
  46.3 3.2 %first_intra.1 = (f32[512,384]{1,0:T(8,128)S(1)}, bf16[512,384]{1,0:T(8,128)(2,1)S(1)}) custom-call(s32[2]{0:T(128)S(1)} %pad_add_fusion.place.refs_0_, bf16[256,768]{1,0:T(8,128)(2,1)S(1)} %copy-done.1, bf16[256,768]{1,0:T(8,128)(2,1)S(1)} %collective-permute-done.3.other_ref, bf16[512,384]{1,0:T(8,128)(2,1)} %get-tuple-element.41.ks, ...), custom_call_target="tpu_custom_call" | custom-call | tf_op jit(solution)/shard_map/first_intra/pallas_call | solution.py:40
  49.4 5.7 %all-to-all-done.1.refs_1_ = bf16[16,32,128]{2,1,0:T(8,128)(2,1)S(1)} async-done(((bf16[16,32,128]{2,1,0:T(8,128)(2,1)}), bf16[16,32,128]{2,1,0:T(8,128)(2,1)S(1)}, u32[]{:S(2)}, u32[]{:S(2)}) %all-to-all-start.1) | async-done | bytes 131104 | tf_op jit(solution)/shard_map/all_to_all | solution.py:415
  55.1 2.9 %finish.2 = (bf16[256,384]{1,0:T(8,128)(2,1)S(1)}, bf16[256,384]{1,0:T(8,128)(2,1)S(1)}, bf16[768,3072]{1,0:T(8,128)(2,1)S(1)}) custom-call(s32[2]{0:T(128)S(1)} %pad_add_fusion.place.refs_0_, bf16[16,32,128]{2,1,0:T(8,128)(2,1)S(1)} %all-to-all-done.1.refs_1_, f32[512,384]{1,0:T(8,128)S(1)} %get-tuple-element.45.refs_2_, ...), custom_call_target="tpu_custom_call" | custom-call | tf_op jit(solution)/shard_map/finish/pallas_call | solution.py:40
  58.0 1.9 collective-permute-start.7
  60.0 1.1 collective-permute-done.7.yours_ref
  61.0 2.6 %project.2 = bf16[8,256,384]{2,1,0:T(8,128)(2,1)S(1)} custom-call(s32[2]{0:T(128)S(1)} %pad_add_fusion.place.refs_0_, bf16[256,384]{1,0:T(8,128)(2,1)S(1)} %get-tuple-element.47.mine_ref, bf16[256,384]{1,0:T(8,128)(2,1)S(1)} %collective-permute-done.7.yours_ref, bf16[768,3072]{1,0:T(8,128)(2,1)S(1)} %get-tuple-element.49.w_ref), custom_call_target="tpu_custom_call" | custom-call | flops 1207959552 | tf_op jit(solution)/shard_map/project/pallas_call | solution.py:40
  63.7 0.0 copy-start.9
  63.7 24.6 %all_to_all.35 = bf16[8,256,384]{2,1,0:T(8,128)(2,1)S(1)} all-to-all(bf16[8,256,384]{2,1,0:T(8,128)(2,1)S(1)} %project.2), channel_id=1, replica_groups=mesh['yh'=2,'z'=8,'c'=2,'x'=4,'yl'=2] {'x','yl'}, dimensions={0} | all-to-all | bytes 3145728 | tf_op jit(solution)/shard_map/all_to_all | solution.py:415
  88.3 0.2 convert_reduce_fusion.1
  88.6 0.0 copy-start.7
  88.6 0.0 all-gather.5.cloned.1.call-update
  88.6 0.6 copy-done.7
  89.2 0.1 broadcast_in_dim.2
  89.4 22.7 %all_to_all.36.h_ref.mine_ref = bf16[8,256,384]{2,1,0:T(8,128)(2,1)S(1)} all-to-all(bf16[8,256,384]{2,1,0:T(8,128)(2,1)S(1)} %broadcast_in_dim.2), channel_id=1, replica_groups=mesh['yh'=2,'z'=8,'c'=2,'x'=4,'yl'=2] {'x','yl'}, dimensions={0} | all-to-all | bytes 3145728 | tf_op jit(solution)/shard_map/all_to_all | solution.py:415
  112.1 2.8 %collective-permute-start.8 = (bf16[8,256,384]{2,1,0:T(8,128)(2,1)S(1)}, bf16[8,256,384]{2,1,0:T(8,128)(2,1)S(1)}, u32[]{:S(2)}, u32[]{:S(2)}) collective-permute-start(bf16[8,256,384]{2,1,0:T(8,128)(2,1)S(1)} %all_to_all.36.h_ref.mine_ref), channel_id=1, source_target_pairs={{0,8},{8,0},{1,9},{9,1},{2,10},{10,2},{3,11},{11,3},{4,12},{12,4},... | collective-permute-start | bytes 4718600 | tf_op jit(solution)/shard_map/ppermute | solution.py:467
  114.9 4.5 %own_kv.1 = (bf16[256,768]{1,0:T(8,128)(2,1)S(1)}, bf16[2,1536,768]{2,1,0:T(8,128)(2,1)S(1)}) custom-call(s32[2]{0:T(128)S(1)} %pad_add_fusion.place.refs_0_, bf16[8,256,384]{2,1,0:T(8,128)(2,1)S(1)} %all_to_all.36.h_ref.mine_ref, bf16[2,1536,768]{2,1,0:T(8,128)(2,1)} %all-gather.3.cloned.1.call-done.w_ref, f32[8,1,384]{2,1,0:T(1,128)S(1)} %bitcast.7), custom_call_target="tpu_custom_call" | custom-call | tf_op jit(solution)/shard_map/own_kv/pallas_call | solution.py:40
  119.4 0.0 collective-permute-done.8.h_ref.yours_ref
  119.4 4.7 %second_state.1 = (bf16[16,32,128]{2,1,0:T(8,128)(2,1)S(1)}, bf16[512,384]{1,0:T(8,128)(2,1)}, bf16[512,384]{1,0:T(8,128)(2,1)}) custom-call(s32[2]{0:T(128)S(1)} %pad_add_fusion.place.refs_0_, bf16[8,256,384]{2,1,0:T(8,128)(2,1)S(1)} %collective-permute-done.8.h_ref.yours_ref, bf16[2,1536,768]{2,1,0:T(8,128)(2,1)S(1)} %get-tuple-element.51.w_ref, ...), custom_call_target="tpu_custom_call" | custom-call | tf_op jit(solution)/shard_map/second_state/pallas_call | solution.py:40
  124.2 14.5 %all_to_all.37.in_ref = bf16[16,32,128]{2,1,0:T(8,128)(2,1)S(1)} all-to-all(bf16[16,32,128]{2,1,0:T(8,128)(2,1)S(1)} %get-tuple-element.53), channel_id=1, replica_groups=mesh['yh'=2,'z'=8,'c'=2,'x'=4,'yl'=2] {'yh','z'}, dimensions={0} | all-to-all | bytes 262144 | tf_op jit(solution)/shard_map/all_to_all | solution.py:415
  138.7 0.6 scan.3
  139.3 0.6 copy-done
  139.9 4.8 %all-to-all-start.5 = ((bf16[16,32,128]{2,1,0:T(8,128)(2,1)}), bf16[16,32,128]{2,1,0:T(8,128)(2,1)S(1)}, u32[]{:S(2)}, u32[]{:S(2)}) async-start(bf16[16,32,128]{2,1,0:T(8,128)(2,1)} %copy-done), calls=%async_computation.5 | async-start | bytes 262144 | tf_op jit(solution)/shard_map/all_to_all | solution.py:415
  144.7 0.0 all-gather.5.cloned.1.call-done.w_ref
  144.7 0.7 copy-done.4
  145.5 8.1 %second_intra.1 = (f32[512,384]{1,0:T(8,128)}, bf16[512,384]{1,0:T(8,128)(2,1)}) custom-call(s32[2]{0:T(128)S(1)} %pad_add_fusion.place.refs_0_, bf16[8,256,384]{2,1,0:T(8,128)(2,1)S(1)} %all_to_all.36.h_ref.mine_ref, bf16[8,256,384]{2,1,0:T(8,128)(2,1)S(1)} %collective-permute-done.8.h_ref.yours_ref, ...), custom_call_target="tpu_custom_call" | custom-call | tf_op jit(solution)/shard_map/second_intra/pallas_call | solution.py:40
  153.6 0.1 all-to-all-done.5.refs_1_
  153.6 0.7 copy-done.6
  154.3 4.1 %finish.3 = (bf16[256,384]{1,0:T(8,128)(2,1)S(1)}, bf16[256,384]{1,0:T(8,128)(2,1)S(1)}, bf16[768,3072]{1,0:T(8,128)(2,1)S(1)}) custom-call(s32[2]{0:T(128)S(1)} %pad_add_fusion.place.refs_0_, bf16[16,32,128]{2,1,0:T(8,128)(2,1)S(1)} %all-to-all-done.5.refs_1_, f32[512,384]{1,0:T(8,128)} %get-tuple-element.58.refs_2_, ...), custom_call_target="tpu_custom_call" | custom-call | tf_op jit(solution)/shard_map/finish/pallas_call | solution.py:40
  158.5 2.2 %collective-permute-start.9 = (bf16[256,384]{1,0:T(8,128)(2,1)S(1)}, bf16[256,384]{1,0:T(8,128)(2,1)S(1)}, u32[]{:S(2)}, u32[]{:S(2)}) collective-permute-start(bf16[256,384]{1,0:T(8,128)(2,1)S(1)} %get-tuple-element.61), channel_id=1, source_target_pairs={{0,8},{8,0},{1,9},{9,1},{2,10},{10,2},{3,11},{11,3},{4,12},{12,4},... | collective-permute-start | bytes 589832 | tf_op jit(solution)/shard_map/ppermute | solution.py:424
  160.6 1.1 collective-permute-done.9.yours_ref
  161.7 2.6 %project.3 = bf16[8,256,384]{2,1,0:T(8,128)(2,1)S(1)} custom-call(s32[2]{0:T(128)S(1)} %pad_add_fusion.place.refs_0_, bf16[256,384]{1,0:T(8,128)(2,1)S(1)} %get-tuple-element.60.mine_ref, bf16[256,384]{1,0:T(8,128)(2,1)S(1)} %collective-permute-done.9.yours_ref, bf16[768,3072]{1,0:T(8,128)(2,1)S(1)} %get-tuple-element.62.w_ref), custom_call_target="tpu_custom_call" | custom-call | flops 1207959552 | tf_op jit(solution)/shard_map/project/pallas_call | solution.py:40
  164.3 0.0 copy-start.8
  164.4 23.1 %all_to_all.38 = bf16[8,256,384]{2,1,0:T(8,128)(2,1)S(1)} all-to-all(bf16[8,256,384]{2,1,0:T(8,128)(2,1)S(1)} %project.3), channel_id=1, replica_groups=mesh['yh'=2,'z'=8,'c'=2,'x'=4,'yl'=2] {'x','yl'}, dimensions={0} | all-to-all | bytes 3145728 | tf_op jit(solution)/shard_map/all_to_all | solution.py:415
  187.5 0.2 convert_reduce_fusion
  187.7 0.7 add_convert_fusion
  (14 shorter events, 0.1 us)
Async XLA Ops:
  6.5 12.5 %copy-start.1 = (bf16[256,768]{1,0:T(8,128)(2,1)S(1)}, bf16[256,768]{1,0:T(8,128)(2,1)}, u32[]{:S(2)}) copy-start(bf16[256,768]{1,0:T(8,128)(2,1)} %q_ref) | copy-start | bytes 1179652
  7.3 7.9 %collective-permute-start.2 = (f32[12,256]{1,0:T(8,128)S(1)}, f32[12,256]{1,0:T(8,128)S(1)}, u32[]{:S(2)}, u32[]{:S(2)}) collective-permute-start(f32[12,256]{1,0:T(8,128)S(1)} %pad_maximum_fusion.decay_ref), channel_id=1, source_target_pairs={{0,8},{8,0},{1,9},{9,1},{2,10},{10,2},{3,11},{11,3},{4,12},{12,4},... | collective-permute-start | bytes 36872 | tf_op jit(solution)/shard_map/ppermute | solution.py:436
  10.6 4.6 %collective-permute-start = (bf16[256,768]{1,0:T(8,128)(2,1)}, bf16[256,768]{1,0:T(8,128)(2,1)S(1)}, u32[]{:S(2)}, u32[]{:S(2)}) collective-permute-start(bf16[256,768]{1,0:T(8,128)(2,1)} %k_ref.1), channel_id=1, source_target_pairs={{0,8},{8,0},{1,9},{9,1},{2,10},{10,2},{3,11},{11,3},{4,12},{12,4},... | collective-permute-start | bytes 1179656 | tf_op jit(solution)/shard_map/ppermute | solution.py:436
  10.6 4.6 %collective-permute-start.1 = (bf16[256,768]{1,0:T(8,128)(2,1)}, bf16[256,768]{1,0:T(8,128)(2,1)S(1)}, u32[]{:S(2)}, u32[]{:S(2)}) collective-permute-start(bf16[256,768]{1,0:T(8,128)(2,1)} %v_ref.1), channel_id=1, source_target_pairs={{0,8},{8,0},{1,9},{9,1},{2,10},{10,2},{3,11},{11,3},{4,12},{12,4},... | collective-permute-start | bytes 1179656 | tf_op jit(solution)/shard_map/ppermute | solution.py:436
  13.8 24.0 %collective-permute-start.5 = (bf16[96,2304]{1,0:T(8,128)(2,1)S(1)}, bf16[96,2304]{1,0:T(8,128)(2,1)S(1)}, u32[]{:S(2)}, u32[]{:S(2)}) collective-permute-start(bf16[96,2304]{1,0:T(8,128)(2,1)S(1)} %constant_dynamic-update-slice_fusion.own_ref), channel_id=1, source_target_pairs={{0,128},{128,0},{1,129},{129,1},{2,130},{130,2},{3,131},{131,3},{4... | collective-permute-start | bytes 1327112 | tf_op jit(solution)/shard_map/ppermute | solution.py:445
  19.1 30.4 %copy-start.3 = (f32[8,512]{1,0:T(8,128)}, f32[8,512]{1,0:T(8,128)S(1)}, u32[]{:S(2)}) copy-start(f32[8,512]{1,0:T(8,128)S(1)} %get-tuple-element.44.across_ref) | copy-start | bytes 49156
  19.1 17.6 %collective-permute-start.3 = (bf16[256,768]{1,0:T(8,128)(2,1)S(1)}, bf16[256,768]{1,0:T(8,128)(2,1)S(1)}, u32[]{:S(2)}, u32[]{:S(2)}) collective-permute-start(bf16[256,768]{1,0:T(8,128)(2,1)S(1)} %copy-done.1), channel_id=1, source_target_pairs={{0,8},{8,0},{1,9},{9,1},{2,10},{10,2},{3,11},{11,3},{4,12},{12,4},... | collective-permute-start | bytes 1179656 | tf_op jit(solution)/shard_map/ppermute | solution.py:436
  19.4 17.2 %all-to-all-start = ((bf16[16,32,128]{2,1,0:T(8,128)(2,1)}), bf16[16,32,128]{2,1,0:T(8,128)(2,1)S(1)}, u32[]{:S(2)}, u32[]{:S(2)}) async-start(bf16[16,32,128]{2,1,0:T(8,128)(2,1)} %get-tuple-element.34), calls=%async_computation | async-start | bytes 262144 | tf_op jit(solution)/shard_map/all_to_all | solution.py:415
  27.7 27.4 %copy-start.5 = (f32[768]{0:T(1024)S(1)}, f32[768]{0:T(1024)}, u32[]{:S(2)}) copy-start(f32[768]{0:T(1024)} %param.18) | copy-start | bytes 9220
  27.7 87.1 %all-gather.3.cloned.1.call-start = ((), (), s32[]{:S(2)}) async-start(), calls=%async_computation.7 | async-start | bytes 5308416 | tf_op jit(solution)/shard_map/all_gather | solution.py:457
  27.8 11.9 %collective-permute-start.4 = (bf16[96,2304]{1,0:T(8,128)(2,1)S(1)}, bf16[96,2304]{1,0:T(8,128)(2,1)S(1)}, u32[]{:S(2)}, u32[]{:S(2)}) collective-permute-start(bf16[96,2304]{1,0:T(8,128)(2,1)S(1)} %constant_dynamic-update-slice_fusion.own_ref), channel_id=1, source_target_pairs={{0,8},{8,0},{1,9},{9,1},{2,10},{10,2},{3,11},{11,3},{4,12},{12,4},... | collective-permute-start | bytes 1327112 | tf_op jit(solution)/shard_map/ppermute | solution.py:436
  37.9 3.2 %collective-permute-start.6 = (bf16[96,2304]{1,0:T(8,128)(2,1)S(1)}, bf16[96,2304]{1,0:T(8,128)(2,1)S(1)}, u32[]{:S(2)}, u32[]{:S(2)}) collective-permute-start(bf16[96,2304]{1,0:T(8,128)(2,1)S(1)} %collective-permute-done.5.far_ref), channel_id=1, source_target_pairs={{0,8},{8,0},{1,9},{9,1},{2,10},{10,2},{3,11},{11,3},{4,12},{12,4},... | collective-permute-start | bytes 1327112 | tf_op jit(solution)/shard_map/ppermute | solution.py:436
  42.7 12.4 %all-to-all-start.1 = ((bf16[16,32,128]{2,1,0:T(8,128)(2,1)}), bf16[16,32,128]{2,1,0:T(8,128)(2,1)S(1)}, u32[]{:S(2)}, u32[]{:S(2)}) async-start(bf16[16,32,128]{2,1,0:T(8,128)(2,1)} %scan.2), calls=%async_computation.1 | async-start | bytes 262144 | tf_op jit(solution)/shard_map/all_to_all | solution.py:415
  46.2 98.5 %all-gather.5.cloned.1.call-start = ((), (), s32[]{:S(2)}) async-start(), calls=%async_computation.8 | async-start | bytes 2654208 | tf_op jit(solution)/shard_map/all_gather | solution.py:457
  58.0 3.0 %collective-permute-start.7 = (bf16[256,384]{1,0:T(8,128)(2,1)S(1)}, bf16[256,384]{1,0:T(8,128)(2,1)S(1)}, u32[]{:S(2)}, u32[]{:S(2)}) collective-permute-start(bf16[256,384]{1,0:T(8,128)(2,1)S(1)} %get-tuple-element.48), channel_id=1, source_target_pairs={{0,8},{8,0},{1,9},{9,1},{2,10},{10,2},{3,11},{11,3},{4,12},{12,4},... | collective-permute-start | bytes 589832 | tf_op jit(solution)/shard_map/ppermute | solution.py:424
  63.7 24.8 %copy-start.9 = (bf16[256,384]{1,0:T(8,128)(2,1)S(1)}, bf16[256,384]{1,0:T(8,128)(2,1)}, u32[]{:S(2)}) copy-start(bf16[256,384]{1,0:T(8,128)(2,1)} %param.20) | copy-start | bytes 589828
  88.6 0.7 copy-start.7
  89.2 25.6 %copy-start.2 = (f32[3072]{0:T(1024)S(1)}, f32[3072]{0:T(1024)}, u32[]{:S(2)}) copy-start(f32[3072]{0:T(1024)} %param.21) | copy-start | bytes 36868
  112.1 7.3 %collective-permute-start.8 = (bf16[8,256,384]{2,1,0:T(8,128)(2,1)S(1)}, bf16[8,256,384]{2,1,0:T(8,128)(2,1)S(1)}, u32[]{:S(2)}, u32[]{:S(2)}) collective-permute-start(bf16[8,256,384]{2,1,0:T(8,128)(2,1)S(1)} %all_to_all.36.h_ref.mine_ref), channel_id=1, source_target_pairs={{0,8},{8,0},{1,9},{9,1},{2,10},{10,2},{3,11},{11,3},{4,12},{12,4},... | collective-permute-start | bytes 4718600 | tf_op jit(solution)/shard_map/ppermute | solution.py:467
  139.3 0.7 copy-start
  139.9 13.7 %all-to-all-start.5 = ((bf16[16,32,128]{2,1,0:T(8,128)(2,1)}), bf16[16,32,128]{2,1,0:T(8,128)(2,1)S(1)}, u32[]{:S(2)}, u32[]{:S(2)}) async-start(bf16[16,32,128]{2,1,0:T(8,128)(2,1)} %copy-done), calls=%async_computation.5 | async-start | bytes 262144 | tf_op jit(solution)/shard_map/all_to_all | solution.py:415
  144.7 0.7 copy-start.4
  153.6 0.7 copy-start.6
  158.5 3.3 %collective-permute-start.9 = (bf16[256,384]{1,0:T(8,128)(2,1)S(1)}, bf16[256,384]{1,0:T(8,128)(2,1)S(1)}, u32[]{:S(2)}, u32[]{:S(2)}) collective-permute-start(bf16[256,384]{1,0:T(8,128)(2,1)S(1)} %get-tuple-element.61), channel_id=1, source_target_pairs={{0,8},{8,0},{1,9},{9,1},{2,10},{10,2},{3,11},{11,3},{4,12},{12,4},... | collective-permute-start | bytes 589832 | tf_op jit(solution)/shard_map/ppermute | solution.py:424
  164.3 23.4 %copy-start.8 = (bf16[256,384]{1,0:T(8,128)(2,1)S(1)}, bf16[256,384]{1,0:T(8,128)(2,1)}, u32[]{:S(2)}) copy-start(bf16[256,384]{1,0:T(8,128)(2,1)} %copy-done.7) | copy-start | bytes 589828
Sparse Core Ops, SparseCore 0:
  42.8 55.8 all-gather.2
  100.5 39.0 all-gather.4

commit v4 on v3

--- a/solution.py
+++ b/solution.py
@@ -124,8 +124,11 @@
 
 
 def both_cores(core, mine_ref, yours_ref, out):
-    out[span(core, BLK), :] = silu(mine_ref[:, span(core, HW)].astype(F32)).astype(BF16)
-    out[span(1 - core, BLK), :] = silu(yours_ref[:, span(core, HW)].astype(F32)).astype(BF16)
+    out[span(core, BLK), :] = silu(mine_ref[...].astype(F32)).astype(BF16)
+    out[span(1 - core, BLK), :] = silu(yours_ref[...].astype(F32)).astype(BF16)
+
+
+HALF = pl.BlockSpec((BLK, HW), lambda _, place: (0, place[0]))
 
 
 def first_state_kernel(
@@ -144,7 +147,7 @@
 HEADS_OUT = pltpu.HBM((TOK, HW), BF16)
 QUERY_OUT = struct((TOK, HW), BF16)
 INTRA_OUT = struct((TOK, HW), F32)
-WO_OUT = pltpu.VMEM((2 * HW, NHEAD * WIDTH), BF16)
+WO_HALF = (2 * HW, NHEAD * WIDTH // 2)
 WKV_OUT = pltpu.VMEM((2, NHEAD * WIDTH // 2, 2 * HW), BF16)
 PIECES_OUT = struct((NCHIP, PIECE, DH), BF16)
 
@@ -152,20 +155,54 @@
 def first_state(place, *args):
     outs = (PIECES_OUT, HEADS_OUT, HEADS_OUT, struct((TOK, DH), F32), struct((8, TOK), F32))
     scratch = (pltpu.VMEM((16, TOK), F32),)
-    return call(first_state_kernel, "first_state", place, args, outs, scratch=scratch)
-
-
-def first_intra_kernel(
-    place, q_ref, other_ref, ks, vs, cum_ref, across_ref, intra_ref, qs
-):
-    core = place[0]
-    both_cores(core, q_ref, other_ref, qs)
+    specs = [HALF] * 4 + [whole(a.shape) for a in args[4:]]
+    return call(
+        first_state_kernel, "first_state", place, args, outs, in_specs=specs, scratch=scratch
+    )
+
+
+def cut_kernel(place, k_ref, v_ref, q_ref, both_ref, give_ref):
+    core = place[0]
+    for n, src in enumerate((k_ref, v_ref, q_ref)):
+        both_ref[:, n * HW : (n + 1) * HW] = src[:, span(core, HW)]
+        give = src[:, span(1 - core, HW)]
+        both_ref[:, (n + 3) * HW : (n + 4) * HW] = give
+        give_ref[:, n * HW : (n + 1) * HW] = give
+
+
+def cut(place, *weights):
+    rows = weights[0].shape[0]
+    outs = (struct((rows, 6 * HW), BF16), struct((rows, 3 * HW), BF16))
+    return call(cut_kernel, "cut", place, weights, outs)
+
+
+def pack_kernel(place, near_ref, near_other_ref, far_ref, far_other_ref, kv_ref, wq_ref):
+    core = place[0]
+    rows = near_ref.shape[0]
+    for n, pair in enumerate(((near_ref, near_other_ref), (far_ref, far_other_ref))):
+        for src, owner in zip(pair, (core, 1 - core)):
+            at = pl.ds(pl.multiple_of(owner * rows, rows), rows)
+            kv_ref[n, at, :] = src[:, : 2 * HW]
+            wq_ref[n, at, :] = src[:, 2 * HW : 3 * HW]
+
+
+def pack(place, *parts):
+    rows = 2 * parts[0].shape[0]
+    outs = (pltpu.HBM((2, rows, 2 * HW), BF16), pltpu.HBM((2, rows, HW), BF16))
+    return call(pack_kernel, "pack", place, parts, outs)
+
+
+def first_intra_kernel(place, q_ref, other_ref, ks, vs, cum_ref, across_ref, intra_ref, qs):
+    both_cores(place[0], q_ref, other_ref, qs)
     make_intra(qs, ks, vs, cum_ref, across_ref, 0, intra_ref)
 
 
 def first_intra(place, q, other, ks, vs, cum, across):
     args = (q, other, in_hbm(ks), in_hbm(vs), cum, across)
-    return call(first_intra_kernel, "first_intra", place, args, (INTRA_OUT, QUERY_OUT))
+    specs = [HALF] * 2 + [whole(a.shape) for a in args[2:]]
+    return call(
+        first_intra_kernel, "first_intra", place, args, (INTRA_OUT, QUERY_OUT), in_specs=specs
+    )
 
 
 def project_step(h_ref, w, gain_ref, acc, square, rows):
@@ -306,29 +343,12 @@
     hs, ws, gs = projection_specs(HW)
     return call(
         second_intra_kernel, "second_intra", place,
-        (mine, yours, in_hbm(w), gain, in_hbm(ks), in_hbm(vs), cum, across),
+        (mine, yours, in_hbm(w), gain, in_hbm(ks), in_hbm(vs), cum, in_hbm(across)),
         (pltpu.HBM((TOK, HW), F32), HEADS_OUT),
         grid=(STEPS,),
         in_specs=[hs, hs, ws, gs] + [whole(a.shape) for a in (ks, vs, cum, across)],
         scratch=(pltpu.VMEM((TOK, HW), F32), pltpu.VMEM((TOK, DH), F32)),
     )
-
-
-def pack_kernel(place, own_ref, other_ref, far_ref, far_other_ref, kv_ref, q_ref):
-    core = place[0]
-    rows = own_ref.shape[0]
-    for n, pair in enumerate(((own_ref, other_ref), (far_ref, far_other_ref))):
-        for src, owner in zip(pair, (core, 1 - core)):
-            at = pl.ds(pl.multiple_of(owner * rows, rows), rows)
-            for i in range(2):
-                kv_ref[n, at, i * HW : (i + 1) * HW] = src[:, span(2 * i + core, HW)]
-            q_ref[n, at, :] = src[:, span(4 + core, HW)]
-
-
-def pack(place, *args):
-    rows = 2 * args[0].shape[0]
-    outs = (struct((2, rows, 2 * HW), BF16), struct((2, rows, HW), BF16))
-    return call(pack_kernel, "pack", place, args, outs)
 
 
 def scan_kernel(place, in_ref, out_ref):
@@ -344,7 +364,8 @@
 
 
 def scan(place, pieces):
-    return call(scan_kernel, "scan", place, (pieces,), (PIECES_OUT,))[0]
+    outs = (pltpu.HBM((NCHIP, PIECE, DH), BF16),)
+    return call(scan_kernel, "scan", place, (pieces,), outs)[0]
 
 
 def finish_kernel(
@@ -352,7 +373,7 @@
     mine_ref, yours_ref, held, out, sem,
 ):
     core = place[0]
-    fetch = pltpu.make_async_copy(wo_ref, held, sem)
+    fetch = pltpu.make_async_copy(wo_ref.at[:, : WO_HALF[1]], held, sem)
     fetch.start()
     pieces = pieces_ref[...].astype(F32)
     for h in range(HC):
@@ -375,39 +396,54 @@
     args = (pieces, intra, cum, qs, gain)
     return call(
         lambda *refs: finish_kernel(layer, *refs), "finish", place, (*args, in_hbm(wo)),
-        (struct((BLK, HW), BF16), struct((BLK, HW), BF16), WO_OUT),
+        (struct((BLK, HW), BF16), struct((BLK, HW), BF16), pltpu.VMEM(WO_HALF, BF16)),
         in_specs=[whole(a.shape) for a in args] + [ANY],
         out_specs=[whole((BLK, HW)), whole((BLK, HW)), IN_VMEM],
         scratch=(pltpu.VMEM((TOK, HW), BF16), pltpu.SemaphoreType.DMA),
     )
 
 
-def project_kernel(place, mine_ref, yours_ref, w_ref, out_ref, rows):
-    core = place[0]
-
-    @pl.when(pl.program_id(0) == 0)
-    def _():
+def project_kernel(place, mine_ref, yours_ref, near_ref, w_ref, out_ref, rows, held, sem):
+    core = place[0]
+    step = pl.program_id(0)
+    half = STEPS // 2
+    fetch = pltpu.make_async_copy(w_ref.at[:, WO_HALF[1] :], held, sem)
+
+    @pl.when(step == 0)
+    def _():
+        fetch.start()
         rows[:, span(core, HW)] = mine_ref[...]
         rows[:, span(1 - core, HW)] = yours_ref[...]
 
-    cols = span(pl.program_id(0), KSTEP)
-    term = jnp.dot(rows[...], w_ref[:, cols], preferred_element_type=F32).astype(BF16)
-    out_ref[0] = term[:, :WIDTH]
-    out_ref[1] = term[:, WIDTH:]
-
-
-def project(place, mine, yours, w):
-    return call(
-        project_kernel, "project", place, (mine, yours, w),
+    @pl.when(step == half)
+    def _():
+        fetch.wait()
+
+    def term(w):
+        cols = span(step % half, KSTEP)
+        part = jnp.dot(rows[...], w[:, cols], preferred_element_type=F32).astype(BF16)
+        out_ref[0] = part[:, :WIDTH]
+        out_ref[1] = part[:, WIDTH:]
+
+    @pl.when(step < half)
+    def _():
+        term(near_ref)
+
+    @pl.when(step >= half)
+    def _():
+        term(held)
+
+
+def project(place, mine, yours, near, w):
+    return call(
+        project_kernel, "project", place, (mine, yours, near, in_hbm(w)),
         (struct((NHEAD, BLK, WIDTH), BF16),),
         grid=(STEPS,),
-        in_specs=[
-            whole(mine.shape), whole(yours.shape),
-            IN_VMEM,
-        ],
+        in_specs=[whole(mine.shape), whole(yours.shape), IN_VMEM, ANY],
         out_specs=[pl.BlockSpec((2, BLK, WIDTH), lambda i, _: (i, 0, 0))],
-        scratch=(pltpu.VMEM((BLK, 2 * HW), BF16),),
-        flops=2 * BLK * 2 * HW * NHEAD * WIDTH,
+        scratch=(
+            pltpu.VMEM((BLK, 2 * HW), BF16), pltpu.VMEM(WO_HALF, BF16), pltpu.SemaphoreType.DMA,
+        ),
     )[0]
 
 
@@ -420,9 +456,10 @@
 
 
 def rest(place, layer, before, intra, cum, qs, gain, w):
-    mine, yours, w = finish(place, layer, before, intra, cum, qs, gain.reshape(2 * HC, DH), w)
+    gain = in_hbm(gain.reshape(2 * HC, DH))
+    mine, yours, near = finish(place, layer, before, intra, cum, qs, gain, w)
     yours = lax.ppermute(yours, "c", SWAP)
-    terms = exchange(project(place, mine, yours, w), ("x", "yl"))
+    terms = exchange(project(place, mine, yours, near, w), ("x", "yl"))
     return jnp.sum(terms.astype(F32), axis=0)
 
 
@@ -441,24 +478,27 @@
         place, in_hbm(k1), other_k, in_hbm(v1), other_v, decays, other_decays
     )
 
-    w_cat = jnp.concatenate([wk2, wv2, wq2], axis=1)
-    far = lax.ppermute(w_cat, "yh", SWAP)
-    other_w, = swapped(w_cat)
+    near, give = cut(place, wk2, wv2, wq2)
+    far = lax.ppermute(near, "yh", SWAP)
+    near_other, = swapped(give)
     q1 = after(q1, pieces)
     other_q, = swapped(q1)
-    sums = after(exchange(pieces, ("yh", "z")), other_q)
+    sums = after(exchange(pieces, ("yh", "z")), other_q, near_other)
     scanned = scan(place, sums)
+    before = exchange(scanned, ("yh", "z"))
     far = after(far, scanned)
-    far_other, = swapped(far)
-    rows_kv, rows_q = pack(place, w_cat, other_w, far, far_other)
-    before = exchange(scanned, ("yh", "z"))
+    far_other, = swapped(far[:, 3 * HW :])
+    intra, qs = first_intra(place, q1, other_q, ks, vs, cum, across)
+    before, intra, *parts = lax.optimization_barrier(
+        (before, intra, near, near_other, far, far_other)
+    )
+    near, near_other, far, far_other = parts
+    rows_kv, rows_q = pack(place, near, in_hbm(near_other), far, in_hbm(far_other))
 
     def gather(rows):
         return lax.all_gather(rows, "z", axis=1, tiled=True)
 
-    ks, rows_kv, rows_q = lax.optimization_barrier((ks, rows_kv, rows_q))
     wkv = gather(rows_kv)
-    intra, qs = first_intra(place, q1, other_q, ks, vs, cum, across)
     first_share = rest(place, 0, before, intra, cum, qs, gain_out1, wo1)
     stream = (stream_in.astype(F32) + first_share).astype(BF16)
     wq = gather(after(rows_q, stream))

time: 196 us -> 209 us (1.066)
  waiting for transfers between devices: 17.7 us -> 27.4 us
  Pallas kernels: 40.1 us -> 42.9 us
    all_gather x2, waiting for transfers between devices: 0.02 us -> 11.5 us  [gather(): return lax.all_gather(rows, 'z', axis=1, tiled=True)]
    pallas_call x12 -> x13, Pallas kernels: 40.1 us -> 42.9 us  [call(): pl.pallas_call(kernel, out_shape=outs, grid_spec=pltpu.PrefetchScalarGrid...]
    all_to_all x3, waiting for transfers between devices: 14.1 us -> 11.8 us  [exchange(): return lax.all_to_all(parts, axes, 0, 0)]
    unnamed x22 -> x20, local copies, waits for them, and re-layouts: 4.56 us -> 3.4 us
  transfers between devices with their start and end apart: 15 -> 15, of which waited for: 6 -> 7; matrix products, arithmetic and copies ran while one was open for 2% -> 1% of each run, Pallas kernels for 16% -> 16%
where the time goes in v4:
time: 209 us; the launch traced here: 208 us
  blocking collectives  84.9 us (41%)
  Pallas kernels  42.9 us (21%)
  starting transfers between devices  33.2 us (16%)
  waiting for transfers between devices  27.4 us (13%)
  between operations  13.6 us (7%)
  local copies, waits for them, and re-layouts  3.56 us (2%)
    all_to_all x4, blocking collectives, exchange(): return lax.all_to_all(parts, axes, 0, 0)  84.9 us
    pallas_call x13, Pallas kernels, call(): pl.pallas_call(kernel, out_shape=outs, grid_spec=pltpu.PrefetchScalarGrid...  42.9 us
    all_to_all x3, starting transfers between devices, exchange(): return lax.all_to_all(parts, axes, 0, 0)  17.1 us
    all_to_all x3, waiting for transfers between devices, exchange(): return lax.all_to_all(parts, axes, 0, 0)  11.8 us
    all_gather x2, waiting for transfers between devices, gather(): return lax.all_gather(rows, 'z', axis=1, tiled=True)  11.5 us
    ppermute x6, starting transfers between devices, swapped(): return [lax.ppermute(a, 'c', SWAP) for a in arrays]  6.21 us
    ppermute x2, starting transfers between devices, rest(): yours = lax.ppermute(yours, 'c', SWAP)  5.78 us
  transfers between devices with their start and end apart: 15, of which 7 were waited for; matrix products, arithmetic and copies ran while one was open for 1% of the time, Pallas kernels for 16%

profile of v4, /device:TPU:1, one launch (start us, length us, event | category | flops | bytes accessed | tf_op | source)
XLA Modules:
  0.0 207.5 jit_solution(6784734777074352169)
XLA Ops:
  6.5 3.2 %collective-permute-start = (bf16[256,768]{1,0:T(8,128)(2,1)}, bf16[256,768]{1,0:T(8,128)(2,1)S(1)}, u32[]{:S(2)}, u32[]{:S(2)}) collective-permute-start(bf16[256,768]{1,0:T(8,128)(2,1)} %k_ref.2), channel_id=1, source_target_pairs={{0,8},{8,0},{1,9},{9,1},{2,10},{10,2},{3,11},{11,3},{4,12},{12,4},... | collective-permute-start | bytes 1179656 | tf_op jit(solution)/shard_map/ppermute | solution.py:473
  9.8 0.0 collective-permute-start.1
  9.8 0.1 pad_add_fusion.place.refs_0_
  9.9 0.9 copy-done.1
  10.8 0.9 copy-done.2
  11.7 0.9 copy-done.3
  12.6 0.6 cut.1
  13.2 1.3 collective-permute-start.5
  14.5 0.7 pad_maximum_fusion.decay_ref
  15.2 0.8 collective-permute-start.2
  16.0 0.8 collective-permute-done.2.other_decay_ref
  16.8 0.0 collective-permute-done.other_k_ref
  16.8 0.0 collective-permute-done.1.other_v_ref
  16.8 3.8 %first_state.1 = (bf16[16,32,128]{2,1,0:T(8,128)(2,1)}, bf16[512,384]{1,0:T(8,128)(2,1)}, bf16[512,384]{1,0:T(8,128)(2,1)}, f32[512,128]{1,0:T(8,128)S(1)}, f32[8,512]{1,0:T(8,128)S(1)}) custom-call(s32[2]{0:T(128)S(1)} %pad_add_fusion.place.refs_0_, bf16[256,768]{1,0:T(8,128)(2,1)} %k_ref.2, bf16[256,768]{1,0:T(8,128)(2,1)S(1)} %collective-permute-done.other_k_ref, ...), custom_call_target="tpu_custom_call" | custom-call | tf_op jit(solution)/shard_map/first_state/pallas_call | solution.py:40
  20.6 0.3 collective-permute-start.3
  20.9 8.3 %all-to-all-start = ((bf16[16,32,128]{2,1,0:T(8,128)(2,1)}), bf16[16,32,128]{2,1,0:T(8,128)(2,1)S(1)}, u32[]{:S(2)}, u32[]{:S(2)}) async-start(bf16[16,32,128]{2,1,0:T(8,128)(2,1)} %get-tuple-element.39), calls=%async_computation | async-start | bytes 262144 | tf_op jit(solution)/shard_map/all_to_all | solution.py:451
  29.2 0.5 collective-permute-start.4
  29.8 1.1 collective-permute-done.4.near_other_ref
  30.9 7.3 %all-to-all-done.in_ref = bf16[16,32,128]{2,1,0:T(8,128)(2,1)S(1)} async-done(((bf16[16,32,128]{2,1,0:T(8,128)(2,1)}), bf16[16,32,128]{2,1,0:T(8,128)(2,1)S(1)}, u32[]{:S(2)}, u32[]{:S(2)}) %all-to-all-start) | async-done | bytes 131104 | tf_op jit(solution)/shard_map/all_to_all | solution.py:451
  38.2 0.0 collective-permute-done.3.other_ref
  38.2 1.2 scan.2
  39.4 4.1 %all-to-all-start.1 = ((bf16[16,32,128]{2,1,0:T(8,128)(2,1)}), bf16[16,32,128]{2,1,0:T(8,128)(2,1)S(1)}, u32[]{:S(2)}, u32[]{:S(2)}) async-start(bf16[16,32,128]{2,1,0:T(8,128)(2,1)} %scan.2), calls=%async_computation.1 | async-start | bytes 262144 | tf_op jit(solution)/shard_map/all_to_all | solution.py:451
  43.5 0.0 all-gather.3.cloned.1.call-start
  43.6 0.0 collective-permute-done.5.far_ref
  43.6 1.3 collective-permute-start.6
  44.9 0.0 copy-done.8
  44.9 0.0 copy-done
  44.9 3.2 %first_intra.1 = (f32[512,384]{1,0:T(8,128)S(1)}, bf16[512,384]{1,0:T(8,128)(2,1)S(1)}) custom-call(s32[2]{0:T(128)S(1)} %pad_add_fusion.place.refs_0_, bf16[256,768]{1,0:T(8,128)(2,1)S(1)} %copy-done, bf16[256,768]{1,0:T(8,128)(2,1)S(1)} %collective-permute-done.3.other_ref, bf16[512,384]{1,0:T(8,128)(2,1)} %get-tuple-element.43.ks, ...), custom_call_target="tpu_custom_call" | custom-call | tf_op jit(solution)/shard_map/first_intra/pallas_call | solution.py:40
  48.1 0.0 collective-permute-done.6.far_other_ref
  48.1 4.5 %all-to-all-done.1.refs_1_ = bf16[16,32,128]{2,1,0:T(8,128)(2,1)S(1)} async-done(((bf16[16,32,128]{2,1,0:T(8,128)(2,1)}), bf16[16,32,128]{2,1,0:T(8,128)(2,1)S(1)}, u32[]{:S(2)}, u32[]{:S(2)}) %all-to-all-start.1) | async-done | bytes 131104 | tf_op jit(solution)/shard_map/all_to_all | solution.py:451
  52.6 2.6 %pack.1 = (bf16[2,192,768]{2,1,0:T(8,128)(2,1)}, bf16[2,192,384]{2,1,0:T(8,128)(2,1)}) custom-call(s32[2]{0:T(128)S(1)} %pad_add_fusion.place.refs_0_, bf16[96,2304]{1,0:T(8,128)(2,1)S(1)} %get-tuple-element.56.near_ref, bf16[96,1152]{1,0:T(8,128)(2,1)} %copy-done.8, bf16[96,2304]{1,0:T(8,128)(2,1)S(1)} %collective-permute-done.5.far_ref, ...), custom_call_target="tpu_custom_call" | custom-call | tf_op jit(solution)/shard_map/pack/pallas_call | solution.py:40
  55.2 0.0 all-gather.3.cloned.1.call-update
  55.2 0.0 copy-done.5
  55.2 0.0 all-gather.5.cloned.1.call-start
  55.2 2.9 %finish.2 = (bf16[256,384]{1,0:T(8,128)(2,1)S(1)}, bf16[256,384]{1,0:T(8,128)(2,1)S(1)}, bf16[768,1536]{1,0:T(8,128)(2,1)S(1)}) custom-call(s32[2]{0:T(128)S(1)} %pad_add_fusion.place.refs_0_, bf16[16,32,128]{2,1,0:T(8,128)(2,1)S(1)} %all-to-all-done.1.refs_1_, f32[512,384]{1,0:T(8,128)S(1)} %get-tuple-element.51.refs_2_, ...), custom_call_target="tpu_custom_call" | custom-call | tf_op jit(solution)/shard_map/finish/pallas_call | solution.py:40
  58.2 2.4 %collective-permute-start.7 = (bf16[256,384]{1,0:T(8,128)(2,1)S(1)}, bf16[256,384]{1,0:T(8,128)(2,1)S(1)}, u32[]{:S(2)}, u32[]{:S(2)}) collective-permute-start(bf16[256,384]{1,0:T(8,128)(2,1)S(1)} %get-tuple-element.54), channel_id=1, source_target_pairs={{0,8},{8,0},{1,9},{9,1},{2,10},{10,2},{3,11},{11,3},{4,12},{12,4},... | collective-permute-start | bytes 589832 | tf_op jit(solution)/shard_map/ppermute | solution.py:461
  60.5 1.1 collective-permute-done.7.yours_ref
  61.6 3.2 %project.2 = bf16[8,256,384]{2,1,0:T(8,128)(2,1)S(1)} custom-call(s32[2]{0:T(128)S(1)} %pad_add_fusion.place.refs_0_, bf16[256,384]{1,0:T(8,128)(2,1)S(1)} %get-tuple-element.53.mine_ref, bf16[256,384]{1,0:T(8,128)(2,1)S(1)} %collective-permute-done.7.yours_ref, bf16[768,1536]{1,0:T(8,128)(2,1)S(1)} %get-tuple-element.55.near_ref, bf16[768,3072]{1,0:T(8,128)(2,1)} %w_ref.2), custom_call_target="tpu_custom_call" | custom-call | tf_op jit(solution)/shard_map/project/pallas_call | solution.py:40
  64.9 0.0 copy-start.9
  64.9 24.6 %all_to_all.35 = bf16[8,256,384]{2,1,0:T(8,128)(2,1)S(1)} all-to-all(bf16[8,256,384]{2,1,0:T(8,128)(2,1)S(1)} %project.2), channel_id=1, replica_groups=mesh['yh'=2,'z'=8,'c'=2,'x'=4,'yl'=2] {'x','yl'}, dimensions={0} | all-to-all | bytes 3145728 | tf_op jit(solution)/shard_map/all_to_all | solution.py:451
  89.5 0.2 convert_reduce_fusion.1
  89.8 0.0 copy-start.6
  89.8 0.0 all-gather.5.cloned.1.call-update
  89.8 0.6 copy-done.6
  90.4 0.1 broadcast_in_dim.2
  90.6 22.7 %all_to_all.36.h_ref.mine_ref = bf16[8,256,384]{2,1,0:T(8,128)(2,1)S(1)} all-to-all(bf16[8,256,384]{2,1,0:T(8,128)(2,1)S(1)} %broadcast_in_dim.2), channel_id=1, replica_groups=mesh['yh'=2,'z'=8,'c'=2,'x'=4,'yl'=2] {'x','yl'}, dimensions={0} | all-to-all | bytes 3145728 | tf_op jit(solution)/shard_map/all_to_all | solution.py:451
  113.3 2.8 %collective-permute-start.8 = (bf16[8,256,384]{2,1,0:T(8,128)(2,1)S(1)}, bf16[8,256,384]{2,1,0:T(8,128)(2,1)S(1)}, u32[]{:S(2)}, u32[]{:S(2)}) collective-permute-start(bf16[8,256,384]{2,1,0:T(8,128)(2,1)S(1)} %all_to_all.36.h_ref.mine_ref), channel_id=1, source_target_pairs={{0,8},{8,0},{1,9},{9,1},{2,10},{10,2},{3,11},{11,3},{4,12},{12,4},... | collective-permute-start | bytes 4718600 | tf_op jit(solution)/shard_map/ppermute | solution.py:507
  116.1 4.5 %own_kv.1 = (bf16[256,768]{1,0:T(8,128)(2,1)S(1)}, bf16[2,1536,768]{2,1,0:T(8,128)(2,1)S(1)}) custom-call(s32[2]{0:T(128)S(1)} %pad_add_fusion.place.refs_0_, bf16[8,256,384]{2,1,0:T(8,128)(2,1)S(1)} %all_to_all.36.h_ref.mine_ref, bf16[2,1536,768]{2,1,0:T(8,128)(2,1)} %all-gather.3.cloned.1.call-done.w_ref, f32[8,1,384]{2,1,0:T(1,128)S(1)} %bitcast.7), custom_call_target="tpu_custom_call" | custom-call | tf_op jit(solution)/shard_map/own_kv/pallas_call | solution.py:40
  120.6 0.0 collective-permute-done.8.h_ref.yours_ref
  120.6 4.7 %second_state.1 = (bf16[16,32,128]{2,1,0:T(8,128)(2,1)S(1)}, bf16[512,384]{1,0:T(8,128)(2,1)}, bf16[512,384]{1,0:T(8,128)(2,1)}) custom-call(s32[2]{0:T(128)S(1)} %pad_add_fusion.place.refs_0_, bf16[8,256,384]{2,1,0:T(8,128)(2,1)S(1)} %collective-permute-done.8.h_ref.yours_ref, bf16[2,1536,768]{2,1,0:T(8,128)(2,1)S(1)} %get-tuple-element.61.w_ref, ...), custom_call_target="tpu_custom_call" | custom-call | tf_op jit(solution)/shard_map/second_state/pallas_call | solution.py:40
  125.3 13.8 %all_to_all.37.in_ref = bf16[16,32,128]{2,1,0:T(8,128)(2,1)S(1)} all-to-all(bf16[16,32,128]{2,1,0:T(8,128)(2,1)S(1)} %get-tuple-element.63), channel_id=1, replica_groups=mesh['yh'=2,'z'=8,'c'=2,'x'=4,'yl'=2] {'yh','z'}, dimensions={0} | all-to-all | bytes 262144 | tf_op jit(solution)/shard_map/all_to_all | solution.py:451
  139.2 1.2 scan.3
  140.4 4.6 %all-to-all-start.5 = ((bf16[16,32,128]{2,1,0:T(8,128)(2,1)}), bf16[16,32,128]{2,1,0:T(8,128)(2,1)S(1)}, u32[]{:S(2)}, u32[]{:S(2)}) async-start(bf16[16,32,128]{2,1,0:T(8,128)(2,1)} %scan.3), calls=%async_computation.5 | async-start | bytes 262144 | tf_op jit(solution)/shard_map/all_to_all | solution.py:451
  145.0 11.5 %all-gather.5.cloned.1.call-done.w_ref = bf16[2,1536,384]{2,1,0:T(8,128)(2,1)} async-done(((bf16[2,192,384]{2,1,0:T(8,128)(2,1)}), bf16[2,1536,384]{2,1,0:T(8,128)(2,1)}) %all-gather.5.cloned.1.call-update) | async-done | bytes 2359312 | tf_op jit(solution)/shard_map/all_gather | solution.py:499
  156.6 8.2 %second_intra.1 = (f32[512,384]{1,0:T(8,128)}, bf16[512,384]{1,0:T(8,128)(2,1)}) custom-call(s32[2]{0:T(128)S(1)} %pad_add_fusion.place.refs_0_, bf16[8,256,384]{2,1,0:T(8,128)(2,1)S(1)} %all_to_all.36.h_ref.mine_ref, bf16[8,256,384]{2,1,0:T(8,128)(2,1)S(1)} %collective-permute-done.8.h_ref.yours_ref, ...), custom_call_target="tpu_custom_call" | custom-call | tf_op jit(solution)/shard_map/second_intra/pallas_call | solution.py:40
  164.7 0.0 all-to-all-done.5.refs_1_
  164.7 3.5 %finish.3 = (bf16[256,384]{1,0:T(8,128)(2,1)S(1)}, bf16[256,384]{1,0:T(8,128)(2,1)S(1)}, bf16[768,1536]{1,0:T(8,128)(2,1)S(1)}) custom-call(s32[2]{0:T(128)S(1)} %pad_add_fusion.place.refs_0_, bf16[16,32,128]{2,1,0:T(8,128)(2,1)S(1)} %all-to-all-done.5.refs_1_, f32[512,384]{1,0:T(8,128)} %get-tuple-element.68.refs_2_, ...), custom_call_target="tpu_custom_call" | custom-call | tf_op jit(solution)/shard_map/finish/pallas_call | solution.py:40
  168.2 3.4 %collective-permute-start.9 = (bf16[256,384]{1,0:T(8,128)(2,1)S(1)}, bf16[256,384]{1,0:T(8,128)(2,1)S(1)}, u32[]{:S(2)}, u32[]{:S(2)}) collective-permute-start(bf16[256,384]{1,0:T(8,128)(2,1)S(1)} %get-tuple-element.71), channel_id=1, source_target_pairs={{0,8},{8,0},{1,9},{9,1},{2,10},{10,2},{3,11},{11,3},{4,12},{12,4},... | collective-permute-start | bytes 589832 | tf_op jit(solution)/shard_map/ppermute | solution.py:461
  171.7 1.1 collective-permute-done.9.yours_ref
  172.7 3.2 %project.3 = bf16[8,256,384]{2,1,0:T(8,128)(2,1)S(1)} custom-call(s32[2]{0:T(128)S(1)} %pad_add_fusion.place.refs_0_, bf16[256,384]{1,0:T(8,128)(2,1)S(1)} %get-tuple-element.70.mine_ref, bf16[256,384]{1,0:T(8,128)(2,1)S(1)} %collective-permute-done.9.yours_ref, bf16[768,1536]{1,0:T(8,128)(2,1)S(1)} %get-tuple-element.72.near_ref, bf16[768,3072]{1,0:T(8,128)(2,1)} %w_ref.3), custom_call_target="tpu_custom_call" | custom-call | tf_op jit(solution)/shard_map/project/pallas_call | solution.py:40
  176.0 0.0 copy-start.7
  176.0 23.7 %all_to_all.38 = bf16[8,256,384]{2,1,0:T(8,128)(2,1)S(1)} all-to-all(bf16[8,256,384]{2,1,0:T(8,128)(2,1)S(1)} %project.3), channel_id=1, replica_groups=mesh['yh'=2,'z'=8,'c'=2,'x'=4,'yl'=2] {'x','yl'}, dimensions={0} | all-to-all | bytes 3145728 | tf_op jit(solution)/shard_map/all_to_all | solution.py:451
  199.7 0.2 convert_reduce_fusion
  199.9 0.7 add_convert_fusion
  (13 shorter events, 0.1 us)
Async XLA Ops:
  6.5 38.4 %copy-start = (bf16[256,768]{1,0:T(8,128)(2,1)S(1)}, bf16[256,768]{1,0:T(8,128)(2,1)}, u32[]{:S(2)}) copy-start(bf16[256,768]{1,0:T(8,128)(2,1)} %q_ref.2) | copy-start | bytes 1179652
  6.5 10.3 %collective-permute-start = (bf16[256,768]{1,0:T(8,128)(2,1)}, bf16[256,768]{1,0:T(8,128)(2,1)S(1)}, u32[]{:S(2)}, u32[]{:S(2)}) collective-permute-start(bf16[256,768]{1,0:T(8,128)(2,1)} %k_ref.2), channel_id=1, source_target_pairs={{0,8},{8,0},{1,9},{9,1},{2,10},{10,2},{3,11},{11,3},{4,12},{12,4},... | collective-permute-start | bytes 1179656 | tf_op jit(solution)/shard_map/ppermute | solution.py:473
  9.8 7.0 %collective-permute-start.1 = (bf16[256,768]{1,0:T(8,128)(2,1)}, bf16[256,768]{1,0:T(8,128)(2,1)S(1)}, u32[]{:S(2)}, u32[]{:S(2)}) collective-permute-start(bf16[256,768]{1,0:T(8,128)(2,1)} %v_ref.2), channel_id=1, source_target_pairs={{0,8},{8,0},{1,9},{9,1},{2,10},{10,2},{3,11},{11,3},{4,12},{12,4},... | collective-permute-start | bytes 1179656 | tf_op jit(solution)/shard_map/ppermute | solution.py:473
  9.9 0.9 copy-start.1
  10.8 0.9 copy-start.2
  11.7 0.9 copy-start.3
  13.2 30.4 %collective-permute-start.5 = (bf16[96,2304]{1,0:T(8,128)(2,1)S(1)}, bf16[96,2304]{1,0:T(8,128)(2,1)S(1)}, u32[]{:S(2)}, u32[]{:S(2)}) collective-permute-start(bf16[96,2304]{1,0:T(8,128)(2,1)S(1)} %get-tuple-element.56.near_ref), channel_id=1, source_target_pairs={{0,128},{128,0},{1,129},{129,1},{2,130},{130,2},{3,131},{131,3},{4... | collective-permute-start | bytes 1327112 | tf_op jit(solution)/shard_map/ppermute | solution.py:482
  15.2 1.6 collective-permute-start.2
  20.6 34.6 %copy-start.5 = (f32[8,512]{1,0:T(8,128)}, f32[8,512]{1,0:T(8,128)S(1)}, u32[]{:S(2)}) copy-start(f32[8,512]{1,0:T(8,128)S(1)} %get-tuple-element.46.across_ref) | copy-start | bytes 49156
  20.6 17.6 %collective-permute-start.3 = (bf16[256,768]{1,0:T(8,128)(2,1)}, bf16[256,768]{1,0:T(8,128)(2,1)S(1)}, u32[]{:S(2)}, u32[]{:S(2)}) collective-permute-start(bf16[256,768]{1,0:T(8,128)(2,1)} %q_ref.2), channel_id=1, source_target_pairs={{0,8},{8,0},{1,9},{9,1},{2,10},{10,2},{3,11},{11,3},{4,12},{12,4},... | collective-permute-start | bytes 1179656 | tf_op jit(solution)/shard_map/ppermute | solution.py:473
  20.9 17.2 %all-to-all-start = ((bf16[16,32,128]{2,1,0:T(8,128)(2,1)}), bf16[16,32,128]{2,1,0:T(8,128)(2,1)S(1)}, u32[]{:S(2)}, u32[]{:S(2)}) async-start(bf16[16,32,128]{2,1,0:T(8,128)(2,1)} %get-tuple-element.39), calls=%async_computation | async-start | bytes 262144 | tf_op jit(solution)/shard_map/all_to_all | solution.py:451
  29.2 1.6 collective-permute-start.4
  30.9 14.1 %copy-start.8 = (bf16[96,1152]{1,0:T(8,128)(2,1)}, bf16[96,1152]{1,0:T(8,128)(2,1)S(1)}, u32[]{:S(2)}) copy-start(bf16[96,1152]{1,0:T(8,128)(2,1)S(1)} %collective-permute-done.4.near_other_ref) | copy-start | bytes 663556
  39.4 13.2 %all-to-all-start.1 = ((bf16[16,32,128]{2,1,0:T(8,128)(2,1)}), bf16[16,32,128]{2,1,0:T(8,128)(2,1)S(1)}, u32[]{:S(2)}, u32[]{:S(2)}) async-start(bf16[16,32,128]{2,1,0:T(8,128)(2,1)} %scan.2), calls=%async_computation.1 | async-start | bytes 262144 | tf_op jit(solution)/shard_map/all_to_all | solution.py:451
  43.5 72.5 %all-gather.3.cloned.1.call-start = ((), (), s32[]{:S(2)}) async-start(), calls=%async_computation.7 | async-start | bytes 5308416 | tf_op jit(solution)/shard_map/all_gather | solution.py:499
  43.6 4.5 %collective-permute-start.6 = (bf16[96,1152]{1,0:T(8,128)(2,1)S(1)}, bf16[96,1152]{1,0:T(8,128)(2,1)}, u32[]{:S(2)}, u32[]{:S(2)}) collective-permute-start(bf16[96,1152]{1,0:T(8,128)(2,1)S(1)} %slice.3), channel_id=1, source_target_pairs={{0,8},{8,0},{1,9},{9,1},{2,10},{10,2},{3,11},{11,3},{4,12},{12,4},... | collective-permute-start | bytes 663560 | tf_op jit(solution)/shard_map/ppermute | solution.py:473
  55.2 101.4 %all-gather.5.cloned.1.call-start = ((), (), s32[]{:S(2)}) async-start(), calls=%async_computation.8 | async-start | bytes 2654208 | tf_op jit(solution)/shard_map/all_gather | solution.py:499
  58.2 3.4 %collective-permute-start.7 = (bf16[256,384]{1,0:T(8,128)(2,1)S(1)}, bf16[256,384]{1,0:T(8,128)(2,1)S(1)}, u32[]{:S(2)}, u32[]{:S(2)}) collective-permute-start(bf16[256,384]{1,0:T(8,128)(2,1)S(1)} %get-tuple-element.54), channel_id=1, source_target_pairs={{0,8},{8,0},{1,9},{9,1},{2,10},{10,2},{3,11},{11,3},{4,12},{12,4},... | collective-permute-start | bytes 589832 | tf_op jit(solution)/shard_map/ppermute | solution.py:461
  64.9 24.8 %copy-start.9 = (bf16[256,384]{1,0:T(8,128)(2,1)S(1)}, bf16[256,384]{1,0:T(8,128)(2,1)}, u32[]{:S(2)}) copy-start(bf16[256,384]{1,0:T(8,128)(2,1)} %param.20) | copy-start | bytes 589828
  89.8 0.7 copy-start.6
  90.4 25.6 %copy-start.4 = (f32[3072]{0:T(1024)S(1)}, f32[3072]{0:T(1024)}, u32[]{:S(2)}) copy-start(f32[3072]{0:T(1024)} %param.21) | copy-start | bytes 36868
  113.3 7.3 %collective-permute-start.8 = (bf16[8,256,384]{2,1,0:T(8,128)(2,1)S(1)}, bf16[8,256,384]{2,1,0:T(8,128)(2,1)S(1)}, u32[]{:S(2)}, u32[]{:S(2)}) collective-permute-start(bf16[8,256,384]{2,1,0:T(8,128)(2,1)S(1)} %all_to_all.36.h_ref.mine_ref), channel_id=1, source_target_pairs={{0,8},{8,0},{1,9},{9,1},{2,10},{10,2},{3,11},{11,3},{4,12},{12,4},... | collective-permute-start | bytes 4718600 | tf_op jit(solution)/shard_map/ppermute | solution.py:507
  140.4 24.3 %all-to-all-start.5 = ((bf16[16,32,128]{2,1,0:T(8,128)(2,1)}), bf16[16,32,128]{2,1,0:T(8,128)(2,1)S(1)}, u32[]{:S(2)}, u32[]{:S(2)}) async-start(bf16[16,32,128]{2,1,0:T(8,128)(2,1)} %scan.3), calls=%async_computation.5 | async-start | bytes 262144 | tf_op jit(solution)/shard_map/all_to_all | solution.py:451
  168.2 4.5 %collective-permute-start.9 = (bf16[256,384]{1,0:T(8,128)(2,1)S(1)}, bf16[256,384]{1,0:T(8,128)(2,1)S(1)}, u32[]{:S(2)}, u32[]{:S(2)}) collective-permute-start(bf16[256,384]{1,0:T(8,128)(2,1)S(1)} %get-tuple-element.71), channel_id=1, source_target_pairs={{0,8},{8,0},{1,9},{9,1},{2,10},{10,2},{3,11},{11,3},{4,12},{12,4},... | collective-permute-start | bytes 589832 | tf_op jit(solution)/shard_map/ppermute | solution.py:461
  176.0 24.0 %copy-start.7 = (bf16[256,384]{1,0:T(8,128)(2,1)S(1)}, bf16[256,384]{1,0:T(8,128)(2,1)}, u32[]{:S(2)}) copy-start(bf16[256,384]{1,0:T(8,128)(2,1)} %copy-done.6) | copy-start | bytes 589828
Sparse Core Ops, SparseCore 0:
  55.3 57.0 all-gather.2
  114.2 42.3 all-gather.4

commit v5 on v3

--- a/solution.py
+++ b/solution.py
@@ -306,7 +306,7 @@
     hs, ws, gs = projection_specs(HW)
     return call(
         second_intra_kernel, "second_intra", place,
-        (mine, yours, in_hbm(w), gain, in_hbm(ks), in_hbm(vs), cum, across),
+        (mine, yours, in_hbm(w), gain, in_hbm(ks), in_hbm(vs), cum, in_hbm(across)),
         (pltpu.HBM((TOK, HW), F32), HEADS_OUT),
         grid=(STEPS,),
         in_specs=[hs, hs, ws, gs] + [whole(a.shape) for a in (ks, vs, cum, across)],
@@ -314,21 +314,35 @@
     )
 
 
-def pack_kernel(place, own_ref, other_ref, far_ref, far_other_ref, kv_ref, q_ref):
-    core = place[0]
-    rows = own_ref.shape[0]
-    for n, pair in enumerate(((own_ref, other_ref), (far_ref, far_other_ref))):
+def cut_kernel(place, k_ref, v_ref, q_ref, both_ref, give_ref):
+    core = place[0]
+    for n, src in enumerate((k_ref, v_ref, q_ref)):
+        both_ref[:, n * HW : (n + 1) * HW] = src[:, span(core, HW)]
+        give = src[:, span(1 - core, HW)]
+        both_ref[:, (n + 3) * HW : (n + 4) * HW] = give
+        give_ref[:, n * HW : (n + 1) * HW] = give
+
+
+def cut(place, *weights):
+    rows = weights[0].shape[0]
+    outs = (struct((rows, 6 * HW), BF16), struct((rows, 3 * HW), BF16))
+    return call(cut_kernel, "cut", place, [in_hbm(w) for w in weights], outs)
+
+
+def pack_kernel(place, near_ref, near_other_ref, far_ref, far_other_ref, kv_ref, wq_ref):
+    core = place[0]
+    rows = near_ref.shape[0]
+    for n, pair in enumerate(((near_ref, near_other_ref), (far_ref, far_other_ref))):
         for src, owner in zip(pair, (core, 1 - core)):
             at = pl.ds(pl.multiple_of(owner * rows, rows), rows)
-            for i in range(2):
-                kv_ref[n, at, i * HW : (i + 1) * HW] = src[:, span(2 * i + core, HW)]
-            q_ref[n, at, :] = src[:, span(4 + core, HW)]
-
-
-def pack(place, *args):
-    rows = 2 * args[0].shape[0]
-    outs = (struct((2, rows, 2 * HW), BF16), struct((2, rows, HW), BF16))
-    return call(pack_kernel, "pack", place, args, outs)
+            kv_ref[n, at, :] = src[:, : 2 * HW]
+            wq_ref[n, at, :] = src[:, 2 * HW : 3 * HW]
+
+
+def pack(place, *parts):
+    rows = 2 * parts[0].shape[0]
+    outs = (pltpu.HBM((2, rows, 2 * HW), BF16), pltpu.HBM((2, rows, HW), BF16))
+    return call(pack_kernel, "pack", place, parts, outs)
 
 
 def scan_kernel(place, in_ref, out_ref):
@@ -420,7 +434,7 @@
 
 
 def rest(place, layer, before, intra, cum, qs, gain, w):
-    mine, yours, w = finish(place, layer, before, intra, cum, qs, gain.reshape(2 * HC, DH), w)
+    mine, yours, w = finish(place, layer, before, intra, cum, qs, in_hbm(gain.reshape(2 * HC, DH)), w)
     yours = lax.ppermute(yours, "c", SWAP)
     terms = exchange(project(place, mine, yours, w), ("x", "yl"))
     return jnp.sum(terms.astype(F32), axis=0)
@@ -441,22 +455,21 @@
         place, in_hbm(k1), other_k, in_hbm(v1), other_v, decays, other_decays
     )
 
-    w_cat = jnp.concatenate([wk2, wv2, wq2], axis=1)
-    far = lax.ppermute(w_cat, "yh", SWAP)
-    other_w, = swapped(w_cat)
+    near, give = cut(place, wk2, wv2, wq2)
+    far = lax.ppermute(near, "yh", SWAP)
+    far = after(far, pieces)
+    near_other, far_other = swapped(give, far[:, 3 * HW :])
+    rows_kv, rows_q = pack(place, near, near_other, far, far_other)
     q1 = after(q1, pieces)
     other_q, = swapped(q1)
-    sums = after(exchange(pieces, ("yh", "z")), other_q)
-    scanned = scan(place, sums)
-    far = after(far, scanned)
-    far_other, = swapped(far)
-    rows_kv, rows_q = pack(place, w_cat, other_w, far, far_other)
-    before = exchange(scanned, ("yh", "z"))
+    sums, _, rows_kv, rows_q = lax.optimization_barrier(
+        (exchange(pieces, ("yh", "z")), other_q, rows_kv, rows_q)
+    )
+    before = exchange(scan(place, sums), ("yh", "z"))
 
     def gather(rows):
         return lax.all_gather(rows, "z", axis=1, tiled=True)
 
-    ks, rows_kv, rows_q = lax.optimization_barrier((ks, rows_kv, rows_q))
     wkv = gather(rows_kv)
     intra, qs = first_intra(place, q1, other_q, ks, vs, cum, across)
     first_share = rest(place, 0, before, intra, cum, qs, gain_out1, wo1)

time: 196 us -> 193 us (0.985)
  local copies, waits for them, and re-layouts: 5.62 us -> 1.48 us
  Pallas kernels: 40.1 us -> 42.5 us
    unnamed x22 -> x14, local copies, waits for them, and re-layouts: 4.56 us -> 1.32 us
    all_to_all x3, waiting for transfers between devices: 14.1 us -> 11.7 us  [exchange(): return lax.all_to_all(parts, axes, 0, 0)]
    pallas_call x12 -> x13, Pallas kernels: 40.1 us -> 42.5 us  [call(): pl.pallas_call(kernel, out_shape=outs, grid_spec=pltpu.PrefetchScalarGrid...]
  transfers between devices with their start and end apart: 15 -> 15, of which waited for: 6 -> 8; matrix products, arithmetic and copies ran while one was open for 2% -> 1% of each run, Pallas kernels for 16% -> 19%
where the time goes in v5:
time: 193 us; the launch traced here: 192 us
  blocking collectives  85.4 us (44%)
  Pallas kernels  42.5 us (22%)
  starting transfers between devices  30.6 us (16%)
  waiting for transfers between devices  16.2 us (8%)
  between operations  13.6 us (7%)
  other arithmetic  2 us (1%)
    all_to_all x4, blocking collectives, exchange(): return lax.all_to_all(parts, axes, 0, 0)  85.4 us
    pallas_call x13, Pallas kernels, call(): pl.pallas_call(kernel, out_shape=outs, grid_spec=pltpu.PrefetchScalarGrid...  42.5 us
    all_to_all x3, starting transfers between devices, exchange(): return lax.all_to_all(parts, axes, 0, 0)  16.8 us
    all_to_all x3, waiting for transfers between devices, exchange(): return lax.all_to_all(parts, axes, 0, 0)  11.7 us
    ppermute x6, starting transfers between devices, swapped(): return [lax.ppermute(a, 'c', SWAP) for a in arrays]  5.13 us
    ppermute x2, starting transfers between devices, rest(): yours = lax.ppermute(yours, 'c', SWAP)  4.55 us
  transfers between devices with their start and end apart: 15, of which 8 were waited for; matrix products, arithmetic and copies ran while one was open for 1% of the time, Pallas kernels for 19%

profile of v5, /device:TPU:1, one launch (start us, length us, event | category | flops | bytes accessed | tf_op | source)
XLA Modules:
  0.0 191.8 jit_solution(17925962376989240307)
XLA Ops:
  6.5 3.2 %collective-permute-start = (bf16[256,768]{1,0:T(8,128)(2,1)}, bf16[256,768]{1,0:T(8,128)(2,1)S(1)}, u32[]{:S(2)}, u32[]{:S(2)}) collective-permute-start(bf16[256,768]{1,0:T(8,128)(2,1)} %k_ref.2), channel_id=1, source_target_pairs={{0,8},{8,0},{1,9},{9,1},{2,10},{10,2},{3,11},{11,3},{4,12},{12,4},... | collective-permute-start | bytes 1179656 | tf_op jit(solution)/shard_map/ppermute | solution.py:450
  9.8 0.0 collective-permute-start.1
  9.8 0.1 pad_add_fusion.place.refs_0_
  9.9 1.6 cut.1
  11.5 1.3 collective-permute-start.5
  12.8 0.7 pad_maximum_fusion.decay_ref
  13.5 0.9 collective-permute-start.2
  14.4 0.8 collective-permute-done.2.other_decay_ref
  15.2 0.0 collective-permute-done.other_k_ref
  15.2 0.0 collective-permute-done.1.other_v_ref
  15.2 3.9 %first_state.1 = (bf16[16,32,128]{2,1,0:T(8,128)(2,1)}, bf16[512,384]{1,0:T(8,128)(2,1)}, bf16[512,384]{1,0:T(8,128)(2,1)}, f32[512,128]{1,0:T(8,128)S(1)}, f32[8,512]{1,0:T(8,128)S(1)}) custom-call(s32[2]{0:T(128)S(1)} %pad_add_fusion.place.refs_0_, bf16[256,768]{1,0:T(8,128)(2,1)} %k_ref.2, bf16[256,768]{1,0:T(8,128)(2,1)S(1)} %collective-permute-done.other_k_ref, ...), custom_call_target="tpu_custom_call" | custom-call | tf_op jit(solution)/shard_map/first_state/pallas_call | solution.py:40
  19.1 0.3 collective-permute-start.3
  19.4 8.3 %all-to-all-start = ((bf16[16,32,128]{2,1,0:T(8,128)(2,1)}), bf16[16,32,128]{2,1,0:T(8,128)(2,1)S(1)}, u32[]{:S(2)}, u32[]{:S(2)}) async-start(bf16[16,32,128]{2,1,0:T(8,128)(2,1)} %get-tuple-element.35), calls=%async_computation | async-start | bytes 262144 | tf_op jit(solution)/shard_map/all_to_all | solution.py:429
  27.7 0.0 all-gather.3.cloned.1.call-start
  27.7 0.5 collective-permute-start.4
  28.3 0.0 collective-permute-done.5.far_ref
  28.3 0.1 collective-permute-start.6
  28.5 0.9 collective-permute-done.4.near_other_ref
  29.4 0.5 collective-permute-done.6.far_other_ref
  29.9 1.6 pack.1
  31.4 5.2 %all-to-all-done.in_ref = bf16[16,32,128]{2,1,0:T(8,128)(2,1)S(1)} async-done(((bf16[16,32,128]{2,1,0:T(8,128)(2,1)}), bf16[16,32,128]{2,1,0:T(8,128)(2,1)S(1)}, u32[]{:S(2)}, u32[]{:S(2)}) %all-to-all-start) | async-done | bytes 131104 | tf_op jit(solution)/shard_map/all_to_all | solution.py:429
  36.6 0.0 collective-permute-done.3.other_ref
  36.6 0.0 all-gather.3.cloned.1.call-update
  36.7 1.2 scan.2
  37.9 4.2 %all-to-all-start.1 = ((bf16[16,32,128]{2,1,0:T(8,128)(2,1)}), bf16[16,32,128]{2,1,0:T(8,128)(2,1)S(1)}, u32[]{:S(2)}, u32[]{:S(2)}) async-start(bf16[16,32,128]{2,1,0:T(8,128)(2,1)} %scan.2), calls=%async_computation.1 | async-start | bytes 262144 | tf_op jit(solution)/shard_map/all_to_all | solution.py:429
  42.1 0.0 all-gather.5.cloned.1.call-start
  42.1 0.0 copy-done.1
  42.1 3.2 %first_intra.1 = (f32[512,384]{1,0:T(8,128)S(1)}, bf16[512,384]{1,0:T(8,128)(2,1)S(1)}) custom-call(s32[2]{0:T(128)S(1)} %pad_add_fusion.place.refs_0_, bf16[256,768]{1,0:T(8,128)(2,1)S(1)} %copy-done.1, bf16[256,768]{1,0:T(8,128)(2,1)S(1)} %collective-permute-done.3.other_ref, bf16[512,384]{1,0:T(8,128)(2,1)} %get-tuple-element.43.ks, ...), custom_call_target="tpu_custom_call" | custom-call | tf_op jit(solution)/shard_map/first_intra/pallas_call | solution.py:40
  45.3 0.0 copy-done.3
  45.3 5.8 %all-to-all-done.1.refs_1_ = bf16[16,32,128]{2,1,0:T(8,128)(2,1)S(1)} async-done(((bf16[16,32,128]{2,1,0:T(8,128)(2,1)}), bf16[16,32,128]{2,1,0:T(8,128)(2,1)S(1)}, u32[]{:S(2)}, u32[]{:S(2)}) %all-to-all-start.1) | async-done | bytes 131104 | tf_op jit(solution)/shard_map/all_to_all | solution.py:429
  51.1 3.6 %finish.2 = (bf16[256,384]{1,0:T(8,128)(2,1)S(1)}, bf16[256,384]{1,0:T(8,128)(2,1)S(1)}, bf16[768,3072]{1,0:T(8,128)(2,1)S(1)}) custom-call(s32[2]{0:T(128)S(1)} %pad_add_fusion.place.refs_0_, bf16[16,32,128]{2,1,0:T(8,128)(2,1)S(1)} %all-to-all-done.1.refs_1_, f32[512,384]{1,0:T(8,128)S(1)} %get-tuple-element.47.refs_2_, ...), custom_call_target="tpu_custom_call" | custom-call | tf_op jit(solution)/shard_map/finish/pallas_call | solution.py:40
  54.7 2.3 %collective-permute-start.7 = (bf16[256,384]{1,0:T(8,128)(2,1)S(1)}, bf16[256,384]{1,0:T(8,128)(2,1)S(1)}, u32[]{:S(2)}, u32[]{:S(2)}) collective-permute-start(bf16[256,384]{1,0:T(8,128)(2,1)S(1)} %get-tuple-element.50), channel_id=1, source_target_pairs={{0,8},{8,0},{1,9},{9,1},{2,10},{10,2},{3,11},{11,3},{4,12},{12,4},... | collective-permute-start | bytes 589832 | tf_op jit(solution)/shard_map/ppermute | solution.py:438
  57.1 1.1 collective-permute-done.7.yours_ref
  58.1 2.6 %project.2 = bf16[8,256,384]{2,1,0:T(8,128)(2,1)S(1)} custom-call(s32[2]{0:T(128)S(1)} %pad_add_fusion.place.refs_0_, bf16[256,384]{1,0:T(8,128)(2,1)S(1)} %get-tuple-element.49.mine_ref, bf16[256,384]{1,0:T(8,128)(2,1)S(1)} %collective-permute-done.7.yours_ref, bf16[768,3072]{1,0:T(8,128)(2,1)S(1)} %get-tuple-element.51.w_ref), custom_call_target="tpu_custom_call" | custom-call | flops 1207959552 | tf_op jit(solution)/shard_map/project/pallas_call | solution.py:40
  60.7 0.0 copy-start.6
  60.8 25.0 %all_to_all.35 = bf16[8,256,384]{2,1,0:T(8,128)(2,1)S(1)} all-to-all(bf16[8,256,384]{2,1,0:T(8,128)(2,1)S(1)} %project.2), channel_id=1, replica_groups=mesh['yh'=2,'z'=8,'c'=2,'x'=4,'yl'=2] {'x','yl'}, dimensions={0} | all-to-all | bytes 3145728 | tf_op jit(solution)/shard_map/all_to_all | solution.py:429
  85.8 0.2 convert_reduce_fusion.1
  86.0 0.0 copy-done.6
  86.1 0.0 copy-start.4
  86.1 0.0 all-gather.5.cloned.1.call-update
  86.1 0.6 copy-done.4
  86.8 0.1 broadcast_in_dim.2
  86.9 22.7 %all_to_all.36.h_ref.mine_ref = bf16[8,256,384]{2,1,0:T(8,128)(2,1)S(1)} all-to-all(bf16[8,256,384]{2,1,0:T(8,128)(2,1)S(1)} %broadcast_in_dim.2), channel_id=1, replica_groups=mesh['yh'=2,'z'=8,'c'=2,'x'=4,'yl'=2] {'x','yl'}, dimensions={0} | all-to-all | bytes 3145728 | tf_op jit(solution)/shard_map/all_to_all | solution.py:429
  109.6 2.8 %collective-permute-start.8 = (bf16[8,256,384]{2,1,0:T(8,128)(2,1)S(1)}, bf16[8,256,384]{2,1,0:T(8,128)(2,1)S(1)}, u32[]{:S(2)}, u32[]{:S(2)}) collective-permute-start(bf16[8,256,384]{2,1,0:T(8,128)(2,1)S(1)} %all_to_all.36.h_ref.mine_ref), channel_id=1, source_target_pairs={{0,8},{8,0},{1,9},{9,1},{2,10},{10,2},{3,11},{11,3},{4,12},{12,4},... | collective-permute-start | bytes 4718600 | tf_op jit(solution)/shard_map/ppermute | solution.py:480
  112.4 0.0 copy-done.2
  112.4 4.5 %own_kv.1 = (bf16[256,768]{1,0:T(8,128)(2,1)S(1)}, bf16[2,1536,768]{2,1,0:T(8,128)(2,1)S(1)}) custom-call(s32[2]{0:T(128)S(1)} %pad_add_fusion.place.refs_0_, bf16[8,256,384]{2,1,0:T(8,128)(2,1)S(1)} %all_to_all.36.h_ref.mine_ref, bf16[2,1536,768]{2,1,0:T(8,128)(2,1)} %all-gather.3.cloned.1.call-done.w_ref, f32[8,1,384]{2,1,0:T(1,128)S(1)} %bitcast.7), custom_call_target="tpu_custom_call" | custom-call | tf_op jit(solution)/shard_map/own_kv/pallas_call | solution.py:40
  116.9 0.0 collective-permute-done.8.h_ref.yours_ref
  116.9 4.7 %second_state.1 = (bf16[16,32,128]{2,1,0:T(8,128)(2,1)S(1)}, bf16[512,384]{1,0:T(8,128)(2,1)}, bf16[512,384]{1,0:T(8,128)(2,1)}) custom-call(s32[2]{0:T(128)S(1)} %pad_add_fusion.place.refs_0_, bf16[8,256,384]{2,1,0:T(8,128)(2,1)S(1)} %collective-permute-done.8.h_ref.yours_ref, bf16[2,1536,768]{2,1,0:T(8,128)(2,1)S(1)} %get-tuple-element.53.w_ref, ...), custom_call_target="tpu_custom_call" | custom-call | tf_op jit(solution)/shard_map/second_state/pallas_call | solution.py:40
  121.7 14.8 %all_to_all.37.in_ref = bf16[16,32,128]{2,1,0:T(8,128)(2,1)S(1)} all-to-all(bf16[16,32,128]{2,1,0:T(8,128)(2,1)S(1)} %get-tuple-element.55), channel_id=1, replica_groups=mesh['yh'=2,'z'=8,'c'=2,'x'=4,'yl'=2] {'yh','z'}, dimensions={0} | all-to-all | bytes 262144 | tf_op jit(solution)/shard_map/all_to_all | solution.py:429
  136.5 0.6 scan.3
  137.1 0.0 copy-start
  137.1 0.6 copy-done
  137.7 4.4 %all-to-all-start.5 = ((bf16[16,32,128]{2,1,0:T(8,128)(2,1)}), bf16[16,32,128]{2,1,0:T(8,128)(2,1)S(1)}, u32[]{:S(2)}, u32[]{:S(2)}) async-start(bf16[16,32,128]{2,1,0:T(8,128)(2,1)} %copy-done), calls=%async_computation.5 | async-start | bytes 262144 | tf_op jit(solution)/shard_map/all_to_all | solution.py:429
  142.1 0.0 all-gather.5.cloned.1.call-done.w_ref
  142.1 8.2 %second_intra.1 = (f32[512,384]{1,0:T(8,128)}, bf16[512,384]{1,0:T(8,128)(2,1)}) custom-call(s32[2]{0:T(128)S(1)} %pad_add_fusion.place.refs_0_, bf16[8,256,384]{2,1,0:T(8,128)(2,1)S(1)} %all_to_all.36.h_ref.mine_ref, bf16[8,256,384]{2,1,0:T(8,128)(2,1)S(1)} %collective-permute-done.8.h_ref.yours_ref, ...), custom_call_target="tpu_custom_call" | custom-call | tf_op jit(solution)/shard_map/second_intra/pallas_call | solution.py:40
  150.3 0.7 all-to-all-done.5.refs_1_
  151.0 4.2 %finish.3 = (bf16[256,384]{1,0:T(8,128)(2,1)S(1)}, bf16[256,384]{1,0:T(8,128)(2,1)S(1)}, bf16[768,3072]{1,0:T(8,128)(2,1)S(1)}) custom-call(s32[2]{0:T(128)S(1)} %pad_add_fusion.place.refs_0_, bf16[16,32,128]{2,1,0:T(8,128)(2,1)S(1)} %all-to-all-done.5.refs_1_, f32[512,384]{1,0:T(8,128)} %get-tuple-element.60.refs_2_, ...), custom_call_target="tpu_custom_call" | custom-call | tf_op jit(solution)/shard_map/finish/pallas_call | solution.py:40
  155.2 2.2 %collective-permute-start.9 = (bf16[256,384]{1,0:T(8,128)(2,1)S(1)}, bf16[256,384]{1,0:T(8,128)(2,1)S(1)}, u32[]{:S(2)}, u32[]{:S(2)}) collective-permute-start(bf16[256,384]{1,0:T(8,128)(2,1)S(1)} %get-tuple-element.63), channel_id=1, source_target_pairs={{0,8},{8,0},{1,9},{9,1},{2,10},{10,2},{3,11},{11,3},{4,12},{12,4},... | collective-permute-start | bytes 589832 | tf_op jit(solution)/shard_map/ppermute | solution.py:438
  157.4 1.1 collective-permute-done.9.yours_ref
  158.5 2.6 %project.3 = bf16[8,256,384]{2,1,0:T(8,128)(2,1)S(1)} custom-call(s32[2]{0:T(128)S(1)} %pad_add_fusion.place.refs_0_, bf16[256,384]{1,0:T(8,128)(2,1)S(1)} %get-tuple-element.62.mine_ref, bf16[256,384]{1,0:T(8,128)(2,1)S(1)} %collective-permute-done.9.yours_ref, bf16[768,3072]{1,0:T(8,128)(2,1)S(1)} %get-tuple-element.64.w_ref), custom_call_target="tpu_custom_call" | custom-call | flops 1207959552 | tf_op jit(solution)/shard_map/project/pallas_call | solution.py:40
  161.1 0.0 copy-start.5
  161.1 22.9 %all_to_all.38 = bf16[8,256,384]{2,1,0:T(8,128)(2,1)S(1)} all-to-all(bf16[8,256,384]{2,1,0:T(8,128)(2,1)S(1)} %project.3), channel_id=1, replica_groups=mesh['yh'=2,'z'=8,'c'=2,'x'=4,'yl'=2] {'x','yl'}, dimensions={0} | all-to-all | bytes 3145728 | tf_op jit(solution)/shard_map/all_to_all | solution.py:429
  184.0 0.2 convert_reduce_fusion
  184.2 0.7 add_convert_fusion
  (7 shorter events, 0.1 us)
Async XLA Ops:
  6.5 8.7 %collective-permute-start = (bf16[256,768]{1,0:T(8,128)(2,1)}, bf16[256,768]{1,0:T(8,128)(2,1)S(1)}, u32[]{:S(2)}, u32[]{:S(2)}) collective-permute-start(bf16[256,768]{1,0:T(8,128)(2,1)} %k_ref.2), channel_id=1, source_target_pairs={{0,8},{8,0},{1,9},{9,1},{2,10},{10,2},{3,11},{11,3},{4,12},{12,4},... | collective-permute-start | bytes 1179656 | tf_op jit(solution)/shard_map/ppermute | solution.py:450
  9.8 5.4 %collective-permute-start.1 = (bf16[256,768]{1,0:T(8,128)(2,1)}, bf16[256,768]{1,0:T(8,128)(2,1)S(1)}, u32[]{:S(2)}, u32[]{:S(2)}) collective-permute-start(bf16[256,768]{1,0:T(8,128)(2,1)} %v_ref.2), channel_id=1, source_target_pairs={{0,8},{8,0},{1,9},{9,1},{2,10},{10,2},{3,11},{11,3},{4,12},{12,4},... | collective-permute-start | bytes 1179656 | tf_op jit(solution)/shard_map/ppermute | solution.py:450
  11.5 16.8 %collective-permute-start.5 = (bf16[96,2304]{1,0:T(8,128)(2,1)S(1)}, bf16[96,2304]{1,0:T(8,128)(2,1)S(1)}, u32[]{:S(2)}, u32[]{:S(2)}) collective-permute-start(bf16[96,2304]{1,0:T(8,128)(2,1)S(1)} %get-tuple-element.37.near_ref), channel_id=1, source_target_pairs={{0,128},{128,0},{1,129},{129,1},{2,130},{130,2},{3,131},{131,3},{4... | collective-permute-start | bytes 1327112 | tf_op jit(solution)/shard_map/ppermute | solution.py:459
  13.5 28.6 %copy-start.1 = (bf16[256,768]{1,0:T(8,128)(2,1)S(1)}, bf16[256,768]{1,0:T(8,128)(2,1)}, u32[]{:S(2)}) copy-start(bf16[256,768]{1,0:T(8,128)(2,1)} %q_ref.2) | copy-start | bytes 1179652
  13.5 1.7 collective-permute-start.2
  19.1 26.2 %copy-start.3 = (f32[8,512]{1,0:T(8,128)}, f32[8,512]{1,0:T(8,128)S(1)}, u32[]{:S(2)}) copy-start(f32[8,512]{1,0:T(8,128)S(1)} %get-tuple-element.46.across_ref) | copy-start | bytes 49156
  19.1 17.6 %collective-permute-start.3 = (bf16[256,768]{1,0:T(8,128)(2,1)}, bf16[256,768]{1,0:T(8,128)(2,1)S(1)}, u32[]{:S(2)}, u32[]{:S(2)}) collective-permute-start(bf16[256,768]{1,0:T(8,128)(2,1)} %q_ref.2), channel_id=1, source_target_pairs={{0,8},{8,0},{1,9},{9,1},{2,10},{10,2},{3,11},{11,3},{4,12},{12,4},... | collective-permute-start | bytes 1179656 | tf_op jit(solution)/shard_map/ppermute | solution.py:450
  19.4 17.2 %all-to-all-start = ((bf16[16,32,128]{2,1,0:T(8,128)(2,1)}), bf16[16,32,128]{2,1,0:T(8,128)(2,1)S(1)}, u32[]{:S(2)}, u32[]{:S(2)}) async-start(bf16[16,32,128]{2,1,0:T(8,128)(2,1)} %get-tuple-element.35), calls=%async_computation | async-start | bytes 262144 | tf_op jit(solution)/shard_map/all_to_all | solution.py:429
  27.7 84.7 %all-gather.3.cloned.1.call-start = ((), (), s32[]{:S(2)}) async-start(), calls=%async_computation.7 | async-start | bytes 5308416 | tf_op jit(solution)/shard_map/all_gather | solution.py:471
  27.7 1.6 collective-permute-start.4
  28.3 1.6 collective-permute-start.6
  37.9 13.2 %all-to-all-start.1 = ((bf16[16,32,128]{2,1,0:T(8,128)(2,1)}), bf16[16,32,128]{2,1,0:T(8,128)(2,1)S(1)}, u32[]{:S(2)}, u32[]{:S(2)}) async-start(bf16[16,32,128]{2,1,0:T(8,128)(2,1)} %scan.2), calls=%async_computation.1 | async-start | bytes 262144 | tf_op jit(solution)/shard_map/all_to_all | solution.py:429
  42.1 100.0 %all-gather.5.cloned.1.call-start = ((), (), s32[]{:S(2)}) async-start(), calls=%async_computation.8 | async-start | bytes 2654208 | tf_op jit(solution)/shard_map/all_gather | solution.py:471
  54.7 3.4 %collective-permute-start.7 = (bf16[256,384]{1,0:T(8,128)(2,1)S(1)}, bf16[256,384]{1,0:T(8,128)(2,1)S(1)}, u32[]{:S(2)}, u32[]{:S(2)}) collective-permute-start(bf16[256,384]{1,0:T(8,128)(2,1)S(1)} %get-tuple-element.50), channel_id=1, source_target_pairs={{0,8},{8,0},{1,9},{9,1},{2,10},{10,2},{3,11},{11,3},{4,12},{12,4},... | collective-permute-start | bytes 589832 | tf_op jit(solution)/shard_map/ppermute | solution.py:438
  60.7 25.3 %copy-start.6 = (bf16[256,384]{1,0:T(8,128)(2,1)S(1)}, bf16[256,384]{1,0:T(8,128)(2,1)}, u32[]{:S(2)}) copy-start(bf16[256,384]{1,0:T(8,128)(2,1)} %param.20) | copy-start | bytes 589828
  86.1 0.7 copy-start.4
  86.8 25.6 %copy-start.2 = (f32[3072]{0:T(1024)S(1)}, f32[3072]{0:T(1024)}, u32[]{:S(2)}) copy-start(f32[3072]{0:T(1024)} %param.21) | copy-start | bytes 36868
  109.6 7.3 %collective-permute-start.8 = (bf16[8,256,384]{2,1,0:T(8,128)(2,1)S(1)}, bf16[8,256,384]{2,1,0:T(8,128)(2,1)S(1)}, u32[]{:S(2)}, u32[]{:S(2)}) collective-permute-start(bf16[8,256,384]{2,1,0:T(8,128)(2,1)S(1)} %all_to_all.36.h_ref.mine_ref), channel_id=1, source_target_pairs={{0,8},{8,0},{1,9},{9,1},{2,10},{10,2},{3,11},{11,3},{4,12},{12,4},... | collective-permute-start | bytes 4718600 | tf_op jit(solution)/shard_map/ppermute | solution.py:480
  137.1 0.7 copy-start
  137.7 13.3 %all-to-all-start.5 = ((bf16[16,32,128]{2,1,0:T(8,128)(2,1)}), bf16[16,32,128]{2,1,0:T(8,128)(2,1)S(1)}, u32[]{:S(2)}, u32[]{:S(2)}) async-start(bf16[16,32,128]{2,1,0:T(8,128)(2,1)} %copy-done), calls=%async_computation.5 | async-start | bytes 262144 | tf_op jit(solution)/shard_map/all_to_all | solution.py:429
  155.2 3.3 %collective-permute-start.9 = (bf16[256,384]{1,0:T(8,128)(2,1)S(1)}, bf16[256,384]{1,0:T(8,128)(2,1)S(1)}, u32[]{:S(2)}, u32[]{:S(2)}) collective-permute-start(bf16[256,384]{1,0:T(8,128)(2,1)S(1)} %get-tuple-element.63), channel_id=1, source_target_pairs={{0,8},{8,0},{1,9},{9,1},{2,10},{10,2},{3,11},{11,3},{4,12},{12,4},... | collective-permute-start | bytes 589832 | tf_op jit(solution)/shard_map/ppermute | solution.py:438
  161.1 23.1 %copy-start.5 = (bf16[256,384]{1,0:T(8,128)(2,1)S(1)}, bf16[256,384]{1,0:T(8,128)(2,1)}, u32[]{:S(2)}) copy-start(bf16[256,384]{1,0:T(8,128)(2,1)} %copy-done.4) | copy-start | bytes 589828
Sparse Core Ops, SparseCore 0:
  36.8 57.7 all-gather.2
  96.4 39.9 all-gather.4

commit v6 on v5

--- a/solution.py
+++ b/solution.py
@@ -67,8 +67,15 @@
     rows[: 4 * HC, span(1 - core, BLK)] = yours_ref[...]
     before = lax.broadcasted_iota(jnp.int32, (TOK, TOK), 0)
     after = lax.broadcasted_iota(jnp.int32, (TOK, TOK), 1)
-    upper = (before <= after).astype(F32)
-    sums = jnp.dot(rows[...], upper, preferred_element_type=F32, precision=lax.Precision.HIGHEST)
+    upper = (before <= after).astype(BF16)
+    left = rows[...]
+    parts = []
+    for _ in range(3):
+        part = left.astype(BF16)
+        parts.append(part)
+        left = left - part.astype(F32)
+    sums = jnp.dot(jnp.concatenate(parts, axis=0), upper, preferred_element_type=F32)
+    sums = sums[:16] + (sums[16:32] + sums[32:])
     first = jnp.where(core == 0, sums[0:HC], sums[HC : 2 * HC])
     second = jnp.where(core == 0, sums[2 * HC : 3 * HC], sums[3 * HC : 4 * HC])
     across = jnp.concatenate([first, second, jnp.zeros((2, TOK), F32)], axis=0)
@@ -168,8 +175,7 @@
     return call(first_intra_kernel, "first_intra", place, args, (INTRA_OUT, QUERY_OUT))
 
 
-def project_step(h_ref, w, gain_ref, acc, square, rows):
-    step = pl.program_id(0)
+def gained(h_ref, gain_ref):
     parts = []
     total = None
     for i in range(2):
@@ -178,19 +184,25 @@
         for n in range(WIDTH // DH):
             tile = wide[:, n * DH : (n + 1) * DH]
             total = tile * tile if total is None else total + tile * tile
-    part = jnp.concatenate(parts, axis=1)
+    return jnp.concatenate(parts, axis=1), total
+
+
+def project_step(h_refs, w, gain_ref, acc, square):
+    step = pl.program_id(0)
+    parts, totals = zip(*(gained(h_ref, gain_ref) for h_ref in h_refs))
+    part, total = jnp.concatenate(parts, axis=0), jnp.concatenate(totals, axis=0)
 
     term = jnp.dot(part, w, preferred_element_type=F32)
 
     @pl.when(step == 0)
     def _():
-        square[rows, :] = total
-        acc[rows, :] = term
+        square[...] = total
+        acc[...] = term
 
     @pl.when(step > 0)
     def _():
-        square[rows, :] += total
-        acc[rows, :] += term
+        square[...] += total
+        acc[...] += term
 
 
 def row_scale(square):
@@ -239,7 +251,7 @@
         def _(n=n):
             fetch(n).wait()
 
-    project_step(h_ref, weight_rows(held)[...], gain_ref, acc, square, slice(0, BLK))
+    project_step([h_ref], weight_rows(held)[...], gain_ref, acc, square)
 
     @pl.when(step == STEPS - 1)
     def _():
@@ -263,7 +275,7 @@
     place, h_ref, w_ref, gain_ref, own_ref, cum_ref, pieces_ref, ks, vs, acc, square
 ):
     core = place[0]
-    project_step(h_ref, weight_rows(w_ref)[...], gain_ref, acc, square, slice(0, BLK))
+    project_step([h_ref], weight_rows(w_ref)[...], gain_ref, acc, square)
 
     @pl.when(pl.program_id(0) == STEPS - 1)
     def _():
@@ -290,9 +302,7 @@
     intra_ref, qs, acc, square,
 ):
     core = place[0]
-    for n, src in enumerate((mine_ref, yours_ref)):
-        rows = slice(n * BLK, (n + 1) * BLK)
-        project_step(src, w_ref[0], gain_ref, acc, square, rows)
+    project_step([mine_ref, yours_ref], w_ref[0], gain_ref, acc, square)
 
     @pl.when(pl.program_id(0) == STEPS - 1)
     def _():
@@ -362,37 +372,46 @@
 
 
 def finish_kernel(
-    layer, place, pieces_ref, intra_ref, cum_ref, qs_ref, gain_ref, wo_ref,
-    mine_ref, yours_ref, held, out, sem,
+    layer, place, pieces_ref, cum_ref, intra_hbm, qs_hbm, gain_hbm, wo_ref,
+    mine_ref, yours_ref, held, out, intra_ref, qs_ref, gain_ref, sems,
 ):
     core = place[0]
-    fetch = pltpu.make_async_copy(wo_ref, held, sem)
-    fetch.start()
+    pairs = ((intra_hbm, intra_ref), (qs_hbm, qs_ref), (gain_hbm, gain_ref), (wo_ref, held))
+    fetches = [pltpu.make_async_copy(a, b, sems.at[n]) for n, (a, b) in enumerate(pairs)]
+    for fetch in fetches:
+        fetch.start()
     pieces = pieces_ref[...].astype(F32)
+    states = [
+        pieces[:, h * SUB : (h + 1) * SUB].reshape(DH, DH).astype(BF16) for h in range(HC)
+    ]
+    scales = [jnp.exp(cum_ref[:, layer * HC + h : layer * HC + h + 1]) for h in range(HC)]
+    for fetch in fetches[:3]:
+        fetch.wait()
     for h in range(HC):
         cols = slice(h * DH, (h + 1) * DH)
-        lane = layer * HC + h
-        state = pieces[:, h * SUB : (h + 1) * SUB].reshape(DH, DH).astype(BF16)
-        carried = jnp.dot(qs_ref[:, cols], state, preferred_element_type=F32)
-        att = intra_ref[:, cols] + carried * jnp.exp(cum_ref[:, lane : lane + 1])
+        carried = jnp.dot(qs_ref[:, cols], states[h], preferred_element_type=F32)
+        att = intra_ref[:, cols] + carried * scales[h]
         square = jnp.mean(att * att, axis=-1, keepdims=True)
         gain = gain_ref[pl.ds(core * HC + h, 1), :]
         out[:, cols] = (att * lax.rsqrt(square + 1e-06) * gain).astype(BF16)
     mine_ref[...] = out[span(core, BLK), :]
     yours_ref[...] = out[span(1 - core, BLK), :]
-    fetch.wait()
+    fetches[3].wait()
 
 
 def finish(place, layer, pieces, intra, cum, qs, gain, wo):
     if layer:
         intra, qs = in_hbm(intra), in_hbm(qs)
-    args = (pieces, intra, cum, qs, gain)
     return call(
-        lambda *refs: finish_kernel(layer, *refs), "finish", place, (*args, in_hbm(wo)),
+        lambda *refs: finish_kernel(layer, *refs), "finish", place,
+        (pieces, cum, intra, qs, gain, in_hbm(wo)),
         (struct((BLK, HW), BF16), struct((BLK, HW), BF16), WO_OUT),
-        in_specs=[whole(a.shape) for a in args] + [ANY],
+        in_specs=[whole(pieces.shape), whole(cum.shape)] + [ANY] * 4,
         out_specs=[whole((BLK, HW)), whole((BLK, HW)), IN_VMEM],
-        scratch=(pltpu.VMEM((TOK, HW), BF16), pltpu.SemaphoreType.DMA),
+        scratch=(
+            pltpu.VMEM((TOK, HW), BF16), pltpu.VMEM((TOK, HW), F32), pltpu.VMEM((TOK, HW), BF16),
+            pltpu.VMEM((2 * HC, DH), F32), pltpu.SemaphoreType.DMA((4,)),
+        ),
     )
 
 

time: 193 us -> 191 us (0.990)
  Pallas kernels: 42.5 us -> 40.4 us
    pallas_call x13, Pallas kernels: 42.5 us -> 40.4 us  [call(): pl.pallas_call(kernel, out_shape=outs, grid_spec=pltpu.PrefetchScalarGrid...]
  transfers between devices with their start and end apart: 15 -> 15, of which waited for: 8 -> 8; matrix products, arithmetic and copies ran while one was open for 1% -> 1% of each run, Pallas kernels for 19% -> 18%
where the time goes in v6:
time: 191 us; the launch traced here: 190 us
  blocking collectives  85.3 us (45%)
  Pallas kernels  40.4 us (21%)
  starting transfers between devices  31 us (16%)
  waiting for transfers between devices  16.7 us (9%)
  between operations  13.6 us (7%)
  other arithmetic  2 us (1%)
    all_to_all x4, blocking collectives, exchange(): return lax.all_to_all(parts, axes, 0, 0)  85.3 us
    pallas_call x13, Pallas kernels, call(): pl.pallas_call(kernel, out_shape=outs, grid_spec=pltpu.PrefetchScalarGrid...  40.4 us
    all_to_all x3, starting transfers between devices, exchange(): return lax.all_to_all(parts, axes, 0, 0)  17.3 us
    all_to_all x3, waiting for transfers between devices, exchange(): return lax.all_to_all(parts, axes, 0, 0)  12.2 us
    ppermute x6, starting transfers between devices, swapped(): return [lax.ppermute(a, 'c', SWAP) for a in arrays]  5.13 us
    ppermute x2, starting transfers between devices, rest(): yours = lax.ppermute(yours, 'c', SWAP)  4.42 us
  transfers between devices with their start and end apart: 15, of which 8 were waited for; matrix products, arithmetic and copies ran while one was open for 1% of the time, Pallas kernels for 18%

profile of v6, /device:TPU:1, one launch (start us, length us, event | category | flops | bytes accessed | tf_op | source)
XLA Modules:
  0.0 190.5 jit_solution(17152040938482400249)
XLA Ops:
  6.5 3.2 %collective-permute-start = (bf16[256,768]{1,0:T(8,128)(2,1)}, bf16[256,768]{1,0:T(8,128)(2,1)S(1)}, u32[]{:S(2)}, u32[]{:S(2)}) collective-permute-start(bf16[256,768]{1,0:T(8,128)(2,1)} %k_ref.2), channel_id=1, source_target_pairs={{0,8},{8,0},{1,9},{9,1},{2,10},{10,2},{3,11},{11,3},{4,12},{12,4},... | collective-permute-start | bytes 1179656 | tf_op jit(solution)/shard_map/ppermute | solution.py:469
  9.8 0.0 collective-permute-start.1
  9.8 0.1 pad_add_fusion.place.refs_0_
  9.9 1.6 cut.1
  11.5 1.3 collective-permute-start.5
  12.8 0.7 pad_maximum_fusion.decay_ref
  13.5 0.9 collective-permute-start.2
  14.4 0.8 collective-permute-done.2.other_decay_ref
  15.2 0.0 collective-permute-done.other_k_ref
  15.2 0.0 collective-permute-done.1.other_v_ref
  15.2 3.6 %first_state.1 = (bf16[16,32,128]{2,1,0:T(8,128)(2,1)}, bf16[512,384]{1,0:T(8,128)(2,1)}, bf16[512,384]{1,0:T(8,128)(2,1)}, f32[512,128]{1,0:T(8,128)S(1)}, f32[8,512]{1,0:T(8,128)S(1)}) custom-call(s32[2]{0:T(128)S(1)} %pad_add_fusion.place.refs_0_, bf16[256,768]{1,0:T(8,128)(2,1)} %k_ref.2, bf16[256,768]{1,0:T(8,128)(2,1)S(1)} %collective-permute-done.other_k_ref, ...), custom_call_target="tpu_custom_call" | custom-call | tf_op jit(solution)/shard_map/first_state/pallas_call | solution.py:40
  18.8 0.3 collective-permute-start.3
  19.1 8.3 %all-to-all-start = ((bf16[16,32,128]{2,1,0:T(8,128)(2,1)}), bf16[16,32,128]{2,1,0:T(8,128)(2,1)S(1)}, u32[]{:S(2)}, u32[]{:S(2)}) async-start(bf16[16,32,128]{2,1,0:T(8,128)(2,1)} %get-tuple-element.35), calls=%async_computation | async-start | bytes 262144 | tf_op jit(solution)/shard_map/all_to_all | solution.py:448
  27.4 0.0 all-gather.3.cloned.1.call-start
  27.5 0.5 collective-permute-start.4
  28.0 0.0 collective-permute-done.5.far_ref
  28.0 0.1 collective-permute-start.6
  28.2 0.9 collective-permute-done.4.near_other_ref
  29.1 0.5 collective-permute-done.6.far_other_ref
  29.6 1.6 pack.1
  31.2 5.2 %all-to-all-done.in_ref = bf16[16,32,128]{2,1,0:T(8,128)(2,1)S(1)} async-done(((bf16[16,32,128]{2,1,0:T(8,128)(2,1)}), bf16[16,32,128]{2,1,0:T(8,128)(2,1)S(1)}, u32[]{:S(2)}, u32[]{:S(2)}) %all-to-all-start) | async-done | bytes 131104 | tf_op jit(solution)/shard_map/all_to_all | solution.py:448
  36.3 0.0 collective-permute-done.3.other_ref
  36.3 0.0 all-gather.3.cloned.1.call-update
  36.4 1.2 scan.2
  37.6 4.2 %all-to-all-start.1 = ((bf16[16,32,128]{2,1,0:T(8,128)(2,1)}), bf16[16,32,128]{2,1,0:T(8,128)(2,1)S(1)}, u32[]{:S(2)}, u32[]{:S(2)}) async-start(bf16[16,32,128]{2,1,0:T(8,128)(2,1)} %scan.2), calls=%async_computation.1 | async-start | bytes 262144 | tf_op jit(solution)/shard_map/all_to_all | solution.py:448
  41.8 0.0 all-gather.5.cloned.1.call-start
  41.8 0.0 copy-done.1
  41.8 3.2 %first_intra.1 = (f32[512,384]{1,0:T(8,128)S(1)}, bf16[512,384]{1,0:T(8,128)(2,1)S(1)}) custom-call(s32[2]{0:T(128)S(1)} %pad_add_fusion.place.refs_0_, bf16[256,768]{1,0:T(8,128)(2,1)S(1)} %copy-done.1, bf16[256,768]{1,0:T(8,128)(2,1)S(1)} %collective-permute-done.3.other_ref, bf16[512,384]{1,0:T(8,128)(2,1)} %get-tuple-element.44.ks, ...), custom_call_target="tpu_custom_call" | custom-call | tf_op jit(solution)/shard_map/first_intra/pallas_call | solution.py:40
  45.0 0.0 copy-done.3
  45.0 5.8 %all-to-all-done.1.refs_1_ = bf16[16,32,128]{2,1,0:T(8,128)(2,1)S(1)} async-done(((bf16[16,32,128]{2,1,0:T(8,128)(2,1)}), bf16[16,32,128]{2,1,0:T(8,128)(2,1)S(1)}, u32[]{:S(2)}, u32[]{:S(2)}) %all-to-all-start.1) | async-done | bytes 131104 | tf_op jit(solution)/shard_map/all_to_all | solution.py:448
  50.8 3.2 %finish.2 = (bf16[256,384]{1,0:T(8,128)(2,1)S(1)}, bf16[256,384]{1,0:T(8,128)(2,1)S(1)}, bf16[768,3072]{1,0:T(8,128)(2,1)S(1)}) custom-call(s32[2]{0:T(128)S(1)} %pad_add_fusion.place.refs_0_, bf16[16,32,128]{2,1,0:T(8,128)(2,1)S(1)} %all-to-all-done.1.refs_1_, f32[512,128]{1,0:T(8,128)S(1)} %get-tuple-element.43.cum_ref.refs_2_, ...), custom_call_target="tpu_custom_call" | custom-call | tf_op jit(solution)/shard_map/finish/pallas_call | solution.py:40
  54.0 2.3 %collective-permute-start.7 = (bf16[256,384]{1,0:T(8,128)(2,1)S(1)}, bf16[256,384]{1,0:T(8,128)(2,1)S(1)}, u32[]{:S(2)}, u32[]{:S(2)}) collective-permute-start(bf16[256,384]{1,0:T(8,128)(2,1)S(1)} %get-tuple-element.50), channel_id=1, source_target_pairs={{0,8},{8,0},{1,9},{9,1},{2,10},{10,2},{3,11},{11,3},{4,12},{12,4},... | collective-permute-start | bytes 589832 | tf_op jit(solution)/shard_map/ppermute | solution.py:457
  56.3 1.1 collective-permute-done.7.yours_ref
  57.4 2.6 %project.2 = bf16[8,256,384]{2,1,0:T(8,128)(2,1)S(1)} custom-call(s32[2]{0:T(128)S(1)} %pad_add_fusion.place.refs_0_, bf16[256,384]{1,0:T(8,128)(2,1)S(1)} %get-tuple-element.49.mine_ref, bf16[256,384]{1,0:T(8,128)(2,1)S(1)} %collective-permute-done.7.yours_ref, bf16[768,3072]{1,0:T(8,128)(2,1)S(1)} %get-tuple-element.51.w_ref), custom_call_target="tpu_custom_call" | custom-call | flops 1207959552 | tf_op jit(solution)/shard_map/project/pallas_call | solution.py:40
  60.0 0.0 copy-start.6
  60.1 25.0 %all_to_all.35 = bf16[8,256,384]{2,1,0:T(8,128)(2,1)S(1)} all-to-all(bf16[8,256,384]{2,1,0:T(8,128)(2,1)S(1)} %project.2), channel_id=1, replica_groups=mesh['yh'=2,'z'=8,'c'=2,'x'=4,'yl'=2] {'x','yl'}, dimensions={0} | all-to-all | bytes 3145728 | tf_op jit(solution)/shard_map/all_to_all | solution.py:448
  85.1 0.2 convert_reduce_fusion.1
  85.3 0.0 copy-done.6
  85.4 0.0 copy-start.4
  85.4 0.0 all-gather.5.cloned.1.call-update
  85.4 0.6 copy-done.4
  86.0 0.1 broadcast_in_dim.2
  86.2 22.7 %all_to_all.36.h_ref.mine_ref = bf16[8,256,384]{2,1,0:T(8,128)(2,1)S(1)} all-to-all(bf16[8,256,384]{2,1,0:T(8,128)(2,1)S(1)} %broadcast_in_dim.2), channel_id=1, replica_groups=mesh['yh'=2,'z'=8,'c'=2,'x'=4,'yl'=2] {'x','yl'}, dimensions={0} | all-to-all | bytes 3145728 | tf_op jit(solution)/shard_map/all_to_all | solution.py:448
  108.9 2.8 %collective-permute-start.8 = (bf16[8,256,384]{2,1,0:T(8,128)(2,1)S(1)}, bf16[8,256,384]{2,1,0:T(8,128)(2,1)S(1)}, u32[]{:S(2)}, u32[]{:S(2)}) collective-permute-start(bf16[8,256,384]{2,1,0:T(8,128)(2,1)S(1)} %all_to_all.36.h_ref.mine_ref), channel_id=1, source_target_pairs={{0,8},{8,0},{1,9},{9,1},{2,10},{10,2},{3,11},{11,3},{4,12},{12,4},... | collective-permute-start | bytes 4718600 | tf_op jit(solution)/shard_map/ppermute | solution.py:499
  111.6 0.0 copy-done.2
  111.7 4.6 %own_kv.1 = (bf16[256,768]{1,0:T(8,128)(2,1)S(1)}, bf16[2,1536,768]{2,1,0:T(8,128)(2,1)S(1)}) custom-call(s32[2]{0:T(128)S(1)} %pad_add_fusion.place.refs_0_, bf16[8,256,384]{2,1,0:T(8,128)(2,1)S(1)} %all_to_all.36.h_ref.mine_ref, bf16[2,1536,768]{2,1,0:T(8,128)(2,1)} %all-gather.3.cloned.1.call-done.w_ref, f32[8,1,384]{2,1,0:T(1,128)S(1)} %bitcast.7), custom_call_target="tpu_custom_call" | custom-call | tf_op jit(solution)/shard_map/own_kv/pallas_call | solution.py:40
  116.2 0.0 collective-permute-done.8.h_ref.yours_ref
  116.2 4.7 %second_state.1 = (bf16[16,32,128]{2,1,0:T(8,128)(2,1)S(1)}, bf16[512,384]{1,0:T(8,128)(2,1)}, bf16[512,384]{1,0:T(8,128)(2,1)}) custom-call(s32[2]{0:T(128)S(1)} %pad_add_fusion.place.refs_0_, bf16[8,256,384]{2,1,0:T(8,128)(2,1)S(1)} %collective-permute-done.8.h_ref.yours_ref, bf16[2,1536,768]{2,1,0:T(8,128)(2,1)S(1)} %get-tuple-element.53.w_ref, ...), custom_call_target="tpu_custom_call" | custom-call | tf_op jit(solution)/shard_map/second_state/pallas_call | solution.py:40
  121.0 14.5 %all_to_all.37.in_ref = bf16[16,32,128]{2,1,0:T(8,128)(2,1)S(1)} all-to-all(bf16[16,32,128]{2,1,0:T(8,128)(2,1)S(1)} %get-tuple-element.55), channel_id=1, replica_groups=mesh['yh'=2,'z'=8,'c'=2,'x'=4,'yl'=2] {'yh','z'}, dimensions={0} | all-to-all | bytes 262144 | tf_op jit(solution)/shard_map/all_to_all | solution.py:448
  135.4 0.6 scan.3
  136.0 0.0 copy-start
  136.0 0.6 copy-done
  136.7 4.8 %all-to-all-start.5 = ((bf16[16,32,128]{2,1,0:T(8,128)(2,1)}), bf16[16,32,128]{2,1,0:T(8,128)(2,1)S(1)}, u32[]{:S(2)}, u32[]{:S(2)}) async-start(bf16[16,32,128]{2,1,0:T(8,128)(2,1)} %copy-done), calls=%async_computation.5 | async-start | bytes 262144 | tf_op jit(solution)/shard_map/all_to_all | solution.py:448
  141.5 0.0 all-gather.5.cloned.1.call-done.w_ref
  141.6 7.7 %second_intra.1 = (f32[512,384]{1,0:T(8,128)}, bf16[512,384]{1,0:T(8,128)(2,1)}) custom-call(s32[2]{0:T(128)S(1)} %pad_add_fusion.place.refs_0_, bf16[8,256,384]{2,1,0:T(8,128)(2,1)S(1)} %all_to_all.36.h_ref.mine_ref, bf16[8,256,384]{2,1,0:T(8,128)(2,1)S(1)} %collective-permute-done.8.h_ref.yours_ref, ...), custom_call_target="tpu_custom_call" | custom-call | tf_op jit(solution)/shard_map/second_intra/pallas_call | solution.py:40
  149.2 1.2 all-to-all-done.5.refs_1_
  150.5 3.3 %finish.3 = (bf16[256,384]{1,0:T(8,128)(2,1)S(1)}, bf16[256,384]{1,0:T(8,128)(2,1)S(1)}, bf16[768,3072]{1,0:T(8,128)(2,1)S(1)}) custom-call(s32[2]{0:T(128)S(1)} %pad_add_fusion.place.refs_0_, bf16[16,32,128]{2,1,0:T(8,128)(2,1)S(1)} %all-to-all-done.5.refs_1_, f32[512,128]{1,0:T(8,128)S(1)} %get-tuple-element.43.cum_ref.refs_2_, ...), custom_call_target="tpu_custom_call" | custom-call | tf_op jit(solution)/shard_map/finish/pallas_call | solution.py:40
  153.8 2.1 %collective-permute-start.9 = (bf16[256,384]{1,0:T(8,128)(2,1)S(1)}, bf16[256,384]{1,0:T(8,128)(2,1)S(1)}, u32[]{:S(2)}, u32[]{:S(2)}) collective-permute-start(bf16[256,384]{1,0:T(8,128)(2,1)S(1)} %get-tuple-element.63), channel_id=1, source_target_pairs={{0,8},{8,0},{1,9},{9,1},{2,10},{10,2},{3,11},{11,3},{4,12},{12,4},... | collective-permute-start | bytes 589832 | tf_op jit(solution)/shard_map/ppermute | solution.py:457
  155.9 1.1 collective-permute-done.9.yours_ref
  156.9 2.6 %project.3 = bf16[8,256,384]{2,1,0:T(8,128)(2,1)S(1)} custom-call(s32[2]{0:T(128)S(1)} %pad_add_fusion.place.refs_0_, bf16[256,384]{1,0:T(8,128)(2,1)S(1)} %get-tuple-element.62.mine_ref, bf16[256,384]{1,0:T(8,128)(2,1)S(1)} %collective-permute-done.9.yours_ref, bf16[768,3072]{1,0:T(8,128)(2,1)S(1)} %get-tuple-element.64.w_ref), custom_call_target="tpu_custom_call" | custom-call | flops 1207959552 | tf_op jit(solution)/shard_map/project/pallas_call | solution.py:40
  159.5 0.0 copy-start.5
  159.6 23.1 %all_to_all.38 = bf16[8,256,384]{2,1,0:T(8,128)(2,1)S(1)} all-to-all(bf16[8,256,384]{2,1,0:T(8,128)(2,1)S(1)} %project.3), channel_id=1, replica_groups=mesh['yh'=2,'z'=8,'c'=2,'x'=4,'yl'=2] {'x','yl'}, dimensions={0} | all-to-all | bytes 3145728 | tf_op jit(solution)/shard_map/all_to_all | solution.py:448
  182.7 0.2 convert_reduce_fusion
  182.9 0.7 add_convert_fusion
  (7 shorter events, 0.1 us)
Async XLA Ops:
  6.5 8.7 %collective-permute-start = (bf16[256,768]{1,0:T(8,128)(2,1)}, bf16[256,768]{1,0:T(8,128)(2,1)S(1)}, u32[]{:S(2)}, u32[]{:S(2)}) collective-permute-start(bf16[256,768]{1,0:T(8,128)(2,1)} %k_ref.2), channel_id=1, source_target_pairs={{0,8},{8,0},{1,9},{9,1},{2,10},{10,2},{3,11},{11,3},{4,12},{12,4},... | collective-permute-start | bytes 1179656 | tf_op jit(solution)/shard_map/ppermute | solution.py:469
  9.8 5.4 %collective-permute-start.1 = (bf16[256,768]{1,0:T(8,128)(2,1)}, bf16[256,768]{1,0:T(8,128)(2,1)S(1)}, u32[]{:S(2)}, u32[]{:S(2)}) collective-permute-start(bf16[256,768]{1,0:T(8,128)(2,1)} %v_ref.2), channel_id=1, source_target_pairs={{0,8},{8,0},{1,9},{9,1},{2,10},{10,2},{3,11},{11,3},{4,12},{12,4},... | collective-permute-start | bytes 1179656 | tf_op jit(solution)/shard_map/ppermute | solution.py:469
  11.5 16.5 %collective-permute-start.5 = (bf16[96,2304]{1,0:T(8,128)(2,1)S(1)}, bf16[96,2304]{1,0:T(8,128)(2,1)S(1)}, u32[]{:S(2)}, u32[]{:S(2)}) collective-permute-start(bf16[96,2304]{1,0:T(8,128)(2,1)S(1)} %get-tuple-element.37.near_ref), channel_id=1, source_target_pairs={{0,128},{128,0},{1,129},{129,1},{2,130},{130,2},{3,131},{131,3},{4... | collective-permute-start | bytes 1327112 | tf_op jit(solution)/shard_map/ppermute | solution.py:478
  13.5 28.3 %copy-start.1 = (bf16[256,768]{1,0:T(8,128)(2,1)S(1)}, bf16[256,768]{1,0:T(8,128)(2,1)}, u32[]{:S(2)}) copy-start(bf16[256,768]{1,0:T(8,128)(2,1)} %q_ref.2) | copy-start | bytes 1179652
  13.5 1.7 collective-permute-start.2
  18.8 26.2 %copy-start.3 = (f32[8,512]{1,0:T(8,128)}, f32[8,512]{1,0:T(8,128)S(1)}, u32[]{:S(2)}) copy-start(f32[8,512]{1,0:T(8,128)S(1)} %get-tuple-element.46.across_ref) | copy-start | bytes 49156
  18.8 17.6 %collective-permute-start.3 = (bf16[256,768]{1,0:T(8,128)(2,1)}, bf16[256,768]{1,0:T(8,128)(2,1)S(1)}, u32[]{:S(2)}, u32[]{:S(2)}) collective-permute-start(bf16[256,768]{1,0:T(8,128)(2,1)} %q_ref.2), channel_id=1, source_target_pairs={{0,8},{8,0},{1,9},{9,1},{2,10},{10,2},{3,11},{11,3},{4,12},{12,4},... | collective-permute-start | bytes 1179656 | tf_op jit(solution)/shard_map/ppermute | solution.py:469
  19.1 17.2 %all-to-all-start = ((bf16[16,32,128]{2,1,0:T(8,128)(2,1)}), bf16[16,32,128]{2,1,0:T(8,128)(2,1)S(1)}, u32[]{:S(2)}, u32[]{:S(2)}) async-start(bf16[16,32,128]{2,1,0:T(8,128)(2,1)} %get-tuple-element.35), calls=%async_computation | async-start | bytes 262144 | tf_op jit(solution)/shard_map/all_to_all | solution.py:448
  27.4 84.2 %all-gather.3.cloned.1.call-start = ((), (), s32[]{:S(2)}) async-start(), calls=%async_computation.7 | async-start | bytes 5308416 | tf_op jit(solution)/shard_map/all_gather | solution.py:490
  27.5 1.6 collective-permute-start.4
  28.0 1.6 collective-permute-start.6
  37.6 13.2 %all-to-all-start.1 = ((bf16[16,32,128]{2,1,0:T(8,128)(2,1)}), bf16[16,32,128]{2,1,0:T(8,128)(2,1)S(1)}, u32[]{:S(2)}, u32[]{:S(2)}) async-start(bf16[16,32,128]{2,1,0:T(8,128)(2,1)} %scan.2), calls=%async_computation.1 | async-start | bytes 262144 | tf_op jit(solution)/shard_map/all_to_all | solution.py:448
  41.8 99.8 %all-gather.5.cloned.1.call-start = ((), (), s32[]{:S(2)}) async-start(), calls=%async_computation.8 | async-start | bytes 2654208 | tf_op jit(solution)/shard_map/all_gather | solution.py:490
  54.0 3.4 %collective-permute-start.7 = (bf16[256,384]{1,0:T(8,128)(2,1)S(1)}, bf16[256,384]{1,0:T(8,128)(2,1)S(1)}, u32[]{:S(2)}, u32[]{:S(2)}) collective-permute-start(bf16[256,384]{1,0:T(8,128)(2,1)S(1)} %get-tuple-element.50), channel_id=1, source_target_pairs={{0,8},{8,0},{1,9},{9,1},{2,10},{10,2},{3,11},{11,3},{4,12},{12,4},... | collective-permute-start | bytes 589832 | tf_op jit(solution)/shard_map/ppermute | solution.py:457
  60.0 25.2 %copy-start.6 = (bf16[256,384]{1,0:T(8,128)(2,1)S(1)}, bf16[256,384]{1,0:T(8,128)(2,1)}, u32[]{:S(2)}) copy-start(bf16[256,384]{1,0:T(8,128)(2,1)} %param.20) | copy-start | bytes 589828
  85.4 0.7 copy-start.4
  86.0 25.6 %copy-start.2 = (f32[3072]{0:T(1024)S(1)}, f32[3072]{0:T(1024)}, u32[]{:S(2)}) copy-start(f32[3072]{0:T(1024)} %param.21) | copy-start | bytes 36868
  108.9 7.3 %collective-permute-start.8 = (bf16[8,256,384]{2,1,0:T(8,128)(2,1)S(1)}, bf16[8,256,384]{2,1,0:T(8,128)(2,1)S(1)}, u32[]{:S(2)}, u32[]{:S(2)}) collective-permute-start(bf16[8,256,384]{2,1,0:T(8,128)(2,1)S(1)} %all_to_all.36.h_ref.mine_ref), channel_id=1, source_target_pairs={{0,8},{8,0},{1,9},{9,1},{2,10},{10,2},{3,11},{11,3},{4,12},{12,4},... | collective-permute-start | bytes 4718600 | tf_op jit(solution)/shard_map/ppermute | solution.py:499
  136.0 0.7 copy-start
  136.7 13.8 %all-to-all-start.5 = ((bf16[16,32,128]{2,1,0:T(8,128)(2,1)}), bf16[16,32,128]{2,1,0:T(8,128)(2,1)S(1)}, u32[]{:S(2)}, u32[]{:S(2)}) async-start(bf16[16,32,128]{2,1,0:T(8,128)(2,1)} %copy-done), calls=%async_computation.5 | async-start | bytes 262144 | tf_op jit(solution)/shard_map/all_to_all | solution.py:448
  153.8 3.1 %collective-permute-start.9 = (bf16[256,384]{1,0:T(8,128)(2,1)S(1)}, bf16[256,384]{1,0:T(8,128)(2,1)S(1)}, u32[]{:S(2)}, u32[]{:S(2)}) collective-permute-start(bf16[256,384]{1,0:T(8,128)(2,1)S(1)} %get-tuple-element.63), channel_id=1, source_target_pairs={{0,8},{8,0},{1,9},{9,1},{2,10},{10,2},{3,11},{11,3},{4,12},{12,4},... | collective-permute-start | bytes 589832 | tf_op jit(solution)/shard_map/ppermute | solution.py:457
  159.5 23.4 %copy-start.5 = (bf16[256,384]{1,0:T(8,128)(2,1)S(1)}, bf16[256,384]{1,0:T(8,128)(2,1)}, u32[]{:S(2)}) copy-start(bf16[256,384]{1,0:T(8,128)(2,1)} %copy-done.4) | copy-start | bytes 589828
Sparse Core Ops, SparseCore 0:
  36.5 57.7 all-gather.2
  96.1 39.5 all-gather.4

commit v7 on v6

--- a/solution.py
+++ b/solution.py
@@ -371,20 +371,25 @@
     return call(scan_kernel, "scan", place, (pieces,), (PIECES_OUT,))[0]
 
 
-def finish_kernel(
-    layer, place, pieces_ref, cum_ref, intra_hbm, qs_hbm, gain_hbm, wo_ref,
-    mine_ref, yours_ref, held, out, intra_ref, qs_ref, gain_ref, sems,
-):
-    core = place[0]
-    pairs = ((intra_hbm, intra_ref), (qs_hbm, qs_ref), (gain_hbm, gain_ref), (wo_ref, held))
+def finish_kernel(layer, own, place, pieces_ref, cum_ref, intra_hbm, qs_hbm, gain_hbm, *refs):
+    core = place[0]
+    rows = span(core if own else 1 - core, BLK)
+    if own:
+        wo_ref, out_ref, held, intra_ref, qs_ref, gain_ref, sems = refs
+    else:
+        out_ref, intra_ref, qs_ref, gain_ref, sems = refs
+    pairs = [(intra_hbm.at[rows, :], intra_ref), (qs_hbm.at[rows, :], qs_ref), (gain_hbm, gain_ref)]
+    if own:
+        pairs.append((wo_ref, held))
     fetches = [pltpu.make_async_copy(a, b, sems.at[n]) for n, (a, b) in enumerate(pairs)]
     for fetch in fetches:
         fetch.start()
     pieces = pieces_ref[...].astype(F32)
+    cum = cum_ref[rows, :]
     states = [
         pieces[:, h * SUB : (h + 1) * SUB].reshape(DH, DH).astype(BF16) for h in range(HC)
     ]
-    scales = [jnp.exp(cum_ref[:, layer * HC + h : layer * HC + h + 1]) for h in range(HC)]
+    scales = [jnp.exp(cum[:, layer * HC + h : layer * HC + h + 1]) for h in range(HC)]
     for fetch in fetches[:3]:
         fetch.wait()
     for h in range(HC):
@@ -393,23 +398,23 @@
         att = intra_ref[:, cols] + carried * scales[h]
         square = jnp.mean(att * att, axis=-1, keepdims=True)
         gain = gain_ref[pl.ds(core * HC + h, 1), :]
-        out[:, cols] = (att * lax.rsqrt(square + 1e-06) * gain).astype(BF16)
-    mine_ref[...] = out[span(core, BLK), :]
-    yours_ref[...] = out[span(1 - core, BLK), :]
-    fetches[3].wait()
-
-
-def finish(place, layer, pieces, intra, cum, qs, gain, wo):
+        out_ref[:, cols] = (att * lax.rsqrt(square + 1e-06) * gain).astype(BF16)
+    for fetch in fetches[3:]:
+        fetch.wait()
+
+
+def finish(place, layer, own, pieces, intra, cum, qs, gain, *wo):
     if layer:
         intra, qs = in_hbm(intra), in_hbm(qs)
+    wo = [in_hbm(w) for w in wo]
+    outs = (struct((BLK, HW), BF16),) + (WO_OUT,) * len(wo)
     return call(
-        lambda *refs: finish_kernel(layer, *refs), "finish", place,
-        (pieces, cum, intra, qs, gain, in_hbm(wo)),
-        (struct((BLK, HW), BF16), struct((BLK, HW), BF16), WO_OUT),
-        in_specs=[whole(pieces.shape), whole(cum.shape)] + [ANY] * 4,
-        out_specs=[whole((BLK, HW)), whole((BLK, HW)), IN_VMEM],
+        lambda *refs: finish_kernel(layer, own, *refs), "finish_own" if own else "finish_other",
+        place, (pieces, cum, intra, qs, gain, *wo), outs,
+        in_specs=[whole(pieces.shape), whole(cum.shape)] + [ANY] * (3 + len(wo)),
+        out_specs=[whole((BLK, HW))] + [IN_VMEM] * len(wo),
         scratch=(
-            pltpu.VMEM((TOK, HW), BF16), pltpu.VMEM((TOK, HW), F32), pltpu.VMEM((TOK, HW), BF16),
+            pltpu.VMEM((BLK, HW), F32), pltpu.VMEM((BLK, HW), BF16),
             pltpu.VMEM((2 * HC, DH), F32), pltpu.SemaphoreType.DMA((4,)),
         ),
     )
@@ -453,8 +458,10 @@
 
 
 def rest(place, layer, before, intra, cum, qs, gain, w):
-    mine, yours, w = finish(place, layer, before, intra, cum, qs, in_hbm(gain.reshape(2 * HC, DH)), w)
+    parts = (before, intra, cum, qs, in_hbm(gain.reshape(2 * HC, DH)))
+    yours, = finish(place, layer, False, *parts)
     yours = lax.ppermute(yours, "c", SWAP)
+    mine, w = finish(place, layer, True, *parts, w)
     terms = exchange(project(place, mine, yours, w), ("x", "yl"))
     return jnp.sum(terms.astype(F32), axis=0)
 

time: 191 us -> 194 us (1.016)
  Pallas kernels: 40.4 us -> 44.7 us
  waiting for transfers between devices: 16.7 us -> 14.6 us
    pallas_call x13 -> x15, Pallas kernels: 40.4 us -> 44.7 us  [call(): pl.pallas_call(kernel, out_shape=outs, grid_spec=pltpu.PrefetchScalarGrid...]
    ppermute x2, waiting for transfers between devices: 2.14 us -> 0.01 us  [rest(): yours = lax.ppermute(yours, 'c', SWAP)]
  transfers between devices with their start and end apart: 15 -> 15, of which waited for: 8 -> 6; matrix products, arithmetic and copies ran while one was open for 1% -> 1% of each run, Pallas kernels for 18% -> 21%
where the time goes in v7:
time: 194 us; the launch traced here: 193 us
  blocking collectives  85.9 us (44%)
  Pallas kernels  44.7 us (23%)
  starting transfers between devices  30.6 us (16%)
  waiting for transfers between devices  14.6 us (8%)
  between operations  13.6 us (7%)
  other arithmetic  2 us (1%)
    all_to_all x4, blocking collectives, exchange(): return lax.all_to_all(parts, axes, 0, 0)  85.9 us
    pallas_call x15, Pallas kernels, call(): pl.pallas_call(kernel, out_shape=outs, grid_spec=pltpu.PrefetchScalarGrid...  44.7 us
    all_to_all x3, starting transfers between devices, exchange(): return lax.all_to_all(parts, axes, 0, 0)  17 us
    all_to_all x3, waiting for transfers between devices, exchange(): return lax.all_to_all(parts, axes, 0, 0)  12.2 us
    ppermute x6, starting transfers between devices, swapped(): return [lax.ppermute(a, 'c', SWAP) for a in arrays]  5.13 us
    ppermute x2, starting transfers between devices, rest(): yours = lax.ppermute(yours, 'c', SWAP)  4.39 us
  transfers between devices with their start and end apart: 15, of which 6 were waited for; matrix products, arithmetic and copies ran while one was open for 1% of the time, Pallas kernels for 21%

profile of v7, /device:TPU:1, one launch (start us, length us, event | category | flops | bytes accessed | tf_op | source)
XLA Modules:
  0.0 192.8 jit_solution(4066567166414596058)
XLA Ops:
  6.5 3.2 %collective-permute-start = (bf16[256,768]{1,0:T(8,128)(2,1)}, bf16[256,768]{1,0:T(8,128)(2,1)S(1)}, u32[]{:S(2)}, u32[]{:S(2)}) collective-permute-start(bf16[256,768]{1,0:T(8,128)(2,1)} %k_ref.2), channel_id=1, source_target_pairs={{0,8},{8,0},{1,9},{9,1},{2,10},{10,2},{3,11},{11,3},{4,12},{12,4},... | collective-permute-start | bytes 1179656 | tf_op jit(solution)/shard_map/ppermute | solution.py:476
  9.8 0.0 collective-permute-start.1
  9.8 0.1 pad_add_fusion.place.refs_0_
  9.9 1.6 cut.1
  11.5 1.3 collective-permute-start.5
  12.8 0.7 pad_maximum_fusion.decay_ref
  13.5 0.9 collective-permute-start.2
  14.4 0.8 collective-permute-done.2.other_decay_ref
  15.2 0.0 collective-permute-done.other_k_ref
  15.2 0.0 collective-permute-done.1.other_v_ref
  15.2 3.6 %first_state.1 = (bf16[16,32,128]{2,1,0:T(8,128)(2,1)}, bf16[512,384]{1,0:T(8,128)(2,1)}, bf16[512,384]{1,0:T(8,128)(2,1)}, f32[512,128]{1,0:T(8,128)S(1)}, f32[8,512]{1,0:T(8,128)S(1)}) custom-call(s32[2]{0:T(128)S(1)} %pad_add_fusion.place.refs_0_, bf16[256,768]{1,0:T(8,128)(2,1)} %k_ref.2, bf16[256,768]{1,0:T(8,128)(2,1)S(1)} %collective-permute-done.other_k_ref, ...), custom_call_target="tpu_custom_call" | custom-call | tf_op jit(solution)/shard_map/first_state/pallas_call | solution.py:40
  18.8 0.3 collective-permute-start.3
  19.1 8.3 %all-to-all-start = ((bf16[16,32,128]{2,1,0:T(8,128)(2,1)}), bf16[16,32,128]{2,1,0:T(8,128)(2,1)S(1)}, u32[]{:S(2)}, u32[]{:S(2)}) async-start(bf16[16,32,128]{2,1,0:T(8,128)(2,1)} %get-tuple-element.33), calls=%async_computation | async-start | bytes 262144 | tf_op jit(solution)/shard_map/all_to_all | solution.py:453
  27.4 0.0 all-gather.3.cloned.1.call-start
  27.5 0.5 collective-permute-start.4
  28.0 0.0 collective-permute-done.5.far_ref
  28.0 0.1 collective-permute-start.6
  28.2 0.9 collective-permute-done.4.near_other_ref
  29.1 0.5 collective-permute-done.6.far_other_ref
  29.6 1.6 pack.1
  31.2 5.2 %all-to-all-done.in_ref = bf16[16,32,128]{2,1,0:T(8,128)(2,1)S(1)} async-done(((bf16[16,32,128]{2,1,0:T(8,128)(2,1)}), bf16[16,32,128]{2,1,0:T(8,128)(2,1)S(1)}, u32[]{:S(2)}, u32[]{:S(2)}) %all-to-all-start) | async-done | bytes 131104 | tf_op jit(solution)/shard_map/all_to_all | solution.py:453
  36.3 0.0 collective-permute-done.3.other_ref
  36.3 0.0 all-gather.3.cloned.1.call-update
  36.4 1.2 scan.2
  37.6 4.2 %all-to-all-start.1 = ((bf16[16,32,128]{2,1,0:T(8,128)(2,1)}), bf16[16,32,128]{2,1,0:T(8,128)(2,1)S(1)}, u32[]{:S(2)}, u32[]{:S(2)}) async-start(bf16[16,32,128]{2,1,0:T(8,128)(2,1)} %scan.2), calls=%async_computation.1 | async-start | bytes 262144 | tf_op jit(solution)/shard_map/all_to_all | solution.py:453
  41.8 0.0 all-gather.5.cloned.1.call-start
  41.8 0.0 copy-done.1
  41.8 3.2 %first_intra.1 = (f32[512,384]{1,0:T(8,128)S(1)}, bf16[512,384]{1,0:T(8,128)(2,1)S(1)}) custom-call(s32[2]{0:T(128)S(1)} %pad_add_fusion.place.refs_0_, bf16[256,768]{1,0:T(8,128)(2,1)S(1)} %copy-done.1, bf16[256,768]{1,0:T(8,128)(2,1)S(1)} %collective-permute-done.3.other_ref, bf16[512,384]{1,0:T(8,128)(2,1)} %get-tuple-element.42.ks, ...), custom_call_target="tpu_custom_call" | custom-call | tf_op jit(solution)/shard_map/first_intra/pallas_call | solution.py:40
  45.0 0.0 copy-done.3
  45.0 5.8 %all-to-all-done.1.refs_1_ = bf16[16,32,128]{2,1,0:T(8,128)(2,1)S(1)} async-done(((bf16[16,32,128]{2,1,0:T(8,128)(2,1)}), bf16[16,32,128]{2,1,0:T(8,128)(2,1)S(1)}, u32[]{:S(2)}, u32[]{:S(2)}) %all-to-all-start.1) | async-done | bytes 131104 | tf_op jit(solution)/shard_map/all_to_all | solution.py:453
  50.8 2.1 %finish_other.2 = bf16[256,384]{1,0:T(8,128)(2,1)S(1)} custom-call(s32[2]{0:T(128)S(1)} %pad_add_fusion.place.refs_0_, bf16[16,32,128]{2,1,0:T(8,128)(2,1)S(1)} %all-to-all-done.1.refs_1_, f32[512,128]{1,0:T(8,128)S(1)} %get-tuple-element.41.cum_ref.refs_2_, f32[512,384]{1,0:T(8,128)S(1)} %get-tuple-element.45.refs_3_, ...), custom_call_target="tpu_custom_call" | custom-call | tf_op jit(solution)/shard_map/finish_other/pallas_call | solution.py:40
  52.9 2.3 %collective-permute-start.7 = (bf16[256,384]{1,0:T(8,128)(2,1)S(1)}, bf16[256,384]{1,0:T(8,128)(2,1)S(1)}, u32[]{:S(2)}, u32[]{:S(2)}) collective-permute-start(bf16[256,384]{1,0:T(8,128)(2,1)S(1)} %finish_other.2), channel_id=1, source_target_pairs={{0,8},{8,0},{1,9},{9,1},{2,10},{10,2},{3,11},{11,3},{4,12},{12,4},... | collective-permute-start | bytes 589832 | tf_op jit(solution)/shard_map/ppermute | solution.py:463
  55.3 3.4 %finish_own.2 = (bf16[256,384]{1,0:T(8,128)(2,1)S(1)}, bf16[768,3072]{1,0:T(8,128)(2,1)S(1)}) custom-call(s32[2]{0:T(128)S(1)} %pad_add_fusion.place.refs_0_, bf16[16,32,128]{2,1,0:T(8,128)(2,1)S(1)} %all-to-all-done.1.refs_1_, f32[512,128]{1,0:T(8,128)S(1)} %get-tuple-element.41.cum_ref.refs_2_, f32[512,384]{1,0:T(8,128)S(1)} %get-tuple-element.45.refs_3_, ...), custom_call_target="tpu_custom_call" | custom-call | tf_op jit(solution)/shard_map/finish_own/pallas_call | solution.py:40
  58.7 0.0 collective-permute-done.7.yours_ref
  58.7 2.6 %project.2 = bf16[8,256,384]{2,1,0:T(8,128)(2,1)S(1)} custom-call(s32[2]{0:T(128)S(1)} %pad_add_fusion.place.refs_0_, bf16[256,384]{1,0:T(8,128)(2,1)S(1)} %get-tuple-element.47.mine_ref, bf16[256,384]{1,0:T(8,128)(2,1)S(1)} %collective-permute-done.7.yours_ref, bf16[768,3072]{1,0:T(8,128)(2,1)S(1)} %get-tuple-element.48.w_ref), custom_call_target="tpu_custom_call" | custom-call | flops 1207959552 | tf_op jit(solution)/shard_map/project/pallas_call | solution.py:40
  61.3 0.0 copy-start.6
  61.3 25.9 %all_to_all.35 = bf16[8,256,384]{2,1,0:T(8,128)(2,1)S(1)} all-to-all(bf16[8,256,384]{2,1,0:T(8,128)(2,1)S(1)} %project.2), channel_id=1, replica_groups=mesh['yh'=2,'z'=8,'c'=2,'x'=4,'yl'=2] {'x','yl'}, dimensions={0} | all-to-all | bytes 3145728 | tf_op jit(solution)/shard_map/all_to_all | solution.py:453
  87.2 0.2 convert_reduce_fusion.1
  87.4 0.0 copy-done.6
  87.5 0.0 copy-start.4
  87.5 0.0 all-gather.5.cloned.1.call-update
  87.5 0.6 copy-done.4
  88.2 0.1 broadcast_in_dim.2
  88.3 21.8 %all_to_all.36.h_ref.mine_ref = bf16[8,256,384]{2,1,0:T(8,128)(2,1)S(1)} all-to-all(bf16[8,256,384]{2,1,0:T(8,128)(2,1)S(1)} %broadcast_in_dim.2), channel_id=1, replica_groups=mesh['yh'=2,'z'=8,'c'=2,'x'=4,'yl'=2] {'x','yl'}, dimensions={0} | all-to-all | bytes 3145728 | tf_op jit(solution)/shard_map/all_to_all | solution.py:453
  110.1 2.8 %collective-permute-start.8 = (bf16[8,256,384]{2,1,0:T(8,128)(2,1)S(1)}, bf16[8,256,384]{2,1,0:T(8,128)(2,1)S(1)}, u32[]{:S(2)}, u32[]{:S(2)}) collective-permute-start(bf16[8,256,384]{2,1,0:T(8,128)(2,1)S(1)} %all_to_all.36.h_ref.mine_ref), channel_id=1, source_target_pairs={{0,8},{8,0},{1,9},{9,1},{2,10},{10,2},{3,11},{11,3},{4,12},{12,4},... | collective-permute-start | bytes 4718600 | tf_op jit(solution)/shard_map/ppermute | solution.py:506
  112.9 4.6 %own_kv.1 = (bf16[256,768]{1,0:T(8,128)(2,1)S(1)}, bf16[2,1536,768]{2,1,0:T(8,128)(2,1)S(1)}) custom-call(s32[2]{0:T(128)S(1)} %pad_add_fusion.place.refs_0_, bf16[8,256,384]{2,1,0:T(8,128)(2,1)S(1)} %all_to_all.36.h_ref.mine_ref, bf16[2,1536,768]{2,1,0:T(8,128)(2,1)} %all-gather.3.cloned.1.call-done.w_ref, f32[8,1,384]{2,1,0:T(1,128)S(1)} %bitcast.7), custom_call_target="tpu_custom_call" | custom-call | tf_op jit(solution)/shard_map/own_kv/pallas_call | solution.py:40
  117.5 0.0 collective-permute-done.8.h_ref.yours_ref
  117.5 4.7 %second_state.1 = (bf16[16,32,128]{2,1,0:T(8,128)(2,1)S(1)}, bf16[512,384]{1,0:T(8,128)(2,1)}, bf16[512,384]{1,0:T(8,128)(2,1)}) custom-call(s32[2]{0:T(128)S(1)} %pad_add_fusion.place.refs_0_, bf16[8,256,384]{2,1,0:T(8,128)(2,1)S(1)} %collective-permute-done.8.h_ref.yours_ref, bf16[2,1536,768]{2,1,0:T(8,128)(2,1)S(1)} %get-tuple-element.50.w_ref, ...), custom_call_target="tpu_custom_call" | custom-call | tf_op jit(solution)/shard_map/second_state/pallas_call | solution.py:40
  122.2 14.8 %all_to_all.37.in_ref = bf16[16,32,128]{2,1,0:T(8,128)(2,1)S(1)} all-to-all(bf16[16,32,128]{2,1,0:T(8,128)(2,1)S(1)} %get-tuple-element.52), channel_id=1, replica_groups=mesh['yh'=2,'z'=8,'c'=2,'x'=4,'yl'=2] {'yh','z'}, dimensions={0} | all-to-all | bytes 262144 | tf_op jit(solution)/shard_map/all_to_all | solution.py:453
  137.0 0.6 scan.3
  137.6 0.6 copy-done
  138.2 4.5 %all-to-all-start.5 = ((bf16[16,32,128]{2,1,0:T(8,128)(2,1)}), bf16[16,32,128]{2,1,0:T(8,128)(2,1)S(1)}, u32[]{:S(2)}, u32[]{:S(2)}) async-start(bf16[16,32,128]{2,1,0:T(8,128)(2,1)} %copy-done), calls=%async_computation.5 | async-start | bytes 262144 | tf_op jit(solution)/shard_map/all_to_all | solution.py:453
  142.8 0.0 all-gather.5.cloned.1.call-done.w_ref
  142.8 7.7 %second_intra.1 = (f32[512,384]{1,0:T(8,128)}, bf16[512,384]{1,0:T(8,128)(2,1)}) custom-call(s32[2]{0:T(128)S(1)} %pad_add_fusion.place.refs_0_, bf16[8,256,384]{2,1,0:T(8,128)(2,1)S(1)} %all_to_all.36.h_ref.mine_ref, bf16[8,256,384]{2,1,0:T(8,128)(2,1)S(1)} %collective-permute-done.8.h_ref.yours_ref, ...), custom_call_target="tpu_custom_call" | custom-call | tf_op jit(solution)/shard_map/second_intra/pallas_call | solution.py:40
  150.4 1.2 all-to-all-done.5.refs_1_
  151.7 2.0 %finish_other.3 = bf16[256,384]{1,0:T(8,128)(2,1)S(1)} custom-call(s32[2]{0:T(128)S(1)} %pad_add_fusion.place.refs_0_, bf16[16,32,128]{2,1,0:T(8,128)(2,1)S(1)} %all-to-all-done.5.refs_1_, f32[512,128]{1,0:T(8,128)S(1)} %get-tuple-element.41.cum_ref.refs_2_, f32[512,384]{1,0:T(8,128)} %get-tuple-element.57.refs_3_, ...), custom_call_target="tpu_custom_call" | custom-call | tf_op jit(solution)/shard_map/finish_other/pallas_call | solution.py:40
  153.8 2.0 %collective-permute-start.9 = (bf16[256,384]{1,0:T(8,128)(2,1)S(1)}, bf16[256,384]{1,0:T(8,128)(2,1)S(1)}, u32[]{:S(2)}, u32[]{:S(2)}) collective-permute-start(bf16[256,384]{1,0:T(8,128)(2,1)S(1)} %finish_other.3), channel_id=1, source_target_pairs={{0,8},{8,0},{1,9},{9,1},{2,10},{10,2},{3,11},{11,3},{4,12},{12,4},... | collective-permute-start | bytes 589832 | tf_op jit(solution)/shard_map/ppermute | solution.py:463
  155.8 3.2 %finish_own.3 = (bf16[256,384]{1,0:T(8,128)(2,1)S(1)}, bf16[768,3072]{1,0:T(8,128)(2,1)S(1)}) custom-call(s32[2]{0:T(128)S(1)} %pad_add_fusion.place.refs_0_, bf16[16,32,128]{2,1,0:T(8,128)(2,1)S(1)} %all-to-all-done.5.refs_1_, f32[512,128]{1,0:T(8,128)S(1)} %get-tuple-element.41.cum_ref.refs_2_, f32[512,384]{1,0:T(8,128)} %get-tuple-element.57.refs_3_, ...), custom_call_target="tpu_custom_call" | custom-call | tf_op jit(solution)/shard_map/finish_own/pallas_call | solution.py:40
  159.0 0.0 collective-permute-done.9.yours_ref
  159.0 2.6 %project.3 = bf16[8,256,384]{2,1,0:T(8,128)(2,1)S(1)} custom-call(s32[2]{0:T(128)S(1)} %pad_add_fusion.place.refs_0_, bf16[256,384]{1,0:T(8,128)(2,1)S(1)} %get-tuple-element.59.mine_ref, bf16[256,384]{1,0:T(8,128)(2,1)S(1)} %collective-permute-done.9.yours_ref, bf16[768,3072]{1,0:T(8,128)(2,1)S(1)} %get-tuple-element.60.w_ref), custom_call_target="tpu_custom_call" | custom-call | flops 1207959552 | tf_op jit(solution)/shard_map/project/pallas_call | solution.py:40
  161.6 0.0 copy-start.5
  161.6 23.4 %all_to_all.38 = bf16[8,256,384]{2,1,0:T(8,128)(2,1)S(1)} all-to-all(bf16[8,256,384]{2,1,0:T(8,128)(2,1)S(1)} %project.3), channel_id=1, replica_groups=mesh['yh'=2,'z'=8,'c'=2,'x'=4,'yl'=2] {'x','yl'}, dimensions={0} | all-to-all | bytes 3145728 | tf_op jit(solution)/shard_map/all_to_all | solution.py:453
  185.1 0.2 convert_reduce_fusion
  185.3 0.7 add_convert_fusion
  (9 shorter events, 0.1 us)
Async XLA Ops:
  6.5 8.7 %collective-permute-start = (bf16[256,768]{1,0:T(8,128)(2,1)}, bf16[256,768]{1,0:T(8,128)(2,1)S(1)}, u32[]{:S(2)}, u32[]{:S(2)}) collective-permute-start(bf16[256,768]{1,0:T(8,128)(2,1)} %k_ref.2), channel_id=1, source_target_pairs={{0,8},{8,0},{1,9},{9,1},{2,10},{10,2},{3,11},{11,3},{4,12},{12,4},... | collective-permute-start | bytes 1179656 | tf_op jit(solution)/shard_map/ppermute | solution.py:476
  9.8 5.4 %collective-permute-start.1 = (bf16[256,768]{1,0:T(8,128)(2,1)}, bf16[256,768]{1,0:T(8,128)(2,1)S(1)}, u32[]{:S(2)}, u32[]{:S(2)}) collective-permute-start(bf16[256,768]{1,0:T(8,128)(2,1)} %v_ref.2), channel_id=1, source_target_pairs={{0,8},{8,0},{1,9},{9,1},{2,10},{10,2},{3,11},{11,3},{4,12},{12,4},... | collective-permute-start | bytes 1179656 | tf_op jit(solution)/shard_map/ppermute | solution.py:476
  11.5 16.5 %collective-permute-start.5 = (bf16[96,2304]{1,0:T(8,128)(2,1)S(1)}, bf16[96,2304]{1,0:T(8,128)(2,1)S(1)}, u32[]{:S(2)}, u32[]{:S(2)}) collective-permute-start(bf16[96,2304]{1,0:T(8,128)(2,1)S(1)} %get-tuple-element.35.near_ref), channel_id=1, source_target_pairs={{0,128},{128,0},{1,129},{129,1},{2,130},{130,2},{3,131},{131,3},{4... | collective-permute-start | bytes 1327112 | tf_op jit(solution)/shard_map/ppermute | solution.py:485
  13.5 28.3 %copy-start.1 = (bf16[256,768]{1,0:T(8,128)(2,1)S(1)}, bf16[256,768]{1,0:T(8,128)(2,1)}, u32[]{:S(2)}) copy-start(bf16[256,768]{1,0:T(8,128)(2,1)} %q_ref.2) | copy-start | bytes 1179652
  13.5 1.7 collective-permute-start.2
  18.8 26.2 %copy-start.3 = (f32[8,512]{1,0:T(8,128)}, f32[8,512]{1,0:T(8,128)S(1)}, u32[]{:S(2)}) copy-start(f32[8,512]{1,0:T(8,128)S(1)} %get-tuple-element.44.across_ref) | copy-start | bytes 49156
  18.8 17.6 %collective-permute-start.3 = (bf16[256,768]{1,0:T(8,128)(2,1)}, bf16[256,768]{1,0:T(8,128)(2,1)S(1)}, u32[]{:S(2)}, u32[]{:S(2)}) collective-permute-start(bf16[256,768]{1,0:T(8,128)(2,1)} %q_ref.2), channel_id=1, source_target_pairs={{0,8},{8,0},{1,9},{9,1},{2,10},{10,2},{3,11},{11,3},{4,12},{12,4},... | collective-permute-start | bytes 1179656 | tf_op jit(solution)/shard_map/ppermute | solution.py:476
  19.1 17.2 %all-to-all-start = ((bf16[16,32,128]{2,1,0:T(8,128)(2,1)}), bf16[16,32,128]{2,1,0:T(8,128)(2,1)S(1)}, u32[]{:S(2)}, u32[]{:S(2)}) async-start(bf16[16,32,128]{2,1,0:T(8,128)(2,1)} %get-tuple-element.33), calls=%async_computation | async-start | bytes 262144 | tf_op jit(solution)/shard_map/all_to_all | solution.py:453
  27.4 85.5 %all-gather.3.cloned.1.call-start = ((), (), s32[]{:S(2)}) async-start(), calls=%async_computation.7 | async-start | bytes 5308416 | tf_op jit(solution)/shard_map/all_gather | solution.py:497
  27.5 1.6 collective-permute-start.4
  28.0 1.6 collective-permute-start.6
  37.6 13.2 %all-to-all-start.1 = ((bf16[16,32,128]{2,1,0:T(8,128)(2,1)}), bf16[16,32,128]{2,1,0:T(8,128)(2,1)S(1)}, u32[]{:S(2)}, u32[]{:S(2)}) async-start(bf16[16,32,128]{2,1,0:T(8,128)(2,1)} %scan.2), calls=%async_computation.1 | async-start | bytes 262144 | tf_op jit(solution)/shard_map/all_to_all | solution.py:453
  41.8 101.0 %all-gather.5.cloned.1.call-start = ((), (), s32[]{:S(2)}) async-start(), calls=%async_computation.8 | async-start | bytes 2654208 | tf_op jit(solution)/shard_map/all_gather | solution.py:497
  52.9 5.8 %collective-permute-start.7 = (bf16[256,384]{1,0:T(8,128)(2,1)S(1)}, bf16[256,384]{1,0:T(8,128)(2,1)S(1)}, u32[]{:S(2)}, u32[]{:S(2)}) collective-permute-start(bf16[256,384]{1,0:T(8,128)(2,1)S(1)} %finish_other.2), channel_id=1, source_target_pairs={{0,8},{8,0},{1,9},{9,1},{2,10},{10,2},{3,11},{11,3},{4,12},{12,4},... | collective-permute-start | bytes 589832 | tf_op jit(solution)/shard_map/ppermute | solution.py:463
  61.3 26.1 %copy-start.6 = (bf16[256,384]{1,0:T(8,128)(2,1)S(1)}, bf16[256,384]{1,0:T(8,128)(2,1)}, u32[]{:S(2)}) copy-start(bf16[256,384]{1,0:T(8,128)(2,1)} %param.20) | copy-start | bytes 589828
  87.5 0.7 copy-start.4
  88.2 24.7 %copy-start.2 = (f32[3072]{0:T(1024)S(1)}, f32[3072]{0:T(1024)}, u32[]{:S(2)}) copy-start(f32[3072]{0:T(1024)} %param.21) | copy-start | bytes 36868
  110.1 7.3 %collective-permute-start.8 = (bf16[8,256,384]{2,1,0:T(8,128)(2,1)S(1)}, bf16[8,256,384]{2,1,0:T(8,128)(2,1)S(1)}, u32[]{:S(2)}, u32[]{:S(2)}) collective-permute-start(bf16[8,256,384]{2,1,0:T(8,128)(2,1)S(1)} %all_to_all.36.h_ref.mine_ref), channel_id=1, source_target_pairs={{0,8},{8,0},{1,9},{9,1},{2,10},{10,2},{3,11},{11,3},{4,12},{12,4},... | collective-permute-start | bytes 4718600 | tf_op jit(solution)/shard_map/ppermute | solution.py:506
  137.6 0.7 copy-start
  138.2 13.5 %all-to-all-start.5 = ((bf16[16,32,128]{2,1,0:T(8,128)(2,1)}), bf16[16,32,128]{2,1,0:T(8,128)(2,1)S(1)}, u32[]{:S(2)}, u32[]{:S(2)}) async-start(bf16[16,32,128]{2,1,0:T(8,128)(2,1)} %copy-done), calls=%async_computation.5 | async-start | bytes 262144 | tf_op jit(solution)/shard_map/all_to_all | solution.py:453
  153.8 5.2 %collective-permute-start.9 = (bf16[256,384]{1,0:T(8,128)(2,1)S(1)}, bf16[256,384]{1,0:T(8,128)(2,1)S(1)}, u32[]{:S(2)}, u32[]{:S(2)}) collective-permute-start(bf16[256,384]{1,0:T(8,128)(2,1)S(1)} %finish_other.3), channel_id=1, source_target_pairs={{0,8},{8,0},{1,9},{9,1},{2,10},{10,2},{3,11},{11,3},{4,12},{12,4},... | collective-permute-start | bytes 589832 | tf_op jit(solution)/shard_map/ppermute | solution.py:463
  161.6 23.7 %copy-start.5 = (bf16[256,384]{1,0:T(8,128)(2,1)S(1)}, bf16[256,384]{1,0:T(8,128)(2,1)}, u32[]{:S(2)}) copy-start(bf16[256,384]{1,0:T(8,128)(2,1)} %copy-done.4) | copy-start | bytes 589828
Sparse Core Ops, SparseCore 0:
  36.5 57.7 all-gather.2
  96.1 39.6 all-gather.4

commit v8 on v6

--- a/solution.py
+++ b/solution.py
@@ -18,8 +18,10 @@
 NHEAD = 8
 STEPS = 4
 KSTEP = 2 * WIDTH
+PAIR = 2
+QUAD = NHEAD // PAIR
 SWAP = [(0, 1), (1, 0)]
-VMEM = 16 * 1024 * 1024
+VMEM = 24 * 1024 * 1024
 F32 = jnp.float32
 BF16 = jnp.bfloat16
 
@@ -131,8 +133,11 @@
 
 
 def both_cores(core, mine_ref, yours_ref, out):
-    out[span(core, BLK), :] = silu(mine_ref[:, span(core, HW)].astype(F32)).astype(BF16)
-    out[span(1 - core, BLK), :] = silu(yours_ref[:, span(core, HW)].astype(F32)).astype(BF16)
+    out[span(core, BLK), :] = silu(mine_ref[...].astype(F32)).astype(BF16)
+    out[span(1 - core, BLK), :] = silu(yours_ref[...].astype(F32)).astype(BF16)
+
+
+HALF = pl.BlockSpec((BLK, HW), lambda _, place: (0, place[0]))
 
 
 def first_state_kernel(
@@ -159,7 +164,10 @@
 def first_state(place, *args):
     outs = (PIECES_OUT, HEADS_OUT, HEADS_OUT, struct((TOK, DH), F32), struct((8, TOK), F32))
     scratch = (pltpu.VMEM((16, TOK), F32),)
-    return call(first_state_kernel, "first_state", place, args, outs, scratch=scratch)
+    specs = [HALF] * 4 + [whole(a.shape) for a in args[4:]]
+    return call(
+        first_state_kernel, "first_state", place, args, outs, in_specs=specs, scratch=scratch
+    )
 
 
 def first_intra_kernel(
@@ -172,13 +180,15 @@
 
 def first_intra(place, q, other, ks, vs, cum, across):
     args = (q, other, in_hbm(ks), in_hbm(vs), cum, across)
-    return call(first_intra_kernel, "first_intra", place, args, (INTRA_OUT, QUERY_OUT))
+    specs = [HALF] * 2 + [whole(a.shape) for a in args[2:]]
+    outs = (INTRA_OUT, QUERY_OUT)
+    return call(first_intra_kernel, "first_intra", place, args, outs, in_specs=specs)
 
 
 def gained(h_ref, gain_ref):
     parts = []
     total = None
-    for i in range(2):
+    for i in range(QUAD):
         wide = h_ref[i].astype(F32)
         parts.append((wide * gain_ref[i]).astype(BF16))
         for n in range(WIDTH // DH):
@@ -211,49 +221,36 @@
 
 
 def chunk_at(i, place):
-    half = STEPS // 2
-    return jnp.where(i < half, place[1] * half + i, (1 - place[1]) * half + i - half), 0, 0
+    return jnp.where(i == 0, place[1], 1 - place[1]), 0, 0
 
 
 def projection_specs(width):
-    half = STEPS // 2
     return (
-        pl.BlockSpec((2, BLK, WIDTH), chunk_at),
-        pl.BlockSpec((1, KSTEP, width), lambda i, _: (i // half, i % half, 0)),
-        pl.BlockSpec((2, 1, WIDTH), chunk_at),
-    )
-
-
-def weight_rows(w_ref):
-    half = STEPS // 2
-    step = pl.program_id(0)
-    return w_ref.at[step // half, pl.ds(pl.multiple_of(step % half * KSTEP, KSTEP), KSTEP), :]
+        pl.BlockSpec((QUAD, BLK, WIDTH), chunk_at),
+        pl.BlockSpec((1, QUAD * WIDTH, width), lambda i, _: (i, 0, 0)),
+        pl.BlockSpec((QUAD, 1, WIDTH), chunk_at),
+    )
 
 
 def own_kv_kernel(place, h_ref, w_ref, gain_ref, out_ref, held, acc, square, sems):
     step = pl.program_id(0)
-    half = STEPS // 2
-
-    def fetch(n):
-        rows = pl.ds(n % half * KSTEP, KSTEP)
-        return pltpu.make_async_copy(
-            w_ref.at[n // half, rows, :], held.at[n // half, rows, :], sems.at[n]
-        )
+    fetches = [
+        pltpu.make_async_copy(w_ref.at[n], held.at[n], sems.at[n]) for n in range(PAIR)
+    ]
 
     @pl.when(step == 0)
     def _():
-        for n in range(STEPS):
-            fetch(n).start()
-
-    for n in range(STEPS):
-
-        @pl.when(step == n)
-        def _(n=n):
-            fetch(n).wait()
-
-    project_step([h_ref], weight_rows(held)[...], gain_ref, acc, square)
-
-    @pl.when(step == STEPS - 1)
+        for fetch in fetches:
+            fetch.start()
+        fetches[0].wait()
+
+    @pl.when(step == 1)
+    def _():
+        fetches[1].wait()
+
+    project_step([h_ref], held[step], gain_ref, acc, square)
+
+    @pl.when(step == PAIR - 1)
     def _():
         out_ref[...] = silu(acc[...] * row_scale(square[...])).astype(BF16)
 
@@ -263,10 +260,10 @@
     return call(
         own_kv_kernel, "own_kv", place, (h, in_hbm(w), gain),
         (struct((BLK, 2 * HW), BF16), WKV_OUT),
-        grid=(STEPS,), in_specs=[hs, ANY, gs], out_specs=[whole((BLK, 2 * HW)), IN_VMEM],
+        grid=(PAIR,), in_specs=[hs, ANY, gs], out_specs=[whole((BLK, 2 * HW)), IN_VMEM],
         scratch=(
             pltpu.VMEM((BLK, 2 * HW), F32), pltpu.VMEM((BLK, DH), F32),
-            pltpu.SemaphoreType.DMA((STEPS,)),
+            pltpu.SemaphoreType.DMA((PAIR,)),
         ),
     )
 
@@ -275,9 +272,9 @@
     place, h_ref, w_ref, gain_ref, own_ref, cum_ref, pieces_ref, ks, vs, acc, square
 ):
     core = place[0]
-    project_step([h_ref], weight_rows(w_ref)[...], gain_ref, acc, square)
-
-    @pl.when(pl.program_id(0) == STEPS - 1)
+    project_step([h_ref], w_ref[pl.program_id(0)], gain_ref, acc, square)
+
+    @pl.when(pl.program_id(0) == PAIR - 1)
     def _():
         scale = row_scale(square[...])
         for n, dst in enumerate((ks, vs)):
@@ -292,7 +289,7 @@
     return call(
         second_state_kernel, "second_state", place, (h, w, gain, own, cum),
         (PIECES_OUT, HEADS_OUT, HEADS_OUT),
-        grid=(STEPS,), in_specs=[hs, IN_VMEM, gs, whole(own.shape), whole(cum.shape)],
+        grid=(PAIR,), in_specs=[hs, IN_VMEM, gs, whole(own.shape), whole(cum.shape)],
         scratch=(pltpu.VMEM((BLK, 2 * HW), F32), pltpu.VMEM((BLK, DH), F32)),
     )
 
@@ -304,7 +301,7 @@
     core = place[0]
     project_step([mine_ref, yours_ref], w_ref[0], gain_ref, acc, square)
 
-    @pl.when(pl.program_id(0) == STEPS - 1)
+    @pl.when(pl.program_id(0) == PAIR - 1)
     def _():
         act = silu(acc[...] * row_scale(square[...])).astype(BF16)
         qs[span(core, BLK), :] = act[:BLK]
@@ -318,7 +315,7 @@
         second_intra_kernel, "second_intra", place,
         (mine, yours, in_hbm(w), gain, in_hbm(ks), in_hbm(vs), cum, in_hbm(across)),
         (pltpu.HBM((TOK, HW), F32), HEADS_OUT),
-        grid=(STEPS,),
+        grid=(PAIR,),
         in_specs=[hs, hs, ws, gs] + [whole(a.shape) for a in (ks, vs, cum, across)],
         scratch=(pltpu.VMEM((TOK, HW), F32), pltpu.VMEM((TOK, DH), F32)),
     )

time: 191 us -> 190 us (level)
  transfers between devices with their start and end apart: 15 -> 15, of which waited for: 8 -> 8; matrix products, arithmetic and copies ran while one was open for 1% -> 1% of each run, Pallas kernels for 18% -> 17%
where the time goes in v8:
time: 190 us; the launch traced here: 189 us
  blocking collectives  85 us (45%)
  Pallas kernels  38.8 us (20%)
  starting transfers between devices  31.1 us (16%)
  waiting for transfers between devices  17.6 us (9%)
  between operations  13.6 us (7%)
  other arithmetic  1.99 us (1%)
    all_to_all x4, blocking collectives, exchange(): return lax.all_to_all(parts, axes, 0, 0)  85 us
    pallas_call x13, Pallas kernels, call(): pl.pallas_call(kernel, out_shape=outs, grid_spec=pltpu.PrefetchScalarGrid...  38.8 us
    all_to_all x3, starting transfers between devices, exchange(): return lax.all_to_all(parts, axes, 0, 0)  17.3 us
    all_to_all x3, waiting for transfers between devices, exchange(): return lax.all_to_all(parts, axes, 0, 0)  13.1 us
    ppermute x6, starting transfers between devices, swapped(): return [lax.ppermute(a, 'c', SWAP) for a in arrays]  5.14 us
    ppermute x2, starting transfers between devices, rest(): yours = lax.ppermute(yours, 'c', SWAP)  4.5 us
  transfers between devices with their start and end apart: 15, of which 8 were waited for; matrix products, arithmetic and copies ran while one was open for 1% of the time, Pallas kernels for 17%

profile of v8, /device:TPU:1, one launch (start us, length us, event | category | flops | bytes accessed | tf_op | source)
XLA Modules:
  0.0 189.5 jit_solution(14619003780661035314)
XLA Ops:
  6.5 3.2 %collective-permute-start = (bf16[256,768]{1,0:T(8,128)(2,1)}, bf16[256,768]{1,0:T(8,128)(2,1)S(1)}, u32[]{:S(2)}, u32[]{:S(2)}) collective-permute-start(bf16[256,768]{1,0:T(8,128)(2,1)} %k_ref.2), channel_id=1, source_target_pairs={{0,8},{8,0},{1,9},{9,1},{2,10},{10,2},{3,11},{11,3},{4,12},{12,4},... | collective-permute-start | bytes 1179656 | tf_op jit(solution)/shard_map/ppermute | solution.py:466
  9.8 0.0 collective-permute-start.1
  9.8 0.1 pad_add_fusion.place.refs_0_
  9.9 1.6 cut.1
  11.5 1.3 collective-permute-start.5
  12.8 0.7 pad_maximum_fusion.decay_ref
  13.5 0.9 collective-permute-start.2
  14.4 0.8 collective-permute-done.2.other_decay_ref
  15.2 0.0 collective-permute-done.other_k_ref
  15.2 0.0 collective-permute-done.1.other_v_ref
  15.2 3.5 %first_state.1 = (bf16[16,32,128]{2,1,0:T(8,128)(2,1)}, bf16[512,384]{1,0:T(8,128)(2,1)}, bf16[512,384]{1,0:T(8,128)(2,1)}, f32[512,128]{1,0:T(8,128)S(1)}, f32[8,512]{1,0:T(8,128)S(1)}) custom-call(s32[2]{0:T(128)S(1)} %pad_add_fusion.place.refs_0_, bf16[256,768]{1,0:T(8,128)(2,1)} %k_ref.2, bf16[256,768]{1,0:T(8,128)(2,1)S(1)} %collective-permute-done.other_k_ref, ...), custom_call_target="tpu_custom_call" | custom-call | tf_op jit(solution)/shard_map/first_state/pallas_call | solution.py:42
  18.7 0.3 collective-permute-start.3
  19.0 8.3 %all-to-all-start = ((bf16[16,32,128]{2,1,0:T(8,128)(2,1)}), bf16[16,32,128]{2,1,0:T(8,128)(2,1)S(1)}, u32[]{:S(2)}, u32[]{:S(2)}) async-start(bf16[16,32,128]{2,1,0:T(8,128)(2,1)} %get-tuple-element.35), calls=%async_computation | async-start | bytes 262144 | tf_op jit(solution)/shard_map/all_to_all | solution.py:445
  27.3 0.0 all-gather.3.cloned.1.call-start
  27.4 0.5 collective-permute-start.4
  27.9 0.0 collective-permute-done.5.far_ref
  27.9 0.1 collective-permute-start.6
  28.1 0.9 collective-permute-done.4.near_other_ref
  29.0 0.5 collective-permute-done.6.far_other_ref
  29.5 1.6 pack.1
  31.1 5.2 %all-to-all-done.in_ref = bf16[16,32,128]{2,1,0:T(8,128)(2,1)S(1)} async-done(((bf16[16,32,128]{2,1,0:T(8,128)(2,1)}), bf16[16,32,128]{2,1,0:T(8,128)(2,1)S(1)}, u32[]{:S(2)}, u32[]{:S(2)}) %all-to-all-start) | async-done | bytes 131104 | tf_op jit(solution)/shard_map/all_to_all | solution.py:445
  36.3 0.0 collective-permute-done.3.other_ref
  36.3 0.0 all-gather.3.cloned.1.call-update
  36.3 1.2 scan.2
  37.5 4.1 %all-to-all-start.1 = ((bf16[16,32,128]{2,1,0:T(8,128)(2,1)}), bf16[16,32,128]{2,1,0:T(8,128)(2,1)S(1)}, u32[]{:S(2)}, u32[]{:S(2)}) async-start(bf16[16,32,128]{2,1,0:T(8,128)(2,1)} %scan.2), calls=%async_computation.1 | async-start | bytes 262144 | tf_op jit(solution)/shard_map/all_to_all | solution.py:445
  41.7 0.0 all-gather.5.cloned.1.call-start
  41.7 0.0 copy-done.1
  41.7 3.2 %first_intra.1 = (f32[512,384]{1,0:T(8,128)S(1)}, bf16[512,384]{1,0:T(8,128)(2,1)S(1)}) custom-call(s32[2]{0:T(128)S(1)} %pad_add_fusion.place.refs_0_, bf16[256,768]{1,0:T(8,128)(2,1)S(1)} %copy-done.1, bf16[256,768]{1,0:T(8,128)(2,1)S(1)} %collective-permute-done.3.other_ref, bf16[512,384]{1,0:T(8,128)(2,1)} %get-tuple-element.44.ks, ...), custom_call_target="tpu_custom_call" | custom-call | tf_op jit(solution)/shard_map/first_intra/pallas_call | solution.py:42
  44.9 0.0 copy-done.3
  44.9 5.8 %all-to-all-done.1.refs_1_ = bf16[16,32,128]{2,1,0:T(8,128)(2,1)S(1)} async-done(((bf16[16,32,128]{2,1,0:T(8,128)(2,1)}), bf16[16,32,128]{2,1,0:T(8,128)(2,1)S(1)}, u32[]{:S(2)}, u32[]{:S(2)}) %all-to-all-start.1) | async-done | bytes 131104 | tf_op jit(solution)/shard_map/all_to_all | solution.py:445
  50.7 3.2 %finish.2 = (bf16[256,384]{1,0:T(8,128)(2,1)S(1)}, bf16[256,384]{1,0:T(8,128)(2,1)S(1)}, bf16[768,3072]{1,0:T(8,128)(2,1)S(1)}) custom-call(s32[2]{0:T(128)S(1)} %pad_add_fusion.place.refs_0_, bf16[16,32,128]{2,1,0:T(8,128)(2,1)S(1)} %all-to-all-done.1.refs_1_, f32[512,128]{1,0:T(8,128)S(1)} %get-tuple-element.43.cum_ref.refs_2_, ...), custom_call_target="tpu_custom_call" | custom-call | tf_op jit(solution)/shard_map/finish/pallas_call | solution.py:42
  53.9 2.4 %collective-permute-start.7 = (bf16[256,384]{1,0:T(8,128)(2,1)S(1)}, bf16[256,384]{1,0:T(8,128)(2,1)S(1)}, u32[]{:S(2)}, u32[]{:S(2)}) collective-permute-start(bf16[256,384]{1,0:T(8,128)(2,1)S(1)} %get-tuple-element.50), channel_id=1, source_target_pairs={{0,8},{8,0},{1,9},{9,1},{2,10},{10,2},{3,11},{11,3},{4,12},{12,4},... | collective-permute-start | bytes 589832 | tf_op jit(solution)/shard_map/ppermute | solution.py:454
  56.3 1.1 collective-permute-done.7.yours_ref
  57.3 2.6 %project.2 = bf16[8,256,384]{2,1,0:T(8,128)(2,1)S(1)} custom-call(s32[2]{0:T(128)S(1)} %pad_add_fusion.place.refs_0_, bf16[256,384]{1,0:T(8,128)(2,1)S(1)} %get-tuple-element.49.mine_ref, bf16[256,384]{1,0:T(8,128)(2,1)S(1)} %collective-permute-done.7.yours_ref, bf16[768,3072]{1,0:T(8,128)(2,1)S(1)} %get-tuple-element.51.w_ref), custom_call_target="tpu_custom_call" | custom-call | flops 1207959552 | tf_op jit(solution)/shard_map/project/pallas_call | solution.py:42
  60.0 0.0 copy-start.6
  60.0 25.0 %all_to_all.35 = bf16[8,256,384]{2,1,0:T(8,128)(2,1)S(1)} all-to-all(bf16[8,256,384]{2,1,0:T(8,128)(2,1)S(1)} %project.2), channel_id=1, replica_groups=mesh['yh'=2,'z'=8,'c'=2,'x'=4,'yl'=2] {'x','yl'}, dimensions={0} | all-to-all | bytes 3145728 | tf_op jit(solution)/shard_map/all_to_all | solution.py:445
  85.0 0.2 convert_reduce_fusion.1
  85.2 0.0 copy-done.6
  85.2 0.0 copy-start.4
  85.2 0.0 all-gather.5.cloned.1.call-update
  85.3 0.6 copy-done.4
  85.9 0.1 broadcast_in_dim.2
  86.1 22.7 %all_to_all.36.h_ref.mine_ref = bf16[8,256,384]{2,1,0:T(8,128)(2,1)S(1)} all-to-all(bf16[8,256,384]{2,1,0:T(8,128)(2,1)S(1)} %broadcast_in_dim.2), channel_id=1, replica_groups=mesh['yh'=2,'z'=8,'c'=2,'x'=4,'yl'=2] {'x','yl'}, dimensions={0} | all-to-all | bytes 3145728 | tf_op jit(solution)/shard_map/all_to_all | solution.py:445
  108.8 2.8 %collective-permute-start.8 = (bf16[8,256,384]{2,1,0:T(8,128)(2,1)S(1)}, bf16[8,256,384]{2,1,0:T(8,128)(2,1)S(1)}, u32[]{:S(2)}, u32[]{:S(2)}) collective-permute-start(bf16[8,256,384]{2,1,0:T(8,128)(2,1)S(1)} %all_to_all.36.h_ref.mine_ref), channel_id=1, source_target_pairs={{0,8},{8,0},{1,9},{9,1},{2,10},{10,2},{3,11},{11,3},{4,12},{12,4},... | collective-permute-start | bytes 4718600 | tf_op jit(solution)/shard_map/ppermute | solution.py:496
  111.5 0.0 copy-done.2
  111.5 4.4 %own_kv.1 = (bf16[256,768]{1,0:T(8,128)(2,1)S(1)}, bf16[2,1536,768]{2,1,0:T(8,128)(2,1)S(1)}) custom-call(s32[2]{0:T(128)S(1)} %pad_add_fusion.place.refs_0_, bf16[8,256,384]{2,1,0:T(8,128)(2,1)S(1)} %all_to_all.36.h_ref.mine_ref, bf16[2,1536,768]{2,1,0:T(8,128)(2,1)} %all-gather.3.cloned.1.call-done.w_ref, f32[8,1,384]{2,1,0:T(1,128)S(1)} %bitcast.7), custom_call_target="tpu_custom_call" | custom-call | tf_op jit(solution)/shard_map/own_kv/pallas_call | solution.py:42
  116.0 0.0 collective-permute-done.8.h_ref.yours_ref
  116.0 4.2 %second_state.1 = (bf16[16,32,128]{2,1,0:T(8,128)(2,1)S(1)}, bf16[512,384]{1,0:T(8,128)(2,1)}, bf16[512,384]{1,0:T(8,128)(2,1)}) custom-call(s32[2]{0:T(128)S(1)} %pad_add_fusion.place.refs_0_, bf16[8,256,384]{2,1,0:T(8,128)(2,1)S(1)} %collective-permute-done.8.h_ref.yours_ref, bf16[2,1536,768]{2,1,0:T(8,128)(2,1)S(1)} %get-tuple-element.53.w_ref, ...), custom_call_target="tpu_custom_call" | custom-call | tf_op jit(solution)/shard_map/second_state/pallas_call | solution.py:42
  120.2 14.4 %all_to_all.37.in_ref = bf16[16,32,128]{2,1,0:T(8,128)(2,1)S(1)} all-to-all(bf16[16,32,128]{2,1,0:T(8,128)(2,1)S(1)} %get-tuple-element.55), channel_id=1, replica_groups=mesh['yh'=2,'z'=8,'c'=2,'x'=4,'yl'=2] {'yh','z'}, dimensions={0} | all-to-all | bytes 262144 | tf_op jit(solution)/shard_map/all_to_all | solution.py:445
  134.5 0.6 scan.3
  135.1 0.0 copy-start
  135.1 0.6 copy-done
  135.8 4.8 %all-to-all-start.5 = ((bf16[16,32,128]{2,1,0:T(8,128)(2,1)}), bf16[16,32,128]{2,1,0:T(8,128)(2,1)S(1)}, u32[]{:S(2)}, u32[]{:S(2)}) async-start(bf16[16,32,128]{2,1,0:T(8,128)(2,1)} %copy-done), calls=%async_computation.5 | async-start | bytes 262144 | tf_op jit(solution)/shard_map/all_to_all | solution.py:445
  140.6 0.0 all-gather.5.cloned.1.call-done.w_ref
  140.7 6.8 %second_intra.1 = (f32[512,384]{1,0:T(8,128)}, bf16[512,384]{1,0:T(8,128)(2,1)}) custom-call(s32[2]{0:T(128)S(1)} %pad_add_fusion.place.refs_0_, bf16[8,256,384]{2,1,0:T(8,128)(2,1)S(1)} %all_to_all.36.h_ref.mine_ref, bf16[8,256,384]{2,1,0:T(8,128)(2,1)S(1)} %collective-permute-done.8.h_ref.yours_ref, ...), custom_call_target="tpu_custom_call" | custom-call | tf_op jit(solution)/shard_map/second_intra/pallas_call | solution.py:42
  147.5 2.1 %all-to-all-done.5.refs_1_ = bf16[16,32,128]{2,1,0:T(8,128)(2,1)S(1)} async-done(((bf16[16,32,128]{2,1,0:T(8,128)(2,1)}), bf16[16,32,128]{2,1,0:T(8,128)(2,1)S(1)}, u32[]{:S(2)}, u32[]{:S(2)}) %all-to-all-start.5) | async-done | bytes 131104 | tf_op jit(solution)/shard_map/all_to_all | solution.py:445
  149.6 3.3 %finish.3 = (bf16[256,384]{1,0:T(8,128)(2,1)S(1)}, bf16[256,384]{1,0:T(8,128)(2,1)S(1)}, bf16[768,3072]{1,0:T(8,128)(2,1)S(1)}) custom-call(s32[2]{0:T(128)S(1)} %pad_add_fusion.place.refs_0_, bf16[16,32,128]{2,1,0:T(8,128)(2,1)S(1)} %all-to-all-done.5.refs_1_, f32[512,128]{1,0:T(8,128)S(1)} %get-tuple-element.43.cum_ref.refs_2_, ...), custom_call_target="tpu_custom_call" | custom-call | tf_op jit(solution)/shard_map/finish/pallas_call | solution.py:42
  152.9 2.1 %collective-permute-start.9 = (bf16[256,384]{1,0:T(8,128)(2,1)S(1)}, bf16[256,384]{1,0:T(8,128)(2,1)S(1)}, u32[]{:S(2)}, u32[]{:S(2)}) collective-permute-start(bf16[256,384]{1,0:T(8,128)(2,1)S(1)} %get-tuple-element.63), channel_id=1, source_target_pairs={{0,8},{8,0},{1,9},{9,1},{2,10},{10,2},{3,11},{11,3},{4,12},{12,4},... | collective-permute-start | bytes 589832 | tf_op jit(solution)/shard_map/ppermute | solution.py:454
  155.0 1.1 collective-permute-done.9.yours_ref
  156.1 2.6 %project.3 = bf16[8,256,384]{2,1,0:T(8,128)(2,1)S(1)} custom-call(s32[2]{0:T(128)S(1)} %pad_add_fusion.place.refs_0_, bf16[256,384]{1,0:T(8,128)(2,1)S(1)} %get-tuple-element.62.mine_ref, bf16[256,384]{1,0:T(8,128)(2,1)S(1)} %collective-permute-done.9.yours_ref, bf16[768,3072]{1,0:T(8,128)(2,1)S(1)} %get-tuple-element.64.w_ref), custom_call_target="tpu_custom_call" | custom-call | flops 1207959552 | tf_op jit(solution)/shard_map/project/pallas_call | solution.py:42
  158.7 0.0 copy-start.5
  158.7 22.9 %all_to_all.38 = bf16[8,256,384]{2,1,0:T(8,128)(2,1)S(1)} all-to-all(bf16[8,256,384]{2,1,0:T(8,128)(2,1)S(1)} %project.3), channel_id=1, replica_groups=mesh['yh'=2,'z'=8,'c'=2,'x'=4,'yl'=2] {'x','yl'}, dimensions={0} | all-to-all | bytes 3145728 | tf_op jit(solution)/shard_map/all_to_all | solution.py:445
  181.7 0.2 convert_reduce_fusion
  181.9 0.7 add_convert_fusion
  (7 shorter events, 0.1 us)
Async XLA Ops:
  6.5 8.7 %collective-permute-start = (bf16[256,768]{1,0:T(8,128)(2,1)}, bf16[256,768]{1,0:T(8,128)(2,1)S(1)}, u32[]{:S(2)}, u32[]{:S(2)}) collective-permute-start(bf16[256,768]{1,0:T(8,128)(2,1)} %k_ref.2), channel_id=1, source_target_pairs={{0,8},{8,0},{1,9},{9,1},{2,10},{10,2},{3,11},{11,3},{4,12},{12,4},... | collective-permute-start | bytes 1179656 | tf_op jit(solution)/shard_map/ppermute | solution.py:466
  9.8 5.4 %collective-permute-start.1 = (bf16[256,768]{1,0:T(8,128)(2,1)}, bf16[256,768]{1,0:T(8,128)(2,1)S(1)}, u32[]{:S(2)}, u32[]{:S(2)}) collective-permute-start(bf16[256,768]{1,0:T(8,128)(2,1)} %v_ref.2), channel_id=1, source_target_pairs={{0,8},{8,0},{1,9},{9,1},{2,10},{10,2},{3,11},{11,3},{4,12},{12,4},... | collective-permute-start | bytes 1179656 | tf_op jit(solution)/shard_map/ppermute | solution.py:466
  11.5 16.4 %collective-permute-start.5 = (bf16[96,2304]{1,0:T(8,128)(2,1)S(1)}, bf16[96,2304]{1,0:T(8,128)(2,1)S(1)}, u32[]{:S(2)}, u32[]{:S(2)}) collective-permute-start(bf16[96,2304]{1,0:T(8,128)(2,1)S(1)} %get-tuple-element.37.near_ref), channel_id=1, source_target_pairs={{0,128},{128,0},{1,129},{129,1},{2,130},{130,2},{3,131},{131,3},{4... | collective-permute-start | bytes 1327112 | tf_op jit(solution)/shard_map/ppermute | solution.py:475
  13.5 28.2 %copy-start.1 = (bf16[256,768]{1,0:T(8,128)(2,1)S(1)}, bf16[256,768]{1,0:T(8,128)(2,1)}, u32[]{:S(2)}) copy-start(bf16[256,768]{1,0:T(8,128)(2,1)} %q_ref.2) | copy-start | bytes 1179652
  13.5 1.7 collective-permute-start.2
  18.7 26.2 %copy-start.3 = (f32[8,512]{1,0:T(8,128)}, f32[8,512]{1,0:T(8,128)S(1)}, u32[]{:S(2)}) copy-start(f32[8,512]{1,0:T(8,128)S(1)} %get-tuple-element.46.across_ref) | copy-start | bytes 49156
  18.7 17.6 %collective-permute-start.3 = (bf16[256,768]{1,0:T(8,128)(2,1)}, bf16[256,768]{1,0:T(8,128)(2,1)S(1)}, u32[]{:S(2)}, u32[]{:S(2)}) collective-permute-start(bf16[256,768]{1,0:T(8,128)(2,1)} %q_ref.2), channel_id=1, source_target_pairs={{0,8},{8,0},{1,9},{9,1},{2,10},{10,2},{3,11},{11,3},{4,12},{12,4},... | collective-permute-start | bytes 1179656 | tf_op jit(solution)/shard_map/ppermute | solution.py:466
  19.0 17.2 %all-to-all-start = ((bf16[16,32,128]{2,1,0:T(8,128)(2,1)}), bf16[16,32,128]{2,1,0:T(8,128)(2,1)S(1)}, u32[]{:S(2)}, u32[]{:S(2)}) async-start(bf16[16,32,128]{2,1,0:T(8,128)(2,1)} %get-tuple-element.35), calls=%async_computation | async-start | bytes 262144 | tf_op jit(solution)/shard_map/all_to_all | solution.py:445
  27.3 84.2 %all-gather.3.cloned.1.call-start = ((), (), s32[]{:S(2)}) async-start(), calls=%async_computation.7 | async-start | bytes 5308416 | tf_op jit(solution)/shard_map/all_gather | solution.py:487
  27.4 1.6 collective-permute-start.4
  27.9 1.6 collective-permute-start.6
  37.5 13.2 %all-to-all-start.1 = ((bf16[16,32,128]{2,1,0:T(8,128)(2,1)}), bf16[16,32,128]{2,1,0:T(8,128)(2,1)S(1)}, u32[]{:S(2)}, u32[]{:S(2)}) async-start(bf16[16,32,128]{2,1,0:T(8,128)(2,1)} %scan.2), calls=%async_computation.1 | async-start | bytes 262144 | tf_op jit(solution)/shard_map/all_to_all | solution.py:445
  41.7 99.0 %all-gather.5.cloned.1.call-start = ((), (), s32[]{:S(2)}) async-start(), calls=%async_computation.8 | async-start | bytes 2654208 | tf_op jit(solution)/shard_map/all_gather | solution.py:487
  53.9 3.4 %collective-permute-start.7 = (bf16[256,384]{1,0:T(8,128)(2,1)S(1)}, bf16[256,384]{1,0:T(8,128)(2,1)S(1)}, u32[]{:S(2)}, u32[]{:S(2)}) collective-permute-start(bf16[256,384]{1,0:T(8,128)(2,1)S(1)} %get-tuple-element.50), channel_id=1, source_target_pairs={{0,8},{8,0},{1,9},{9,1},{2,10},{10,2},{3,11},{11,3},{4,12},{12,4},... | collective-permute-start | bytes 589832 | tf_op jit(solution)/shard_map/ppermute | solution.py:454
  60.0 25.2 %copy-start.6 = (bf16[256,384]{1,0:T(8,128)(2,1)S(1)}, bf16[256,384]{1,0:T(8,128)(2,1)}, u32[]{:S(2)}) copy-start(bf16[256,384]{1,0:T(8,128)(2,1)} %param.20) | copy-start | bytes 589828
  85.2 0.7 copy-start.4
  85.9 25.6 %copy-start.2 = (f32[3072]{0:T(1024)S(1)}, f32[3072]{0:T(1024)}, u32[]{:S(2)}) copy-start(f32[3072]{0:T(1024)} %param.21) | copy-start | bytes 36868
  108.8 7.2 %collective-permute-start.8 = (bf16[8,256,384]{2,1,0:T(8,128)(2,1)S(1)}, bf16[8,256,384]{2,1,0:T(8,128)(2,1)S(1)}, u32[]{:S(2)}, u32[]{:S(2)}) collective-permute-start(bf16[8,256,384]{2,1,0:T(8,128)(2,1)S(1)} %all_to_all.36.h_ref.mine_ref), channel_id=1, source_target_pairs={{0,8},{8,0},{1,9},{9,1},{2,10},{10,2},{3,11},{11,3},{4,12},{12,4},... | collective-permute-start | bytes 4718600 | tf_op jit(solution)/shard_map/ppermute | solution.py:496
  135.1 0.7 copy-start
  135.8 13.8 %all-to-all-start.5 = ((bf16[16,32,128]{2,1,0:T(8,128)(2,1)}), bf16[16,32,128]{2,1,0:T(8,128)(2,1)S(1)}, u32[]{:S(2)}, u32[]{:S(2)}) async-start(bf16[16,32,128]{2,1,0:T(8,128)(2,1)} %copy-done), calls=%async_computation.5 | async-start | bytes 262144 | tf_op jit(solution)/shard_map/all_to_all | solution.py:445
  152.9 3.2 %collective-permute-start.9 = (bf16[256,384]{1,0:T(8,128)(2,1)S(1)}, bf16[256,384]{1,0:T(8,128)(2,1)S(1)}, u32[]{:S(2)}, u32[]{:S(2)}) collective-permute-start(bf16[256,384]{1,0:T(8,128)(2,1)S(1)} %get-tuple-element.63), channel_id=1, source_target_pairs={{0,8},{8,0},{1,9},{9,1},{2,10},{10,2},{3,11},{11,3},{4,12},{12,4},... | collective-permute-start | bytes 589832 | tf_op jit(solution)/shard_map/ppermute | solution.py:454
  158.7 23.2 %copy-start.5 = (bf16[256,384]{1,0:T(8,128)(2,1)S(1)}, bf16[256,384]{1,0:T(8,128)(2,1)}, u32[]{:S(2)}) copy-start(bf16[256,384]{1,0:T(8,128)(2,1)} %copy-done.4) | copy-start | bytes 589828
Sparse Core Ops, SparseCore 0:
  36.4 57.7 all-gather.2
  96.0 39.3 all-gather.4

commit v9 on v8

--- a/solution.py
+++ b/solution.py
@@ -16,8 +16,8 @@
 PIECE = 32
 WIDTH = 384
 NHEAD = 8
-STEPS = 4
-KSTEP = 2 * WIDTH
+STEPS = 2
+KSTEP = NHEAD // STEPS * WIDTH
 PAIR = 2
 QUAD = NHEAD // PAIR
 SWAP = [(0, 1), (1, 0)]
@@ -162,7 +162,7 @@
 
 
 def first_state(place, *args):
-    outs = (PIECES_OUT, HEADS_OUT, HEADS_OUT, struct((TOK, DH), F32), struct((8, TOK), F32))
+    outs = (PIECES_OUT, QUERY_OUT, QUERY_OUT, struct((TOK, DH), F32), struct((8, TOK), F32))
     scratch = (pltpu.VMEM((16, TOK), F32),)
     specs = [HALF] * 4 + [whole(a.shape) for a in args[4:]]
     return call(
@@ -179,7 +179,7 @@
 
 
 def first_intra(place, q, other, ks, vs, cum, across):
-    args = (q, other, in_hbm(ks), in_hbm(vs), cum, across)
+    args = (q, other, ks, vs, cum, across)
     specs = [HALF] * 2 + [whole(a.shape) for a in args[2:]]
     outs = (INTRA_OUT, QUERY_OUT)
     return call(first_intra_kernel, "first_intra", place, args, outs, in_specs=specs)
@@ -422,8 +422,8 @@
 
     cols = span(pl.program_id(0), KSTEP)
     term = jnp.dot(rows[...], w_ref[:, cols], preferred_element_type=F32).astype(BF16)
-    out_ref[0] = term[:, :WIDTH]
-    out_ref[1] = term[:, WIDTH:]
+    for i in range(NHEAD // STEPS):
+        out_ref[i] = term[:, i * WIDTH : (i + 1) * WIDTH]
 
 
 def project(place, mine, yours, w):
@@ -435,7 +435,7 @@
             whole(mine.shape), whole(yours.shape),
             IN_VMEM,
         ],
-        out_specs=[pl.BlockSpec((2, BLK, WIDTH), lambda i, _: (i, 0, 0))],
+        out_specs=[pl.BlockSpec((NHEAD // STEPS, BLK, WIDTH), lambda i, _: (i, 0, 0))],
         scratch=(pltpu.VMEM((BLK, 2 * HW), BF16),),
         flops=2 * BLK * 2 * HW * NHEAD * WIDTH,
     )[0]

time: 190 us -> 189 us (level)
  no operation moved by 1% of the time
where the time goes in v9:
time: 189 us
  blocking collectives  84.9 us (45%)
  Pallas kernels  37 us (20%)
  starting transfers between devices  31.2 us (17%)
  waiting for transfers between devices  18.6 us (10%)
  between operations  13.6 us (7%)
  other arithmetic  1.96 us (1%)
    all_to_all x4, blocking collectives, exchange(): return lax.all_to_all(parts, axes, 0, 0)  84.9 us
    pallas_call x13, Pallas kernels, call(): pl.pallas_call(kernel, out_shape=outs, grid_spec=pltpu.PrefetchScalarGrid...  37 us
    all_to_all x3, starting transfers between devices, exchange(): return lax.all_to_all(parts, axes, 0, 0)  17.6 us
    all_to_all x3, waiting for transfers between devices, exchange(): return lax.all_to_all(parts, axes, 0, 0)  14.2 us
    ppermute x6, starting transfers between devices, swapped(): return [lax.ppermute(a, 'c', SWAP) for a in arrays]  5.14 us
    ppermute x2, starting transfers between devices, rest(): yours = lax.ppermute(yours, 'c', SWAP)  4.36 us
  transfers between devices with their start and end apart: 15, of which 8 were waited for; matrix products, arithmetic and copies ran while one was open for 1% of the time, Pallas kernels for 17%

profile of v9, /device:TPU:1, one launch (start us, length us, event | category | flops | bytes accessed | tf_op | source)
XLA Modules:
  0.0 188.7 jit_solution(17803080250694048276)
XLA Ops:
  6.5 3.2 %collective-permute-start = (bf16[256,768]{1,0:T(8,128)(2,1)}, bf16[256,768]{1,0:T(8,128)(2,1)S(1)}, u32[]{:S(2)}, u32[]{:S(2)}) collective-permute-start(bf16[256,768]{1,0:T(8,128)(2,1)} %k_ref.2), channel_id=1, source_target_pairs={{0,8},{8,0},{1,9},{9,1},{2,10},{10,2},{3,11},{11,3},{4,12},{12,4},... | collective-permute-start | bytes 1179656 | tf_op jit(solution)/shard_map/ppermute | solution.py:466
  9.8 0.0 collective-permute-start.1
  9.8 0.1 pad_add_fusion.place.refs_0_
  9.9 1.6 cut.1
  11.5 1.3 collective-permute-start.5
  12.8 0.7 pad_maximum_fusion.decay_ref
  13.5 0.9 collective-permute-start.2
  14.4 0.8 collective-permute-done.2.other_decay_ref
  15.2 0.0 collective-permute-done.other_k_ref
  15.2 0.0 collective-permute-done.1.other_v_ref
  15.2 3.5 %first_state.1 = (bf16[16,32,128]{2,1,0:T(8,128)(2,1)}, bf16[512,384]{1,0:T(8,128)(2,1)S(1)}, bf16[512,384]{1,0:T(8,128)(2,1)S(1)}, f32[512,128]{1,0:T(8,128)S(1)}, f32[8,512]{1,0:T(8,128)S(1)}) custom-call(s32[2]{0:T(128)S(1)} %pad_add_fusion.place.refs_0_, bf16[256,768]{1,0:T(8,128)(2,1)} %k_ref.2, bf16[256,768]{1,0:T(8,128)(2,1)S(1)} %collective-permute-done.other_k_ref, ...), custom_call_target="tpu_custom_call" | custom-call | tf_op jit(solution)/shard_map/first_state/pallas_call | solution.py:42
  18.7 0.3 collective-permute-start.3
  19.0 8.3 %all-to-all-start = ((bf16[16,32,128]{2,1,0:T(8,128)(2,1)}), bf16[16,32,128]{2,1,0:T(8,128)(2,1)S(1)}, u32[]{:S(2)}, u32[]{:S(2)}) async-start(bf16[16,32,128]{2,1,0:T(8,128)(2,1)} %get-tuple-element.35), calls=%async_computation | async-start | bytes 262144 | tf_op jit(solution)/shard_map/all_to_all | solution.py:445
  27.3 0.0 all-gather.3.cloned.1.call-start
  27.4 0.0 copy-done.3
  27.4 0.0 copy-start.4
  27.4 0.5 collective-permute-start.4
  27.9 0.0 collective-permute-done.5.far_ref
  28.0 0.1 collective-permute-start.6
  28.1 0.9 collective-permute-done.4.near_other_ref
  29.0 0.5 collective-permute-done.6.far_other_ref
  29.5 1.6 pack.1
  31.1 5.2 %all-to-all-done.in_ref = bf16[16,32,128]{2,1,0:T(8,128)(2,1)S(1)} async-done(((bf16[16,32,128]{2,1,0:T(8,128)(2,1)}), bf16[16,32,128]{2,1,0:T(8,128)(2,1)S(1)}, u32[]{:S(2)}, u32[]{:S(2)}) %all-to-all-start) | async-done | bytes 131104 | tf_op jit(solution)/shard_map/all_to_all | solution.py:445
  36.3 0.0 collective-permute-done.3.other_ref
  36.3 0.0 all-gather.3.cloned.1.call-update
  36.3 1.2 scan.2
  37.5 4.2 %all-to-all-start.1 = ((bf16[16,32,128]{2,1,0:T(8,128)(2,1)}), bf16[16,32,128]{2,1,0:T(8,128)(2,1)S(1)}, u32[]{:S(2)}, u32[]{:S(2)}) async-start(bf16[16,32,128]{2,1,0:T(8,128)(2,1)} %scan.2), calls=%async_computation.1 | async-start | bytes 262144 | tf_op jit(solution)/shard_map/all_to_all | solution.py:445
  41.7 0.0 all-gather.5.cloned.1.call-start
  41.8 0.0 copy-done.1
  41.8 0.0 copy-done.4
  41.8 2.1 %first_intra.1 = (f32[512,384]{1,0:T(8,128)S(1)}, bf16[512,384]{1,0:T(8,128)(2,1)S(1)}) custom-call(s32[2]{0:T(128)S(1)} %pad_add_fusion.place.refs_0_, bf16[256,768]{1,0:T(8,128)(2,1)S(1)} %copy-done.1, bf16[256,768]{1,0:T(8,128)(2,1)S(1)} %collective-permute-done.3.other_ref, bf16[512,384]{1,0:T(8,128)(2,1)S(1)} %get-tuple-element.44.ks, ...), custom_call_target="tpu_custom_call" | custom-call | tf_op jit(solution)/shard_map/first_intra/pallas_call | solution.py:42
  43.8 6.9 %all-to-all-done.1.refs_1_ = bf16[16,32,128]{2,1,0:T(8,128)(2,1)S(1)} async-done(((bf16[16,32,128]{2,1,0:T(8,128)(2,1)}), bf16[16,32,128]{2,1,0:T(8,128)(2,1)S(1)}, u32[]{:S(2)}, u32[]{:S(2)}) %all-to-all-start.1) | async-done | bytes 131104 | tf_op jit(solution)/shard_map/all_to_all | solution.py:445
  50.7 3.2 %finish.2 = (bf16[256,384]{1,0:T(8,128)(2,1)S(1)}, bf16[256,384]{1,0:T(8,128)(2,1)S(1)}, bf16[768,3072]{1,0:T(8,128)(2,1)S(1)}) custom-call(s32[2]{0:T(128)S(1)} %pad_add_fusion.place.refs_0_, bf16[16,32,128]{2,1,0:T(8,128)(2,1)S(1)} %all-to-all-done.1.refs_1_, f32[512,128]{1,0:T(8,128)S(1)} %get-tuple-element.43.cum_ref.refs_2_, ...), custom_call_target="tpu_custom_call" | custom-call | tf_op jit(solution)/shard_map/finish/pallas_call | solution.py:42
  53.9 2.3 %collective-permute-start.7 = (bf16[256,384]{1,0:T(8,128)(2,1)S(1)}, bf16[256,384]{1,0:T(8,128)(2,1)S(1)}, u32[]{:S(2)}, u32[]{:S(2)}) collective-permute-start(bf16[256,384]{1,0:T(8,128)(2,1)S(1)} %get-tuple-element.50), channel_id=1, source_target_pairs={{0,8},{8,0},{1,9},{9,1},{2,10},{10,2},{3,11},{11,3},{4,12},{12,4},... | collective-permute-start | bytes 589832 | tf_op jit(solution)/shard_map/ppermute | solution.py:454
  56.3 1.1 collective-permute-done.7.yours_ref
  57.3 2.2 %project.2 = bf16[8,256,384]{2,1,0:T(8,128)(2,1)S(1)} custom-call(s32[2]{0:T(128)S(1)} %pad_add_fusion.place.refs_0_, bf16[256,384]{1,0:T(8,128)(2,1)S(1)} %get-tuple-element.49.mine_ref, bf16[256,384]{1,0:T(8,128)(2,1)S(1)} %collective-permute-done.7.yours_ref, bf16[768,3072]{1,0:T(8,128)(2,1)S(1)} %get-tuple-element.51.w_ref), custom_call_target="tpu_custom_call" | custom-call | flops 1207959552 | tf_op jit(solution)/shard_map/project/pallas_call | solution.py:42
  59.6 0.0 copy-start.7
  59.6 25.0 %all_to_all.35 = bf16[8,256,384]{2,1,0:T(8,128)(2,1)S(1)} all-to-all(bf16[8,256,384]{2,1,0:T(8,128)(2,1)S(1)} %project.2), channel_id=1, replica_groups=mesh['yh'=2,'z'=8,'c'=2,'x'=4,'yl'=2] {'x','yl'}, dimensions={0} | all-to-all | bytes 3145728 | tf_op jit(solution)/shard_map/all_to_all | solution.py:445
  84.6 0.2 convert_reduce_fusion.1
  84.8 0.0 copy-done.7
  84.9 0.0 copy-start.5
  84.9 0.0 all-gather.5.cloned.1.call-update
  84.9 0.6 copy-done.5
  85.5 0.1 broadcast_in_dim.2
  85.7 22.7 %all_to_all.36.h_ref.mine_ref = bf16[8,256,384]{2,1,0:T(8,128)(2,1)S(1)} all-to-all(bf16[8,256,384]{2,1,0:T(8,128)(2,1)S(1)} %broadcast_in_dim.2), channel_id=1, replica_groups=mesh['yh'=2,'z'=8,'c'=2,'x'=4,'yl'=2] {'x','yl'}, dimensions={0} | all-to-all | bytes 3145728 | tf_op jit(solution)/shard_map/all_to_all | solution.py:445
  108.4 2.8 %collective-permute-start.8 = (bf16[8,256,384]{2,1,0:T(8,128)(2,1)S(1)}, bf16[8,256,384]{2,1,0:T(8,128)(2,1)S(1)}, u32[]{:S(2)}, u32[]{:S(2)}) collective-permute-start(bf16[8,256,384]{2,1,0:T(8,128)(2,1)S(1)} %all_to_all.36.h_ref.mine_ref), channel_id=1, source_target_pairs={{0,8},{8,0},{1,9},{9,1},{2,10},{10,2},{3,11},{11,3},{4,12},{12,4},... | collective-permute-start | bytes 4718600 | tf_op jit(solution)/shard_map/ppermute | solution.py:496
  111.2 4.4 %own_kv.1 = (bf16[256,768]{1,0:T(8,128)(2,1)S(1)}, bf16[2,1536,768]{2,1,0:T(8,128)(2,1)S(1)}) custom-call(s32[2]{0:T(128)S(1)} %pad_add_fusion.place.refs_0_, bf16[8,256,384]{2,1,0:T(8,128)(2,1)S(1)} %all_to_all.36.h_ref.mine_ref, bf16[2,1536,768]{2,1,0:T(8,128)(2,1)} %all-gather.3.cloned.1.call-done.w_ref, f32[8,1,384]{2,1,0:T(1,128)S(1)} %bitcast.7), custom_call_target="tpu_custom_call" | custom-call | tf_op jit(solution)/shard_map/own_kv/pallas_call | solution.py:42
  115.6 0.0 collective-permute-done.8.h_ref.yours_ref
  115.6 4.2 %second_state.1 = (bf16[16,32,128]{2,1,0:T(8,128)(2,1)S(1)}, bf16[512,384]{1,0:T(8,128)(2,1)}, bf16[512,384]{1,0:T(8,128)(2,1)}) custom-call(s32[2]{0:T(128)S(1)} %pad_add_fusion.place.refs_0_, bf16[8,256,384]{2,1,0:T(8,128)(2,1)S(1)} %collective-permute-done.8.h_ref.yours_ref, bf16[2,1536,768]{2,1,0:T(8,128)(2,1)S(1)} %get-tuple-element.53.w_ref, ...), custom_call_target="tpu_custom_call" | custom-call | tf_op jit(solution)/shard_map/second_state/pallas_call | solution.py:42
  119.8 14.3 %all_to_all.37.in_ref = bf16[16,32,128]{2,1,0:T(8,128)(2,1)S(1)} all-to-all(bf16[16,32,128]{2,1,0:T(8,128)(2,1)S(1)} %get-tuple-element.55), channel_id=1, replica_groups=mesh['yh'=2,'z'=8,'c'=2,'x'=4,'yl'=2] {'yh','z'}, dimensions={0} | all-to-all | bytes 262144 | tf_op jit(solution)/shard_map/all_to_all | solution.py:445
  134.1 0.6 scan.3
  134.7 0.6 copy-done
  135.3 5.1 %all-to-all-start.5 = ((bf16[16,32,128]{2,1,0:T(8,128)(2,1)}), bf16[16,32,128]{2,1,0:T(8,128)(2,1)S(1)}, u32[]{:S(2)}, u32[]{:S(2)}) async-start(bf16[16,32,128]{2,1,0:T(8,128)(2,1)} %copy-done), calls=%async_computation.5 | async-start | bytes 262144 | tf_op jit(solution)/shard_map/all_to_all | solution.py:445
  140.4 0.0 all-gather.5.cloned.1.call-done.w_ref
  140.5 6.8 %second_intra.1 = (f32[512,384]{1,0:T(8,128)}, bf16[512,384]{1,0:T(8,128)(2,1)}) custom-call(s32[2]{0:T(128)S(1)} %pad_add_fusion.place.refs_0_, bf16[8,256,384]{2,1,0:T(8,128)(2,1)S(1)} %all_to_all.36.h_ref.mine_ref, bf16[8,256,384]{2,1,0:T(8,128)(2,1)S(1)} %collective-permute-done.8.h_ref.yours_ref, ...), custom_call_target="tpu_custom_call" | custom-call | tf_op jit(solution)/shard_map/second_intra/pallas_call | solution.py:42
  147.3 2.1 %all-to-all-done.5.refs_1_ = bf16[16,32,128]{2,1,0:T(8,128)(2,1)S(1)} async-done(((bf16[16,32,128]{2,1,0:T(8,128)(2,1)}), bf16[16,32,128]{2,1,0:T(8,128)(2,1)S(1)}, u32[]{:S(2)}, u32[]{:S(2)}) %all-to-all-start.5) | async-done | bytes 131104 | tf_op jit(solution)/shard_map/all_to_all | solution.py:445
  149.4 3.3 %finish.3 = (bf16[256,384]{1,0:T(8,128)(2,1)S(1)}, bf16[256,384]{1,0:T(8,128)(2,1)S(1)}, bf16[768,3072]{1,0:T(8,128)(2,1)S(1)}) custom-call(s32[2]{0:T(128)S(1)} %pad_add_fusion.place.refs_0_, bf16[16,32,128]{2,1,0:T(8,128)(2,1)S(1)} %all-to-all-done.5.refs_1_, f32[512,128]{1,0:T(8,128)S(1)} %get-tuple-element.43.cum_ref.refs_2_, ...), custom_call_target="tpu_custom_call" | custom-call | tf_op jit(solution)/shard_map/finish/pallas_call | solution.py:42
  152.7 2.0 %collective-permute-start.9 = (bf16[256,384]{1,0:T(8,128)(2,1)S(1)}, bf16[256,384]{1,0:T(8,128)(2,1)S(1)}, u32[]{:S(2)}, u32[]{:S(2)}) collective-permute-start(bf16[256,384]{1,0:T(8,128)(2,1)S(1)} %get-tuple-element.63), channel_id=1, source_target_pairs={{0,8},{8,0},{1,9},{9,1},{2,10},{10,2},{3,11},{11,3},{4,12},{12,4},... | collective-permute-start | bytes 589832 | tf_op jit(solution)/shard_map/ppermute | solution.py:454
  154.7 1.1 collective-permute-done.9.yours_ref
  155.8 2.2 %project.3 = bf16[8,256,384]{2,1,0:T(8,128)(2,1)S(1)} custom-call(s32[2]{0:T(128)S(1)} %pad_add_fusion.place.refs_0_, bf16[256,384]{1,0:T(8,128)(2,1)S(1)} %get-tuple-element.62.mine_ref, bf16[256,384]{1,0:T(8,128)(2,1)S(1)} %collective-permute-done.9.yours_ref, bf16[768,3072]{1,0:T(8,128)(2,1)S(1)} %get-tuple-element.64.w_ref), custom_call_target="tpu_custom_call" | custom-call | flops 1207959552 | tf_op jit(solution)/shard_map/project/pallas_call | solution.py:42
  158.0 0.0 copy-start.6
  158.0 23.0 %all_to_all.38 = bf16[8,256,384]{2,1,0:T(8,128)(2,1)S(1)} all-to-all(bf16[8,256,384]{2,1,0:T(8,128)(2,1)S(1)} %project.3), channel_id=1, replica_groups=mesh['yh'=2,'z'=8,'c'=2,'x'=4,'yl'=2] {'x','yl'}, dimensions={0} | all-to-all | bytes 3145728 | tf_op jit(solution)/shard_map/all_to_all | solution.py:445
  181.0 0.2 convert_reduce_fusion
  181.2 0.7 add_convert_fusion
  (9 shorter events, 0.1 us)
Async XLA Ops:
  6.5 8.7 %collective-permute-start = (bf16[256,768]{1,0:T(8,128)(2,1)}, bf16[256,768]{1,0:T(8,128)(2,1)S(1)}, u32[]{:S(2)}, u32[]{:S(2)}) collective-permute-start(bf16[256,768]{1,0:T(8,128)(2,1)} %k_ref.2), channel_id=1, source_target_pairs={{0,8},{8,0},{1,9},{9,1},{2,10},{10,2},{3,11},{11,3},{4,12},{12,4},... | collective-permute-start | bytes 1179656 | tf_op jit(solution)/shard_map/ppermute | solution.py:466
  9.8 5.4 %collective-permute-start.1 = (bf16[256,768]{1,0:T(8,128)(2,1)}, bf16[256,768]{1,0:T(8,128)(2,1)S(1)}, u32[]{:S(2)}, u32[]{:S(2)}) collective-permute-start(bf16[256,768]{1,0:T(8,128)(2,1)} %v_ref.2), channel_id=1, source_target_pairs={{0,8},{8,0},{1,9},{9,1},{2,10},{10,2},{3,11},{11,3},{4,12},{12,4},... | collective-permute-start | bytes 1179656 | tf_op jit(solution)/shard_map/ppermute | solution.py:466
  11.5 16.4 %collective-permute-start.5 = (bf16[96,2304]{1,0:T(8,128)(2,1)S(1)}, bf16[96,2304]{1,0:T(8,128)(2,1)S(1)}, u32[]{:S(2)}, u32[]{:S(2)}) collective-permute-start(bf16[96,2304]{1,0:T(8,128)(2,1)S(1)} %get-tuple-element.37.near_ref), channel_id=1, source_target_pairs={{0,128},{128,0},{1,129},{129,1},{2,130},{130,2},{3,131},{131,3},{4... | collective-permute-start | bytes 1327112 | tf_op jit(solution)/shard_map/ppermute | solution.py:475
  13.5 28.3 %copy-start.1 = (bf16[256,768]{1,0:T(8,128)(2,1)S(1)}, bf16[256,768]{1,0:T(8,128)(2,1)}, u32[]{:S(2)}) copy-start(bf16[256,768]{1,0:T(8,128)(2,1)} %q_ref.2) | copy-start | bytes 1179652
  13.5 1.7 collective-permute-start.2
  18.7 8.7 %copy-start.3 = (f32[8,512]{1,0:T(8,128)}, f32[8,512]{1,0:T(8,128)S(1)}, u32[]{:S(2)}) copy-start(f32[8,512]{1,0:T(8,128)S(1)} %get-tuple-element.46.across_ref) | copy-start | bytes 49156
  18.7 17.6 %collective-permute-start.3 = (bf16[256,768]{1,0:T(8,128)(2,1)}, bf16[256,768]{1,0:T(8,128)(2,1)S(1)}, u32[]{:S(2)}, u32[]{:S(2)}) collective-permute-start(bf16[256,768]{1,0:T(8,128)(2,1)} %q_ref.2), channel_id=1, source_target_pairs={{0,8},{8,0},{1,9},{9,1},{2,10},{10,2},{3,11},{11,3},{4,12},{12,4},... | collective-permute-start | bytes 1179656 | tf_op jit(solution)/shard_map/ppermute | solution.py:466
  19.0 17.2 %all-to-all-start = ((bf16[16,32,128]{2,1,0:T(8,128)(2,1)}), bf16[16,32,128]{2,1,0:T(8,128)(2,1)S(1)}, u32[]{:S(2)}, u32[]{:S(2)}) async-start(bf16[16,32,128]{2,1,0:T(8,128)(2,1)} %get-tuple-element.35), calls=%async_computation | async-start | bytes 262144 | tf_op jit(solution)/shard_map/all_to_all | solution.py:445
  27.3 83.8 %all-gather.3.cloned.1.call-start = ((), (), s32[]{:S(2)}) async-start(), calls=%async_computation.7 | async-start | bytes 5308416 | tf_op jit(solution)/shard_map/all_gather | solution.py:487
  27.4 14.4 %copy-start.4 = (f32[8,512]{1,0:T(8,128)S(1)}, f32[8,512]{1,0:T(8,128)}, u32[]{:S(2)}) copy-start(f32[8,512]{1,0:T(8,128)} %copy-done.3) | copy-start | bytes 49156
  27.4 1.6 collective-permute-start.4
  28.0 1.6 collective-permute-start.6
  37.5 13.2 %all-to-all-start.1 = ((bf16[16,32,128]{2,1,0:T(8,128)(2,1)}), bf16[16,32,128]{2,1,0:T(8,128)(2,1)S(1)}, u32[]{:S(2)}, u32[]{:S(2)}) async-start(bf16[16,32,128]{2,1,0:T(8,128)(2,1)} %scan.2), calls=%async_computation.1 | async-start | bytes 262144 | tf_op jit(solution)/shard_map/all_to_all | solution.py:445
  41.7 98.8 %all-gather.5.cloned.1.call-start = ((), (), s32[]{:S(2)}) async-start(), calls=%async_computation.8 | async-start | bytes 2654208 | tf_op jit(solution)/shard_map/all_gather | solution.py:487
  53.9 3.4 %collective-permute-start.7 = (bf16[256,384]{1,0:T(8,128)(2,1)S(1)}, bf16[256,384]{1,0:T(8,128)(2,1)S(1)}, u32[]{:S(2)}, u32[]{:S(2)}) collective-permute-start(bf16[256,384]{1,0:T(8,128)(2,1)S(1)} %get-tuple-element.50), channel_id=1, source_target_pairs={{0,8},{8,0},{1,9},{9,1},{2,10},{10,2},{3,11},{11,3},{4,12},{12,4},... | collective-permute-start | bytes 589832 | tf_op jit(solution)/shard_map/ppermute | solution.py:454
  59.6 25.2 %copy-start.7 = (bf16[256,384]{1,0:T(8,128)(2,1)S(1)}, bf16[256,384]{1,0:T(8,128)(2,1)}, u32[]{:S(2)}) copy-start(bf16[256,384]{1,0:T(8,128)(2,1)} %param.20) | copy-start | bytes 589828
  84.9 0.7 copy-start.5
  85.5 25.6 %copy-start.2 = (f32[3072]{0:T(1024)S(1)}, f32[3072]{0:T(1024)}, u32[]{:S(2)}) copy-start(f32[3072]{0:T(1024)} %param.21) | copy-start | bytes 36868
  108.4 7.2 %collective-permute-start.8 = (bf16[8,256,384]{2,1,0:T(8,128)(2,1)S(1)}, bf16[8,256,384]{2,1,0:T(8,128)(2,1)S(1)}, u32[]{:S(2)}, u32[]{:S(2)}) collective-permute-start(bf16[8,256,384]{2,1,0:T(8,128)(2,1)S(1)} %all_to_all.36.h_ref.mine_ref), channel_id=1, source_target_pairs={{0,8},{8,0},{1,9},{9,1},{2,10},{10,2},{3,11},{11,3},{4,12},{12,4},... | collective-permute-start | bytes 4718600 | tf_op jit(solution)/shard_map/ppermute | solution.py:496
  134.7 0.7 copy-start
  135.3 14.0 %all-to-all-start.5 = ((bf16[16,32,128]{2,1,0:T(8,128)(2,1)}), bf16[16,32,128]{2,1,0:T(8,128)(2,1)S(1)}, u32[]{:S(2)}, u32[]{:S(2)}) async-start(bf16[16,32,128]{2,1,0:T(8,128)(2,1)} %copy-done), calls=%async_computation.5 | async-start | bytes 262144 | tf_op jit(solution)/shard_map/all_to_all | solution.py:445
  152.7 3.1 %collective-permute-start.9 = (bf16[256,384]{1,0:T(8,128)(2,1)S(1)}, bf16[256,384]{1,0:T(8,128)(2,1)S(1)}, u32[]{:S(2)}, u32[]{:S(2)}) collective-permute-start(bf16[256,384]{1,0:T(8,128)(2,1)S(1)} %get-tuple-element.63), channel_id=1, source_target_pairs={{0,8},{8,0},{1,9},{9,1},{2,10},{10,2},{3,11},{11,3},{4,12},{12,4},... | collective-permute-start | bytes 589832 | tf_op jit(solution)/shard_map/ppermute | solution.py:454
  158.0 23.2 %copy-start.6 = (bf16[256,384]{1,0:T(8,128)(2,1)S(1)}, bf16[256,384]{1,0:T(8,128)(2,1)}, u32[]{:S(2)}) copy-start(bf16[256,384]{1,0:T(8,128)(2,1)} %copy-done.5) | copy-start | bytes 589828
Sparse Core Ops, SparseCore 0:
  36.4 57.7 all-gather.2
  96.0 39.4 all-gather.4
